TPU v7x, 32 devices: a whole 2x2x4 slice. The times are simulated.
32 devices in a mesh: dp: 8 (over y, x, core), fsdp: 4 (over z).
Axes of the slice: x: 2, y: 2, z: 4, core: 2. Of those that a mesh axis runs over, the one named last changes fastest.
Arguments:
- layer_in: bfloat16 [32, 1024, 1024], P(('dp', 'fsdp')), may hold values from -16 to 16
- first_values: bfloat16 [32, 1024, 1024], P(('dp', 'fsdp')), may hold values from -16 to 16
- first_values_grad: float32 [32, 1024, 1024], P(('dp', 'fsdp')), may hold values from -6 to 6
- cotangent: bfloat16 [32, 1024, 1024], P(('dp', 'fsdp')), may hold values from -6 to 6
- doc_lengths: int32 [32, 8], P(('dp', 'fsdp')), may hold values from 1 to 512, 1024 in all within a row
- norm1_gain: bfloat16 [1024], P('fsdp'), may hold values from 0.5 to 1.5
- w_query: bfloat16 [1024, 1024], P('fsdp'), may hold values from -0.1875 to 0.1875
- w_key: bfloat16 [1024, 1024], P('fsdp'), may hold values from -0.1875 to 0.1875
- w_value: bfloat16 [1024, 1024], P('fsdp'), may hold values from -0.1875 to 0.1875
- w_out: bfloat16 [1024, 1024], P('fsdp'), may hold values from -0.75 to 0.75
- norm2_gain: bfloat16 [1024], P('fsdp'), may hold values from 0.5 to 1.5
- w_gate: bfloat16 [1024, 2816], P('fsdp'), may hold values from -0.1875 to 0.1875
- w_up: bfloat16 [1024, 2816], P('fsdp'), may hold values from -0.1875 to 0.1875
- w_down: bfloat16 [2816, 1024], P('fsdp'), may hold values from -0.109375 to 0.109375
Outputs:
- layer_out: bfloat16 [32, 1024, 1024], P(('dp', 'fsdp'))
- input_grad: float32 [32, 1024, 1024], P(('dp', 'fsdp'))
- first_values_grad_out: float32 [32, 1024, 1024], P(('dp', 'fsdp'))
- grad_norm1_gain: float32 [1024], P('fsdp')
- grad_w_query: float32 [1024, 1024], P('fsdp')
- grad_w_key: float32 [1024, 1024], P('fsdp')
- grad_w_value: float32 [1024, 1024], P('fsdp')
- grad_w_out: float32 [1024, 1024], P('fsdp')
- grad_norm2_gain: float32 [1024], P('fsdp')
- grad_w_gate: float32 [1024, 2816], P('fsdp')
- grad_w_up: float32 [1024, 2816], P('fsdp')
- grad_w_down: float32 [2816, 1024], P('fsdp')
- value_norms: float32 [2], replicated
Inputs may be any that keep to these rules, and one draw needn't show every extreme that they name: `doc_lengths`: each row's entries sum to 1024; some entry of each row equals 512.
All inputs are finite; a program needn't handle non-finite values.
Results may differ from a plain program's by a relative error of at most 0.02.
Values may be sent and summed in bfloat16 or wider, within the bound.
No kernel may reach another device: no remote copies, remote signals or barrier semaphores. Data moves between devices by JAX's collectives and lax.ppermute only.
A program may use at most 384 MiB of HBM per device.

v0:
```python
import jax
import jax.numpy as jnp
from jax import lax
from jax.sharding import PartitionSpec as P

HEADS = 16
HEAD_DIM = 64


EPS = 1e-06


def layout(lengths, length):
    position = jnp.arange(length, dtype=jnp.int32)
    ends = jnp.cumsum(lengths, axis=1)
    seg = jnp.sum((position[None, :, None] >= ends[:, None, :]).astype(jnp.int32), 2)
    starts = ends - lengths
    onehot = seg[:, :, None] == jnp.arange(lengths.shape[1], dtype=jnp.int32)[None, None, :]
    first = jnp.sum(jnp.where(onehot, starts[:, None, :], 0), 2)
    rel = (position[None, :] - first).astype(jnp.float32)
    inverse = 10000.0 ** (-jnp.arange(HEAD_DIM // 2, dtype=jnp.float32) * 2.0 / HEAD_DIM)
    angle = rel[:, :, None] * inverse[None, None, :]
    keep = (seg < lengths.shape[1] - 1).astype(jnp.float32)
    return (jnp.cos(angle), jnp.sin(angle), seg, keep)


def rotate(t, cosv, sinv):
    half = t.shape[-1] // 2
    first, second = (t[..., :half], t[..., half:])
    c = cosv[:, :, None, :]
    s = sinv[:, :, None, :]
    return jnp.concatenate([first * c - second * s, second * c + first * s], -1)


def unrotate(t, cosv, sinv):
    half = t.shape[-1] // 2
    first, second = (t[..., :half], t[..., half:])
    c = cosv[:, :, None, :]
    s = sinv[:, :, None, :]
    return jnp.concatenate([first * c + second * s, second * c - first * s], -1)


def block_scores(qblock, key, seg, start):
    length = key.shape[0]
    block = qblock.shape[0]
    position = jnp.arange(length, dtype=jnp.int32)
    scores = jnp.einsum("qhd,khd->hqk", qblock, key, preferred_element_type=jnp.float32) * 0.125
    allowed = (seg[start : start + block, None] == seg[None, :]) & (
        position[start : start + block, None] >= position[None, :]
    )
    return jnp.where(allowed[None], scores, -1e30)


def attend_forward(item):
    query, key, value, seg = item
    length = query.shape[0]
    block = min(512, length)
    outputs = []
    totals = []
    for start in range(0, length, block):
        scores = block_scores(query[start : start + block], key, seg, start)
        top = jnp.max(scores, -1, keepdims=True)
        expo = jnp.exp(scores - top)
        summed = jnp.sum(expo, -1, keepdims=True)
        probs = (expo / summed).astype(jnp.bfloat16)
        outputs.append(jnp.einsum("hqk,khd->qhd", probs, value, preferred_element_type=jnp.float32))
        totals.append((top + jnp.log(summed))[..., 0])
    return (jnp.concatenate(outputs, 0), jnp.concatenate(totals, 1))


def attend_backward(item):
    query, key, value, grad_out, logsum, seg = item
    length = query.shape[0]
    block = min(512, length)
    grad_key = jnp.zeros(key.shape, jnp.float32)
    grad_value = jnp.zeros(value.shape, jnp.float32)
    grad_query = []
    for start in range(0, length, block):
        qblock = query[start : start + block]
        gblock = grad_out[start : start + block]
        scores = block_scores(qblock, key, seg, start)
        probs = jnp.exp(scores - logsum[:, start : start + block, None])
        grad_value = grad_value + jnp.einsum(
            "hqk,qhd->khd", probs.astype(jnp.bfloat16), gblock, preferred_element_type=jnp.float32
        )
        grad_probs = jnp.einsum("qhd,khd->hqk", gblock, value, preferred_element_type=jnp.float32)
        grad_scores = (
            probs * (grad_probs - jnp.sum(probs * grad_probs, -1, keepdims=True))
        ).astype(jnp.bfloat16)
        grad_query.append(
            0.125 * jnp.einsum("hqk,khd->qhd", grad_scores, key, preferred_element_type=jnp.float32)
        )
        grad_key = grad_key + 0.125 * jnp.einsum(
            "hqk,qhd->khd", grad_scores, qblock, preferred_element_type=jnp.float32
        )
    return (jnp.concatenate(grad_query, 0), grad_key, grad_value)


def local(
    layer_in,
    first_values,
    first_values_grad,
    cotangent,
    doc_lengths,
    norm1_gain,
    w_query,
    w_key,
    w_value,
    w_out,
    norm2_gain,
    w_gate,
    w_up,
    w_down,
):
    rows, length, width = layer_in.shape
    count = rows * length
    full = (
        lax.all_gather(norm1_gain, "fsdp", axis=0, tiled=True),
        lax.all_gather(w_query, "fsdp", axis=0, tiled=True),
        lax.all_gather(w_key, "fsdp", axis=0, tiled=True),
        lax.all_gather(w_value, "fsdp", axis=0, tiled=True),
        lax.all_gather(w_out, "fsdp", axis=0, tiled=True),
        lax.all_gather(norm2_gain, "fsdp", axis=0, tiled=True),
        lax.all_gather(w_gate, "fsdp", axis=0, tiled=True),
        lax.all_gather(w_up, "fsdp", axis=0, tiled=True),
        lax.all_gather(w_down, "fsdp", axis=0, tiled=True),
    )
    g1, wq, wk, wv, wo, g2, wg, wu, wd = full
    cosv, sinv, seg, keep = layout(doc_lengths, length)
    keep_col = keep.reshape(count, 1)
    xf = layer_in.reshape(count, width).astype(jnp.float32)
    vf = first_values.reshape(count, width).astype(jnp.float32)
    rinv1 = lax.rsqrt(jnp.mean(xf * xf, -1, keepdims=True) + EPS)
    n1 = xf * rinv1
    h1 = (n1 * g1.astype(jnp.float32)).astype(jnp.bfloat16)
    query = jnp.dot(h1, wq, preferred_element_type=jnp.float32).reshape(
        rows, length, HEADS, HEAD_DIM
    )
    key = jnp.dot(h1, wk, preferred_element_type=jnp.float32).reshape(rows, length, HEADS, HEAD_DIM)
    own = jnp.dot(h1, wv, preferred_element_type=jnp.float32)
    query_rot = rotate(query, cosv, sinv).astype(jnp.bfloat16)
    key_rot = rotate(key, cosv, sinv).astype(jnp.bfloat16)
    mixed_flat = (0.5 * own + 0.5 * vf).astype(jnp.bfloat16)
    mixed_wide = mixed_flat.astype(jnp.float32)
    mixed = mixed_flat.reshape(rows, length, HEADS, HEAD_DIM)
    attn, logsum = lax.map(attend_forward, (query_rot, key_rot, mixed, seg))
    attn_low = (attn.reshape(count, width) * keep_col).astype(jnp.bfloat16)
    r1 = xf + jnp.dot(attn_low, wo, preferred_element_type=jnp.float32)
    rinv2 = lax.rsqrt(jnp.mean(r1 * r1, -1, keepdims=True) + EPS)
    n2 = r1 * rinv2
    h2 = (n2 * g2.astype(jnp.float32)).astype(jnp.bfloat16)
    gate = jnp.dot(h2, wg, preferred_element_type=jnp.float32)
    up = jnp.dot(h2, wu, preferred_element_type=jnp.float32)
    sigma = jax.nn.sigmoid(gate)
    silu_gate = gate * sigma
    hidden = (silu_gate * up).astype(jnp.bfloat16)
    result = (r1 + jnp.dot(hidden, wd, preferred_element_type=jnp.float32)).astype(jnp.bfloat16)
    squares = lax.psum((jnp.sum(vf * vf), jnp.sum(mixed_wide * mixed_wide)), ("dp", "fsdp"))
    entries = count * width * lax.axis_size("dp") * lax.axis_size("fsdp")
    value_norms = jnp.stack([squares[0], squares[1]]) / entries
    again = (
        lax.all_gather(norm1_gain, "fsdp", axis=0, tiled=True),
        lax.all_gather(w_query, "fsdp", axis=0, tiled=True),
        lax.all_gather(w_key, "fsdp", axis=0, tiled=True),
        lax.all_gather(w_value, "fsdp", axis=0, tiled=True),
        lax.all_gather(w_out, "fsdp", axis=0, tiled=True),
        lax.all_gather(norm2_gain, "fsdp", axis=0, tiled=True),
        lax.all_gather(w_gate, "fsdp", axis=0, tiled=True),
        lax.all_gather(w_up, "fsdp", axis=0, tiled=True),
        lax.all_gather(w_down, "fsdp", axis=0, tiled=True),
    )
    g1, wq, wk, wv, wo, g2, wg, wu, wd = again
    dy = cotangent.reshape(count, width).astype(jnp.float32)
    d_ff = cotangent.reshape(count, width)
    grad_wd = jnp.einsum("nf,nd->fd", hidden, d_ff, preferred_element_type=jnp.float32)
    d_hidden = jnp.einsum("nd,fd->nf", d_ff, wd, preferred_element_type=jnp.float32)
    d_gate = (d_hidden * up * sigma * (1.0 + gate * (1.0 - sigma))).astype(jnp.bfloat16)
    d_up = (d_hidden * silu_gate).astype(jnp.bfloat16)
    grad_wg = jnp.einsum("nd,nf->df", h2, d_gate, preferred_element_type=jnp.float32)
    grad_wu = jnp.einsum("nd,nf->df", h2, d_up, preferred_element_type=jnp.float32)
    d_h2 = jnp.einsum("nf,df->nd", d_gate, wg, preferred_element_type=jnp.float32) + jnp.einsum(
        "nf,df->nd", d_up, wu, preferred_element_type=jnp.float32
    )
    grad_g2 = jnp.sum(d_h2 * n2, 0)
    d_n2 = d_h2 * g2.astype(jnp.float32)
    d_r1 = dy + rinv2 * (d_n2 - n2 * jnp.mean(d_n2 * n2, -1, keepdims=True))
    d_attn = d_r1.astype(jnp.bfloat16)
    grad_wo = jnp.einsum("nd,ne->de", attn_low, d_attn, preferred_element_type=jnp.float32)
    d_out = (
        jnp.einsum("ne,de->nd", d_attn, wo, preferred_element_type=jnp.float32) * keep_col
    ).astype(jnp.bfloat16)
    d_query, d_key, d_value = lax.map(
        attend_backward,
        (query_rot, key_rot, mixed, d_out.reshape(rows, length, HEADS, HEAD_DIM), logsum, seg),
    )
    d_value_low = d_value.astype(jnp.bfloat16).reshape(count, width).astype(jnp.float32)
    first_out = first_values_grad + 0.5 * d_value_low.reshape(rows, length, width)
    d_own = (0.5 * d_value_low).astype(jnp.bfloat16)
    d_q = unrotate(d_query, cosv, sinv).astype(jnp.bfloat16).reshape(count, width)
    d_k = unrotate(d_key, cosv, sinv).astype(jnp.bfloat16).reshape(count, width)
    grad_wq = jnp.einsum("nd,ne->de", h1, d_q, preferred_element_type=jnp.float32)
    grad_wk = jnp.einsum("nd,ne->de", h1, d_k, preferred_element_type=jnp.float32)
    grad_wv = jnp.einsum("nd,ne->de", h1, d_own, preferred_element_type=jnp.float32)
    d_h1 = jnp.einsum("ne,de->nd", d_q, wq, preferred_element_type=jnp.float32)
    d_h1 = d_h1 + jnp.einsum("ne,de->nd", d_k, wk, preferred_element_type=jnp.float32)
    d_h1 = d_h1 + jnp.einsum("ne,de->nd", d_own, wv, preferred_element_type=jnp.float32)
    grad_g1 = jnp.sum(d_h1 * n1, 0)
    d_n1 = d_h1 * g1.astype(jnp.float32)
    d_x = d_r1 + rinv1 * (d_n1 - n1 * jnp.mean(d_n1 * n1, -1, keepdims=True))
    shards = (
        lax.psum_scatter(
            grad_g1.astype(jnp.bfloat16), "fsdp", scatter_dimension=0, tiled=True
        ).astype(jnp.float32),
        lax.psum_scatter(
            grad_wq.astype(jnp.bfloat16), "fsdp", scatter_dimension=0, tiled=True
        ).astype(jnp.float32),
        lax.psum_scatter(
            grad_wk.astype(jnp.bfloat16), "fsdp", scatter_dimension=0, tiled=True
        ).astype(jnp.float32),
        lax.psum_scatter(
            grad_wv.astype(jnp.bfloat16), "fsdp", scatter_dimension=0, tiled=True
        ).astype(jnp.float32),
        lax.psum_scatter(
            grad_wo.astype(jnp.bfloat16), "fsdp", scatter_dimension=0, tiled=True
        ).astype(jnp.float32),
        lax.psum_scatter(
            grad_g2.astype(jnp.bfloat16), "fsdp", scatter_dimension=0, tiled=True
        ).astype(jnp.float32),
        lax.psum_scatter(
            grad_wg.astype(jnp.bfloat16), "fsdp", scatter_dimension=0, tiled=True
        ).astype(jnp.float32),
        lax.psum_scatter(
            grad_wu.astype(jnp.bfloat16), "fsdp", scatter_dimension=0, tiled=True
        ).astype(jnp.float32),
        lax.psum_scatter(
            grad_wd.astype(jnp.bfloat16), "fsdp", scatter_dimension=0, tiled=True
        ).astype(jnp.float32),
    )
    sg1, sq, sk, sv, so, sg2, sg, su, sd = shards
    owned = (
        lax.psum(sg1.astype(jnp.bfloat16), "dp").astype(jnp.float32),
        lax.psum(sq.astype(jnp.bfloat16), "dp").astype(jnp.float32),
        lax.psum(sk.astype(jnp.bfloat16), "dp").astype(jnp.float32),
        lax.psum(sv.astype(jnp.bfloat16), "dp").astype(jnp.float32),
        lax.psum(so.astype(jnp.bfloat16), "dp").astype(jnp.float32),
        lax.psum(sg2.astype(jnp.bfloat16), "dp").astype(jnp.float32),
        lax.psum(sg.astype(jnp.bfloat16), "dp").astype(jnp.float32),
        lax.psum(su.astype(jnp.bfloat16), "dp").astype(jnp.float32),
        lax.psum(sd.astype(jnp.bfloat16), "dp").astype(jnp.float32),
    )
    return (
        result.reshape(rows, length, width),
        d_x.reshape(rows, length, width),
        first_out,
        owned[0],
        owned[1],
        owned[2],
        owned[3],
        owned[4],
        owned[5],
        owned[6],
        owned[7],
        owned[8],
        value_norms,
    )


def solution(mesh):
    return jax.shard_map(
        local,
        mesh=mesh,
        in_specs=(
            P(("dp", "fsdp"), None, None),
            P(("dp", "fsdp"), None, None),
            P(("dp", "fsdp"), None, None),
            P(("dp", "fsdp"), None, None),
            P(("dp", "fsdp"), None),
            P("fsdp"),
            P("fsdp", None),
            P("fsdp", None),
            P("fsdp", None),
            P("fsdp", None),
            P("fsdp"),
            P("fsdp", None),
            P("fsdp", None),
            P("fsdp", None),
        ),
        out_specs=(
            P(("dp", "fsdp"), None, None),
            P(("dp", "fsdp"), None, None),
            P(("dp", "fsdp"), None, None),
            P("fsdp"),
            P("fsdp", None),
            P("fsdp", None),
            P("fsdp", None),
            P("fsdp", None),
            P("fsdp"),
            P("fsdp", None),
            P("fsdp", None),
            P("fsdp", None),
            P(),
        ),
        check_vma=False,
    )
```

profile of v0, /device:TPU:9, one launch (start us, length us, event | category | flops | bytes accessed | tf_op | source)
XLA Modules:
  0.0 1305.4 jit_solution(15450683530981667103)
XLA Ops:
  42.5 12.6 all-gather.14.cloned.1.call-done
  59.0 42.3 %all-gather.12.cloned.1.call-done = bf16[1024,1024]{1,0:T(8,128)(2,1)} async-done(((bf16[256,1024]{1,0:T(8,128)(2,1)}), bf16[1024,1024]{1,0:T(8,128)(2,1)}) %all-gather.12.cloned.1.call-update) | async-done | bytes 2097168 | tf_op jit(solution)/shard_map/all_gather | solution.py:119
  113.7 14.2 %fusion.88 = (f32[16,512]{1,0:T(8,128)S(1)}, f32[16,512,1024]{2,1,0:T(8,128)}) fusion(bf16[1024,16,32]{0,2,1:T(8,128)(2,1)S(1)} %get-tuple-element.128, bf16[1024,16,32]{0,2,1:T(8,128)(2,1)S(1)} %get-tuple-element.127, bf16[1,1024,16,32]{1,3,2,0:T(8,128)(2,1)S(1)} %get-tuple-element.135, bf16[1,1024,16,32]{1,3,2,0:T(8,128)(2,1)S(1)} %get-tuple-element.136, ...), kind=kOutput, calls=%fused_computation.143 | convolution fusion | flops 1105190912 | bytes 38305792 | tf_op jit(solution)/shard_map/while/body/eval_jaxpr/qhd,khd->hqk/dot_general | solution.py:47
  127.9 13.8 %fusion.89 = (f32[16,512]{1,0:T(8,128)S(1)}, f32[16,512,1024]{2,1,0:T(8,128)}) fusion(bf16[1024,16,32]{0,2,1:T(8,128)(2,1)S(1)} %get-tuple-element.128, bf16[1024,16,32]{0,2,1:T(8,128)(2,1)S(1)} %get-tuple-element.127, bf16[1,1024,16,32]{1,3,2,0:T(8,128)(2,1)S(1)} %get-tuple-element.136, bf16[1,1024,16,32]{1,3,2,0:T(8,128)(2,1)S(1)} %get-tuple-element.135, ...), kind=kOutput, calls=%fused_computation.144 | convolution fusion | flops 1105190912 | bytes 38305792 | tf_op jit(solution)/shard_map/while/body/eval_jaxpr/qhd,khd->hqk/dot_general | solution.py:47
  141.8 14.3 %fusion.1 = f32[16,512]{1,0:T(8,128)S(1)} fusion(f32[16,512,1024]{2,1,0:T(8,128)} %get-tuple-element.144, f32[16,512]{1,0:T(8,128)S(1)} %get-tuple-element.143), kind=kLoop, calls=%fused_computation.13 | loop fusion | flops 16769024 | bytes 33619968 | tf_op jit(solution)/shard_map/while/body/eval_jaxpr/reduce_sum | solution.py:64
  162.6 13.7 %fusion.65 = f32[512,16,64]{0,2,1:T(8,128)S(1)} fusion(bf16[1024,16,64]{0,2,1:T(8,128)(2,1)S(1)} %bitcast.185, f32[16,512,1024]{2,1,0:T(8,128)} %get-tuple-element.144, f32[16,512]{1,0:T(8,128)S(1)} %fusion.1, f32[16,512]{1,0:T(8,128)S(1)} %get-tuple-element.143), kind=kOutput, calls=%fused_computation.111 | convolution fusion | flops 1098907648 | bytes 37814272 | tf_op jit(solution)/shard_map/while/body/eval_jaxpr/hqk,khd->qhd/dot_general | solution.py:66
  176.3 14.9 %fusion = f32[16,512]{1,0:T(8,128)S(1)} fusion(f32[16,512,1024]{2,1,0:T(8,128)} %get-tuple-element.146, f32[16,512]{1,0:T(8,128)S(1)} %get-tuple-element.145), kind=kLoop, calls=%fused_computation.12 | loop fusion | flops 16769024 | bytes 33619968 | tf_op jit(solution)/shard_map/while/body/eval_jaxpr/reduce_sum | solution.py:64
  191.2 12.9 fusion.66
  214.2 85.5 %all-gather.20.cloned.1.call-done = bf16[1024,2816]{1,0:T(8,128)(2,1)} async-done(((bf16[256,2816]{1,0:T(8,128)(2,1)}), bf16[1024,2816]{1,0:T(8,128)(2,1)}) %all-gather.20.cloned.1.call-update) | async-done | bytes 5767184 | tf_op jit(solution)/shard_map/all_gather | solution.py:125
  299.7 11.8 fusion.92
  311.4 94.7 %all-gather.18.cloned.1.call-done = bf16[1024,2816]{1,0:T(8,128)(2,1)} async-done(((bf16[256,2816]{1,0:T(8,128)(2,1)}), bf16[1024,2816]{1,0:T(8,128)(2,1)}) %all-gather.18.cloned.1.call-update) | async-done | bytes 5767184 | tf_op jit(solution)/shard_map/all_gather | solution.py:124
  406.1 12.2 fusion.91
  418.3 94.4 %all-gather.22.cloned.1.call-done = bf16[2816,1024]{1,0:T(8,128)(2,1)} async-done(((bf16[704,1024]{1,0:T(8,128)(2,1)}), bf16[2816,1024]{1,0:T(8,128)(2,1)}) %all-gather.22.cloned.1.call-update) | async-done | bytes 5767184 | tf_op jit(solution)/shard_map/all_gather | solution.py:126
  512.8 21.7 %multiply_convert_fusion.2 = (bf16[1024,2816]{1,0:T(8,128)(2,1)}, bf16[1024,2816]{1,0:T(8,128)(2,1)}, bf16[1024,2816]{1,0:T(8,128)(2,1)}) fusion(f32[1024,2816]{1,0:T(8,128)} %fusion.91, f32[1024,2816]{1,0:T(8,128)} %fusion.92, bf16[2816,1024]{1,0:T(8,128)(2,1)} %all-gather.22.cloned.1.call-done, bf16[1,1024,1024]{2,1,0:T(8,128)(2,1)S(1)} %copy-done.18), kind=kOutput, calls=%fused_computation.22 | convolution fusion | flops 5948833792 | bytes 48234496 | tf_op jit(solution)/shard_map/nd,fd->nf/dot_general | solution.py:176
  565.7 16.2 %fusion.4 = f32[16,64,1024]{2,1,0:T(8,128)} fusion(bf16[512,16,64]{0,2,1:T(8,128)(2,1)S(1)} %bitcast.190, f32[16,512,1024]{2,1,0:T(8,128)} %get-tuple-element.144, f32[16,512]{1,0:T(8,128)S(1)} %log_add_fusion), kind=kOutput, calls=%fused_computation.16 | convolution fusion | flops 1090519040 | bytes 38830080 | tf_op jit(solution)/shard_map/while/body/eval_jaxpr/hqk,qhd->khd/dot_general | solution.py:83
  581.9 22.5 %multiply_reduce_fusion.1 = (f32[16,512]{1,0:T(8,128)S(1)}, f32[16,512,1024]{2,1,0:T(8,128)}) fusion(f32[16,512,1024]{2,1,0:T(8,128)} %get-tuple-element.146, f32[16,512]{1,0:T(8,128)S(1)} %log_add_fusion.1, bf16[512,16,64]{0,2,1:T(8,128)(2,1)S(1)} %bitcast.192, bf16[1024,16,64]{0,2,1:T(8,128)(2,1)S(1)} %bitcast.188), kind=kOutput, calls=%fused_computation.4 | convolution fusion | flops 1098899456 | bytes 70320128 | tf_op jit(solution)/shard_map/while/body/eval_jaxpr/qhd,khd->hqk/dot_general | solution.py:86
  604.4 27.8 %multiply_convert_fusion.1 = bf16[16,512,1024]{2,1,0:T(8,128)(2,1)} fusion(f32[16,512,1024]{2,1,0:T(8,128)} %get-tuple-element.151, f32[16,512,1024]{2,1,0:T(8,128)} %get-tuple-element.146, f32[16,512]{1,0:T(8,128)S(1)} %get-tuple-element.150, f32[16,512]{1,0:T(8,128)S(1)} %log_add_fusion.1), kind=kLoop, calls=%fused_computation.3 | loop fusion | flops 33554432 | bytes 83951616 | tf_op jit(solution)/shard_map/while/body/eval_jaxpr/convert_element_type | solution.py:89
  632.2 17.8 %fusion.90 = (bf16[16,64,1024]{2,1,0:T(8,128)(2,1)}, f32[16,64,1024]{2,1,0:T(8,128)}) fusion(f32[16,64,1024]{2,1,0:T(8,128)} %fusion.4, bf16[512,16,64]{0,2,1:T(8,128)(2,1)S(1)} %bitcast.193, f32[16,512,1024]{2,1,0:T(8,128)} %get-tuple-element.146, f32[16,512]{1,0:T(8,128)S(1)} %log_add_fusion.1), kind=kOutput, calls=%fused_computation.145 | convolution fusion | flops 1095761920 | bytes 45121536 | tf_op jit(solution)/shard_map/while/body/eval_jaxpr/hqk,qhd->khd/dot_general | solution.py:83
  655.4 12.6 multiply_bitcast_fusion.2
  668.1 23.4 %multiply_reduce_fusion = (f32[16,512]{1,0:T(8,128)S(1)}, f32[16,512,1024]{2,1,0:T(8,128)}) fusion(f32[16,512,1024]{2,1,0:T(8,128)} %get-tuple-element.144, f32[16,512]{1,0:T(8,128)S(1)} %log_add_fusion, bf16[512,16,64]{0,2,1:T(8,128)(2,1)} %bitcast.191, bf16[1024,16,64]{0,2,1:T(8,128)(2,1)} %bitcast.187), kind=kOutput, calls=%fused_computation.1 | convolution fusion | flops 1098899456 | bytes 70320128 | tf_op jit(solution)/shard_map/while/body/eval_jaxpr/qhd,khd->hqk/dot_general | solution.py:86
  691.5 28.4 %multiply_convert_fusion = bf16[16,512,1024]{2,1,0:T(8,128)(2,1)} fusion(f32[16,512,1024]{2,1,0:T(8,128)} %get-tuple-element.153, f32[16,512,1024]{2,1,0:T(8,128)} %get-tuple-element.144, f32[16,512]{1,0:T(8,128)S(1)} %get-tuple-element.152, f32[16,512]{1,0:T(8,128)S(1)} %log_add_fusion), kind=kLoop, calls=%fused_computation | loop fusion | flops 33554432 | bytes 83951616 | tf_op jit(solution)/shard_map/while/body/eval_jaxpr/convert_element_type | solution.py:89
  719.9 12.7 multiply_bitcast_fusion.1
  737.6 10.9 fusion.78
  773.4 11.2 convolution_convert_fusion.2
  795.6 11.1 convolution_convert_fusion
  811.9 46.1 %all-reduce.2 = (f32[1]{0:T(128)}, f32[1]{0:T(128)}) all-reduce(f32[1]{0:T(128)} %bitcast.46, f32[1]{0:T(128)} %bitcast.45), channel_id=1, replica_groups=mesh['dp'=8,'fsdp'=4] {'dp','fsdp'}, use_global_device_ids=true, to_apply=%region_36.37 | all-reduce | flops 2 | bytes 16 | tf_op jit(solution)/shard_map/psum | solution.py:158
  859.9 104.1 %reduce-scatter.16.cloned.1.call-done = bf16[256,2816]{1,0:T(8,128)(2,1)} async-done(((bf16[1024,2816]{1,0:T(8,128)(2,1)}), bf16[256,2816]{1,0:T(8,128)(2,1)}) %reduce-scatter.16.cloned.1.call-update) | async-done | bytes 1441808 | tf_op jit(solution)/shard_map/reduce_scatter | solution.py:229
  964.0 105.1 %reduce-scatter.18.cloned.1.call-done = bf16[256,2816]{1,0:T(8,128)(2,1)} async-done(((bf16[1024,2816]{1,0:T(8,128)(2,1)}), bf16[256,2816]{1,0:T(8,128)(2,1)}) %reduce-scatter.18.cloned.1.call-update) | async-done | bytes 1441808 | tf_op jit(solution)/shard_map/reduce_scatter | solution.py:232
  1069.1 105.0 %reduce-scatter.20.cloned.1.call-done = bf16[704,1024]{1,0:T(8,128)(2,1)} async-done(((bf16[2816,1024]{1,0:T(8,128)(2,1)}), bf16[704,1024]{1,0:T(8,128)(2,1)}) %reduce-scatter.20.cloned.1.call-update) | async-done | bytes 1441808 | tf_op jit(solution)/shard_map/reduce_scatter | solution.py:235
  1174.1 11.5 fusion.34
  1214.9 14.2 %all-reduce.3 = (bf16[256]{0:T(256)(128)(2,1)S(1)}, bf16[256]{0:T(256)(128)(2,1)S(1)}) all-reduce(bf16[256]{0:T(256)(128)(2,1)S(1)} %dynamic-slice.2, bf16[256]{0:T(256)(128)(2,1)S(1)} %dynamic-slice.4), channel_id=1, replica_groups=mesh['dp'=8,'fsdp'=4] {'dp'}, use_global_device_ids=true, to_apply=%region_15.16 | all-reduce | flops 512 | bytes 2048 | tf_op jit(solution)/shard_map/psum | solution.py:241
  1249.2 36.2 %all-reduce.8.cloned.1.call-done = (bf16[256,1024]{1,0:T(8,128)(2,1)}, bf16[256,1024]{1,0:T(8,128)(2,1)}, bf16[256,1024]{1,0:T(8,128)(2,1)}, bf16[256,1024]{1,0:...) async-done(((bf16[256,1024]{1,0:T(8,128)(2,1)}, bf16[256,1024]{1,0:T(8,128)(2,1)}, bf16[256,1024]{1,0:T(8,128)(2,1)}, ...) | async-done | bytes 6422544 | tf_op jit(solution)/shard_map/psum | solution.py:242
  (214 shorter events, 214.2 us)
Async XLA Ops:
  7.2 47.8 %all-gather.14.cloned.1.call-start = ((), (), s32[]{:S(2)}) async-start(), calls=%async_computation.9 | async-start | bytes 2621440 | tf_op jit(solution)/shard_map/all_gather | solution.py:120
  7.9 93.4 %all-gather.12.cloned.1.call-start = ((), (), s32[]{:S(2)}) async-start(), calls=%async_computation.8 | async-start | bytes 2621440 | tf_op jit(solution)/shard_map/all_gather | solution.py:119
  8.7 147.4 %all-gather.10.cloned.1.call-start = ((), (), s32[]{:S(2)}) async-start(), calls=%async_computation.7 | async-start | bytes 2621440 | tf_op jit(solution)/shard_map/all_gather | solution.py:121
  9.4 197.2 %all-gather.16.cloned.1.call-start = ((), (), s32[]{:S(2)}) async-start(), calls=%async_computation.10 | async-start | bytes 2621440 | tf_op jit(solution)/shard_map/all_gather | solution.py:122
  10.0 289.7 %all-gather.20.cloned.1.call-start = ((), (), s32[]{:S(2)}) async-start(), calls=%async_computation.12 | async-start | bytes 7208960 | tf_op jit(solution)/shard_map/all_gather | solution.py:125
  10.6 395.6 %all-gather.18.cloned.1.call-start = ((), (), s32[]{:S(2)}) async-start(), calls=%async_computation.11 | async-start | bytes 7208960 | tf_op jit(solution)/shard_map/all_gather | solution.py:124
  11.2 501.6 %all-gather.22.cloned.1.call-start = ((), (), s32[]{:S(2)}) async-start(), calls=%async_computation.13 | async-start | bytes 7208960 | tf_op jit(solution)/shard_map/all_gather | solution.py:126
  11.9 848.0 %reduce-scatter.14.cloned.1.call-start = ((), (), s32[]{:S(2)}) async-start(), calls=%async_computation.17 | async-start | bytes 2621440 | tf_op jit(solution)/shard_map/reduce_scatter | solution.py:223
  28.4 127.7 %copy-start.33 = (f32[4,1,256]{2,1,0:T(1,128)}, f32[4,1,256]{2,1,0:T(1,128)S(1)}, u32[]{:S(2)}) copy-start(f32[4,1,256]{2,1,0:T(1,128)S(1)} %convert_element_type.336) | copy-start | bytes 12292
  32.1 174.6 %copy-start = (bf16[1,1024,1024]{1,2,0:T(8,128)(2,1)}, bf16[1,1024,1024]{1,2,0:T(8,128)(2,1)S(1)}, u32[]{:S(2)}) copy-start(bf16[1,1024,1024]{1,2,0:T(8,128)(2,1)S(1)} %copy.59) | copy-start | bytes 6291460
  32.6 123.5 %copy-start.35 = (f32[1024]{0:T(1024)}, f32[1024]{0:T(1024)S(1)}, u32[]{:S(2)}) copy-start(f32[1024]{0:T(1024)S(1)} %add_rsqrt_fusion.1) | copy-start | bytes 12292
  41.2 70.9 %copy-start.28 = (f32[1024,32]{0,1:T(8,128)}, f32[1024,32]{0,1:T(8,128)S(1)}, u32[]{:S(2)}) copy-start(f32[1024,32]{0,1:T(8,128)S(1)} %get-tuple-element.137) | copy-start | bytes 393220
  41.3 70.9 %copy-start.30 = (f32[1024,32]{0,1:T(8,128)}, f32[1024,32]{0,1:T(8,128)S(1)}, u32[]{:S(2)}) copy-start(f32[1024,32]{0,1:T(8,128)S(1)} %get-tuple-element.138) | copy-start | bytes 393220
  113.7 14.2 %copy-start.4 = (bf16[1,1024,16,32]{1,3,2,0:T(8,128)(2,1)}, bf16[1,1024,16,32]{1,3,2,0:T(8,128)(2,1)S(1)}, u32[]{:S(2)}) copy-start(bf16[1,1024,16,32]{1,3,2,0:T(8,128)(2,1)S(1)} %get-tuple-element.135) | copy-start | bytes 3145732
  113.7 14.2 %copy-start.6 = (bf16[1,1024,16,32]{1,3,2,0:T(8,128)(2,1)}, bf16[1,1024,16,32]{1,3,2,0:T(8,128)(2,1)S(1)}, u32[]{:S(2)}) copy-start(bf16[1,1024,16,32]{1,3,2,0:T(8,128)(2,1)S(1)} %get-tuple-element.136) | copy-start | bytes 3145732
  113.7 14.2 %copy-start.8 = (bf16[1024,16,32]{0,2,1:T(8,128)(2,1)}, bf16[1024,16,32]{0,2,1:T(8,128)(2,1)S(1)}, u32[]{:S(2)}) copy-start(bf16[1024,16,32]{0,2,1:T(8,128)(2,1)S(1)} %get-tuple-element.127) | copy-start | bytes 3145732
  162.6 28.6 %copy-start.2 = (bf16[1024,1024]{0,1:T(8,128)(2,1)}, bf16[1024,1024]{0,1:T(8,128)(2,1)S(1)}, u32[]{:S(2)}) copy-start(bf16[1024,1024]{0,1:T(8,128)(2,1)S(1)} %get-tuple-element.158) | copy-start | bytes 6291460
  214.2 85.5 %copy-start.20 = (bf16[1024,1024]{0,1:T(8,128)(2,1)}, bf16[1024,1024]{0,1:T(8,128)(2,1)S(1)}, u32[]{:S(2)}) copy-start(bf16[1024,1024]{0,1:T(8,128)(2,1)S(1)} %multiply_convert_fusion.6) | copy-start | bytes 6291460
  311.4 201.3 %copy-start.18 = (bf16[1,1024,1024]{2,1,0:T(8,128)(2,1)S(1)}, bf16[1,1024,1024]{2,1,0:T(8,128)(2,1)}, u32[]{:S(2)}) copy-start(bf16[1,1024,1024]{2,1,0:T(8,128)(2,1)} %param.17) | copy-start | bytes 6291460
  565.6 16.3 %copy-start.14 = (bf16[512,1024]{0,1:T(8,128)(2,1)}, bf16[512,1024]{0,1:T(8,128)(2,1)S(1)}, u32[]{:S(2)}) copy-start(bf16[512,1024]{0,1:T(8,128)(2,1)S(1)} %get-tuple-element.132) | copy-start | bytes 3145732
  565.7 294.2 %reduce-scatter.12.cloned.1.call-start = ((), (), s32[]{:S(2)}) async-start(), calls=%async_computation.16 | async-start | bytes 2621440 | tf_op jit(solution)/shard_map/reduce_scatter | solution.py:220
  565.7 16.2 %copy-start.3 = (bf16[1024,1024]{0,1:T(8,128)(2,1)S(1)}, bf16[1024,1024]{0,1:T(8,128)(2,1)}, u32[]{:S(2)}) copy-start(bf16[1024,1024]{0,1:T(8,128)(2,1)} %copy-done.2) | copy-start | bytes 6291460
  632.2 17.8 %copy-start.1 = (bf16[1,1024,1024]{1,2,0:T(8,128)(2,1)S(1)}, bf16[1,1024,1024]{1,2,0:T(8,128)(2,1)}, u32[]{:S(2)}) copy-start(bf16[1,1024,1024]{1,2,0:T(8,128)(2,1)} %copy-done) | copy-start | bytes 6291460
  632.2 17.9 %copy-start.34 = (f32[4,1,256]{2,1,0:T(1,128)S(1)}, f32[4,1,256]{2,1,0:T(1,128)}, u32[]{:S(2)}) copy-start(f32[4,1,256]{2,1,0:T(1,128)} %copy-done.33) | copy-start | bytes 12292
  632.2 17.9 %copy-start.36 = (f32[1024]{0:T(1024)S(1)}, f32[1024]{0:T(1024)}, u32[]{:S(2)}) copy-start(f32[1024]{0:T(1024)} %copy-done.35) | copy-start | bytes 12292
  691.5 168.4 %reduce-scatter.10.cloned.1.call-start = ((), (), s32[]{:S(2)}) async-start(), calls=%async_computation.15 | async-start | bytes 2621440 | tf_op jit(solution)/shard_map/reduce_scatter | solution.py:217
  732.6 15.9 %slice-start = ((s8[16777216]{0:T(1024)(128)(4,1)}), s8[4194304]{0:T(1024)(128)(4,1)S(1)}, s32[]{:S(2)}) async-start(s8[16777216]{0:T(1024)(128)(4,1)} %bitcast.183), calls=%async_computation.22 | async-start | bytes 8388608
  768.0 91.9 %reduce-scatter.8.cloned.1.call-start = ((), (), s32[]{:S(2)}) async-start(), calls=%async_computation.14 | async-start | bytes 2621440 | tf_op jit(solution)/shard_map/reduce_scatter | solution.py:214
  773.3 190.6 %reduce-scatter.16.cloned.1.call-start = ((), (), s32[]{:S(2)}) async-start(), calls=%async_computation.18 | async-start | bytes 7208960 | tf_op jit(solution)/shard_map/reduce_scatter | solution.py:229
  784.6 284.4 %reduce-scatter.18.cloned.1.call-start = ((), (), s32[]{:S(2)}) async-start(), calls=%async_computation.19 | async-start | bytes 7208960 | tf_op jit(solution)/shard_map/reduce_scatter | solution.py:232
  795.6 378.4 %reduce-scatter.20.cloned.1.call-start = ((), (), s32[]{:S(2)}) async-start(), calls=%async_computation.20 | async-start | bytes 7208960 | tf_op jit(solution)/shard_map/reduce_scatter | solution.py:235
  806.7 478.7 %all-reduce.8.cloned.1.call-start = ((), (), s32[]{:S(2)}) async-start(), calls=%async_computation.21 | async-start | bytes 12845056 | tf_op jit(solution)/shard_map/psum | solution.py:242
  (33 other events, 191.2 us)
Sparse Core Ops, SparseCore 0:
  9.6 45.3 all-gather.13
  56.6 44.6 all-gather.11
  102.9 44.6 all-gather.9
  149.0 44.6 all-gather.15
  195.1 104.5 all-gather.19
  301.1 104.9 all-gather.17
  407.7 104.9 all-gather.21
  565.8 42.6 reduce-scatter.13
  691.6 42.5 reduce-scatter.11
  768.1 42.4 reduce-scatter.9
  813.6 44.3 reduce-scatter.7
  860.1 103.7 reduce-scatter.15
  966.3 102.7 reduce-scatter.17
  1071.2 102.7 reduce-scatter.19
  1178.0 107.3 all-reduce.7
where the time goes:
time: 1320 us; the launch traced here: 1310 us
  waiting for transfers between devices  684 us (52%)
  matrix products  342 us (26%)
  other arithmetic  139 us (11%)
  blocking collectives  83.2 us (6%)
  local copies, waits for them, and re-layouts  41.1 us (3%)
  between operations  15.5 us (1%)
    reduce_scatter x1, waiting for transfers between devices, local(): lax.psum_scatter(grad_wu.astype(jnp.bfloat16), 'fsdp', scatter_dimension=...  105 us
    reduce_scatter x1, waiting for transfers between devices, local(): lax.psum_scatter(grad_wd.astype(jnp.bfloat16), 'fsdp', scatter_dimension=...  105 us
    reduce_scatter x1, waiting for transfers between devices, local(): lax.psum_scatter(grad_wg.astype(jnp.bfloat16), 'fsdp', scatter_dimension=...  104 us
    all_gather x1, waiting for transfers between devices, local(): lax.all_gather(w_gate, 'fsdp', axis=0, tiled=True)  94.7 us
    all_gather x1, waiting for transfers between devices, local(): lax.all_gather(w_down, 'fsdp', axis=0, tiled=True)  94.4 us
    all_gather x1, waiting for transfers between devices, local(): lax.all_gather(w_up, 'fsdp', axis=0, tiled=True)  85.5 us
    convert_element_type x2, other arithmetic, attend_backward(): grad_scores = (probs * (grad_probs - jnp.sum(probs * grad_probs, -1, keep...  56.2 us
    psum x1, blocking collectives, local(): lax.psum((jnp.sum(vf * vf), jnp.sum(mixed_wide * mixed_wide)), ('dp', 'fs...  46.1 us
  transfers between devices with their start and end apart: 15, of which 9 were waited for; matrix products, arithmetic and copies ran while one was open for 35% of the time, Pallas kernels for 0%

commit v1 on v0

v1 whole, which is shorter than its diff:
```python
import jax
import jax.numpy as jnp
from jax import lax
from jax.experimental import pallas as pl
from jax.experimental.pallas import tpu as pltpu
from jax.sharding import PartitionSpec as P

HEADS = 16
HEAD_DIM = 64
EPS = 1e-06
NEG = -1e30
QB = 256
G = 32
L = 128
bf16 = jnp.bfloat16
f32 = jnp.float32
ANY = pl.BlockSpec(memory_space=pl.ANY)
SMEM = pl.BlockSpec(memory_space=pltpu.SMEM)


def params(mib=58):
    return pltpu.CompilerParams(vmem_limit_bytes=mib * 2**20)


def cost(flops, moved):
    return pl.CostEstimate(flops=int(flops), bytes_accessed=int(moved), transcendentals=0)


def shape(dims, dtype=bf16):
    return jax.ShapeDtypeStruct(dims, dtype)


def nt(a, b):
    return lax.dot_general(a, b, (((1,), (1,)), ((), ())), preferred_element_type=f32)


def nn(a, b):
    return lax.dot_general(a, b, (((1,), (0,)), ((), ())), preferred_element_type=f32)


def tn(a, b):
    return lax.dot_general(a, b, (((0,), (0,)), ((), ())), preferred_element_type=f32)


def fast_mesh(dp, fsdp, shard_rows):
    return dp == 8 and fsdp == 4 and shard_rows == 8 * G


def row_pieces(w, count):
    return w.reshape(count, G, w.shape[1] // L, L).transpose(0, 2, 1, 3)


def column_pieces(w, count):
    return w.reshape(w.shape[0] // G, G, count, L).transpose(2, 0, 1, 3)


def dp_swap(x, bit):
    return lax.ppermute(x, "dp", [(i, i ^ bit) for i in range(lax.axis_size("dp"))])


def after(x, *first):
    return lax.optimization_barrier((x, first))[0]


def fsdp_shift(x, step):
    size = lax.axis_size("fsdp")
    return lax.ppermute(x, "fsdp", [(i, (i + step) % size) for i in range(size)])


class Gather:
    def __init__(self, mine, extra=None):
        self.count = mine.shape[0]
        self.extras = None
        sent = mine if extra is None else jnp.concatenate([mine, extra[None]])
        far = [fsdp_shift(sent, s) for s in (1, 2, 3)]
        if extra is not None:
            self.extras = [extra] + [x[self.count] for x in far]
        self.start = jnp.stack([x[: self.count] for x in far])

    def near(self, *gate):
        self.start = after(self.start, *gate)
        self.x, self.y = dp_swap(self.start, 2), dp_swap(self.start, 4)

    def corner(self, *gate):
        cut = self.count // 2
        self.c1 = dp_swap(after(self.x[:, :cut], *gate), 4)
        self.c2 = dp_swap(after(self.y[:, cut:], *gate), 2)

    def core(self, *gate):
        self.other = [dp_swap(after(a, *gate), 1) for a in (self.start, self.x, self.y)]

    def core_corner(self, *gate):
        self.other += [dp_swap(after(a, *gate), 1) for a in (self.c1, self.c2)]

    def arrays(self):
        return [self.start, self.x, self.y, self.c1, self.c2] + self.other


def piece_sources(count):
    cut = count // 2
    found = []
    for core in range(2):
        for i, (mask, low, size) in enumerate(
            ((0, 0, count), (2, 0, count), (4, 0, count), (6, 0, cut), (6, cut, count - cut))
        ):
            found.append((5 * core + i, mask | core, low, size))
    return found


class Group:
    def __init__(self, tensors, arrays, whole):
        self.tensors, self.arrays, self.whole = tensors, list(arrays), whole

    def specs(self):
        return [ANY] * len(self.arrays)

    def fetch(self, index, refs, pos, scratch, sem):
        if self.whole:
            pltpu.make_async_copy(refs[index], scratch, sem).start()
            return
        z, d = pos[0], pos[1]
        at = sum(t[0] for t in self.tensors[:index])
        blocks, by_rows = self.tensors[index]

        def target(shard, piece, low, size):
            if by_rows:
                return scratch.at[pl.ds(low, size), shard * 8 + piece]
            return scratch.at[piece, pl.ds(shard * blocks + low, size)]

        for piece in range(8):
            pltpu.make_async_copy(
                refs[0].at[piece, pl.ds(at, blocks)], target(z, piece, 0, blocks), sem
            ).start()
        for array, mask, low, size in piece_sources(sum(t[0] for t in self.tensors)):
            begin, end = max(at, low), min(at + blocks, low + size)
            if end <= begin:
                continue
            for s in range(3):
                pltpu.make_async_copy(
                    refs[1 + array].at[s, pl.ds(begin - low, end - begin)],
                    target(lax.rem(z + 3 - s, 4), d ^ mask, begin - at, end - begin),
                    sem,
                ).start()


def wait_all(scratch, sem):
    pltpu.make_async_copy(scratch, scratch, sem).wait()


def two(w, i):
    rows = w.shape[1] * w.shape[2]
    return jnp.concatenate([w[2 * i].reshape(rows, L), w[2 * i + 1].reshape(rows, L)], 1)


def swap_halves(t):
    lane = lax.broadcasted_iota(jnp.int32, t.shape, 1) % 64
    return jnp.where(lane < 32, pltpu.roll(t, 96, 1), pltpu.roll(t, 32, 1))


def qkv_body(group, pos, x_ref, v1_ref, gain_ref, cos_ref, sin_ref, *rest):
    count = len(group.arrays)
    w_refs = rest[:count]
    q_ref, k_ref, v_ref, h_ref, ht_ref, sums_ref, *rest = rest[count:]
    outs, (wq, wk, wv, sem) = rest[:3], rest[3:]
    step = pl.program_id(0)
    length = x_ref.shape[0]

    @pl.when(step == 0)
    def _():
        for i, w in enumerate((wq, wk, wv)):
            group.fetch(i, w_refs, pos, w, sem.at[i])
        sums_ref[...] = jnp.zeros_like(sums_ref)
        for i in range(length // QB):
            rows = slice(i * QB, (i + 1) * QB)
            x = x_ref[rows, :].astype(f32)
            n1 = x * lax.rsqrt(jnp.mean(x * x, -1, keepdims=True) + EPS)
            h = n1 * gain_ref[...]
            h_ref[rows, :] = h.astype(bf16)
            ht_ref[:, :, :, rows] = h.T.astype(bf16).reshape(ht_ref.shape[:3] + (QB,))
        wait_all(wq, sem.at[0])
        wait_all(wk, sem.at[1])
        wait_all(wv, sem.at[2])
        for i, w in enumerate((wq, wk, wv)):
            pltpu.make_async_copy(w, outs[i], sem.at[3 + i]).start()

    cos, sin = cos_ref[...], sin_ref[...]
    h = h_ref[...]

    def rope(t):
        return jnp.concatenate(
            [t[:, i * L : (i + 1) * L] * cos + swap_halves(t[:, i * L : (i + 1) * L]) * sin for i in range(2)], 1
        )

    def pair(w):
        rows = w.shape[1] * G
        return jnp.concatenate([w[2 * step].reshape(rows, L), w[2 * step + 1].reshape(rows, L)], 1)

    q_ref[...] = (rope(nn(h, pair(wq))).astype(bf16).astype(f32) * 0.125).astype(bf16)
    k_ref[...] = rope(nn(h, pair(wk))).astype(bf16)
    v1 = v1_ref[...].astype(f32)
    vm = (0.5 * nn(h, pair(wv)) + 0.5 * v1).astype(bf16)
    v_ref[...] = vm
    vm = vm.astype(f32)
    total_1 = jnp.sum((v1 * v1).reshape(length // 8, 8, 2 * L), 0)
    total_2 = jnp.sum((vm * vm).reshape(length // 8, 8, 2 * L), 0)
    sums_ref[0] += total_1
    sums_ref[1] += total_2

    @pl.when(step == pl.num_programs(0) - 1)
    def _():
        for i, w in enumerate((wq, wk, wv)):
            pltpu.make_async_copy(w, outs[i], sem.at[3 + i]).wait()


def qkv(pos, x, v1, gain, cos_w, sin_w, group):
    length, width = x.shape
    blocks = width // L
    col = pl.BlockSpec((length, 2 * L), lambda i: (0, i))

    def fixed(*dims):
        return pl.BlockSpec(dims, lambda i: (0,) * len(dims))

    weight = pltpu.VMEM((blocks, width // G, G, L), bf16)
    return pl.pallas_call(
        lambda *refs: qkv_body(group, *refs),
        grid=(blocks // 2,),
        in_specs=[SMEM, fixed(length, width), col, fixed(1, width), fixed(length, L), fixed(length, L)]
        + group.specs(),
        out_specs=[col, col, col, fixed(length, width), fixed(width // G // 2, 2, G, length), fixed(2, 8, 2 * L)] + [ANY] * 3,
        out_shape=[
            shape((length, width)),
            shape((length, width)),
            shape((length, width)),
            shape((length, width)),
            shape((width // G // 2, 2, G, length)),
            shape((2, 8, 2 * L), f32),
        ]
        + [shape((blocks, width // G, G, L))] * 3,
        scratch_shapes=[weight, weight, weight, pltpu.SemaphoreType.DMA((6,))],
        compiler_params=params(),
        cost_estimate=cost(6 * length * width * width, 24 * length * width),
        name="qkv",
    )(pos, x, v1, gain, cos_w, sin_w, *group.arrays)
def half_mask(rows, which):
    lane = lax.broadcasted_iota(jnp.int32, (rows, 128), 1)
    return (lane < 64) if which == 0 else (lane >= 64)


def pick(x, which):
    return jnp.where(half_mask(x.shape[0], which), x, jnp.zeros_like(x))


def attend_fwd_body(q_ref, k_ref, v_ref, end_ref, keep_ref, *rest):
    o_ref, lse_ref, bias = rest[-3:]
    pair = pl.program_id(0)
    length = q_ref.shape[0]
    blocks = length // QB

    @pl.when(pair == 0)
    def _():
        for i in range(blocks):
            size = (i + 1) * QB
            q_at = lax.broadcasted_iota(jnp.int32, (QB, size), 0) + i * QB
            k_at = lax.broadcasted_iota(jnp.int32, (QB, size), 1)
            ok = (q_at >= k_at) & (q_at < end_ref[:, :size])
            bias[i * QB : (i + 1) * QB, :size] = jnp.where(ok, 0.0, NEG)

    lane = lax.broadcasted_iota(jnp.int32, (QB, 128), 1)
    for i in range(blocks):
        rows = slice(i * QB, (i + 1) * QB)
        size = (i + 1) * QB
        outs = []
        old = lse_ref[rows, :]
        for h in range(2):
            s = nt(pick(q_ref[rows, :], h), k_ref[:size, :]) + bias[rows, :size]
            top = jnp.max(s, -1, keepdims=True)
            expo = jnp.exp(s - top)
            total = jnp.sum(expo, -1, keepdims=True)
            outs.append(nn(expo.astype(bf16), v_ref[:size, :]) / total)
            old = jnp.where(lane == 2 * pair + h, top + jnp.log(total), old)
        lse_ref[rows, :] = old
        o = jnp.where(lane < 64, outs[0], outs[1]) * keep_ref[rows, :]
        o_ref[rows, :] = o.astype(bf16)


def attend_fwd(q, k, v, end_row, keep_col, first, pairs, before=None):
    length, width = q.shape
    col = pl.BlockSpec((length, 128), lambda p: (0, p + first))
    return pl.pallas_call(
        attend_fwd_body,
        grid=(pairs,),
        in_specs=[
            col,
            col,
            col,
            pl.BlockSpec((1, length), lambda p: (0, 0)),
            pl.BlockSpec((length, 1), lambda p: (0, 0)),
        ]
        + ([] if before is None else [ANY]),
        out_specs=[col, pl.BlockSpec((length, 128), lambda p: (0, 0))],
        out_shape=[
            jax.ShapeDtypeStruct((length, width), bf16),
            jax.ShapeDtypeStruct((length, 128), f32),
        ],
        scratch_shapes=[pltpu.VMEM((length, length), f32)],
        compiler_params=params(),
        cost_estimate=cost(5 * length * length * width, 16 * length * width),
        input_output_aliases={} if before is None else {5: 0},
        name="attend_fwd",
    )(q, k, v, end_row, keep_col, *([] if before is None else [before]))


def attend_bwd_body(
    q_ref, k_ref, v_ref, do_ref, lse_ref, first_ref, cos_ref, sin_ref, fg_ref, *rest,
):
    dq_ref, dk_ref, dv_ref, fo_ref, bias, dk_acc, dv_acc = rest[-7:]
    pair = pl.program_id(0)
    length = q_ref.shape[0]
    blocks = length // QB

    @pl.when(pair == 0)
    def _():
        for i in range(blocks):
            size = (i + 1) * QB
            k_at = lax.broadcasted_iota(jnp.int32, (size, QB), 0)
            q_at = lax.broadcasted_iota(jnp.int32, (size, QB), 1) + i * QB
            ok = (q_at >= k_at) & (k_at >= first_ref[:, i * QB : (i + 1) * QB])
            bias[:size, i * QB : (i + 1) * QB] = jnp.where(ok, 0.0, NEG)

    k_t = k_ref[...].astype(f32).T.astype(bf16)
    for i in reversed(range(blocks)):
        rows = slice(i * QB, (i + 1) * QB)
        size = (i + 1) * QB
        part_k = None
        part_v = None
        part_q = []
        for h in range(2):
            qh = pick(q_ref[rows, :], h)
            dh = pick(do_ref[rows, :], h)
            lse = lse_ref[pl.ds(2 * pair + h, 1), rows]
            p = jnp.exp(nt(k_ref[:size, :], qh) + bias[:size, rows] - lse)
            dp = nt(v_ref[:size, :], dh)
            delta = jnp.sum(p * dp, 0, keepdims=True)
            ds = (p * (dp - delta)).astype(bf16)
            av = nn(p.astype(bf16), dh)
            ak = nn(ds, qh)
            part_v = av if part_v is None else part_v + av
            part_k = ak if part_k is None else part_k + ak
            part_q.append(nn(k_t[h * 64 : (h + 1) * 64, :size], ds))
        if i == blocks - 1:
            dk_acc[...] = part_k
            dv_acc[...] = part_v
        else:
            dk_acc[:size, :] += part_k
            dv_acc[:size, :] += part_v
        dq = jnp.concatenate(part_q, 0).T * 0.125
        dq = dq * cos_ref[rows, :] + swap_halves(dq) * sin_ref[rows, :]
        dq_ref[rows, :] = dq.astype(bf16)
    dk = dk_acc[...]
    dk_ref[...] = (dk * cos_ref[...] + swap_halves(dk) * sin_ref[...]).astype(bf16)
    dv = dv_acc[...].astype(bf16).astype(f32) * 0.5
    dv_ref[...] = dv.astype(bf16)
    fo_ref[...] = fg_ref[...] + dv


def attend_bwd(q, k, v, do, lse_t, first_row, cos_w, sin_back, fgrad, first, pairs, before=None):
    length, width = q.shape
    col = pl.BlockSpec((length, 128), lambda p: (0, p + first))
    before = [] if before is None else list(before)

    def whole(a):
        return pl.BlockSpec(a.shape, lambda p: (0, 0))

    wide = jax.ShapeDtypeStruct((length, width), bf16)
    return pl.pallas_call(
        attend_bwd_body,
        grid=(pairs,),
        in_specs=[col] * 4 + [whole(lse_t), whole(first_row), whole(cos_w), whole(sin_back), col]
        + [ANY] * len(before),
        out_specs=[col] * 4,
        out_shape=[wide, wide, wide, jax.ShapeDtypeStruct((length, width), f32)],
        scratch_shapes=[
            pltpu.VMEM((length, length), f32),
            pltpu.VMEM((length, 128), f32),
            pltpu.VMEM((length, 128), f32),
        ],
        compiler_params=params(),
        cost_estimate=cost(12 * length * length * width, 24 * length * width),
        input_output_aliases={9 + i: i for i in range(len(before))},
        name="attend_bwd",
    )(q, k, v, do, lse_t, first_row, cos_w, sin_back, fgrad, *before)


def chosen_columns(ref, parity):
    blocks = ref.shape[1] // L
    return jnp.concatenate(
        [ref[:, pl.ds(pl.multiple_of((2 * p + parity) * L, L), L)] for p in range(blocks // 2)], 1
    )


def chosen_rows(ref, parity):
    return ref[:, parity].reshape(ref.shape[0] * G, ref.shape[3])


def wd_rows(wd, t):
    return jnp.concatenate([wd[c, pl.ds(8 * t, 8)].reshape(8 * G, L) for c in range(wd.shape[0])], 1)


def pair_at(w, t):
    rows = w.shape[1] * G
    return jnp.concatenate([w[2 * t].reshape(rows, L), w[2 * t + 1].reshape(rows, L)], 1)


def ffn_up_body(groups, pos, x_ref, o_ref, gain_ref, *rest):
    count = [len(g.arrays) for g in groups]
    refs_1, refs_2 = rest[: count[0]], rest[count[0] : sum(count)]
    (r1_ref, h_ref, ht_ref, hid_ref, ga_ref, ua_ref, wo_ref, wg_ref, wu_ref,
     wo, wg, wu, sem) = rest[sum(count):]
    step = pl.program_id(0)
    length = x_ref.shape[0]

    @pl.when(step == 0)
    def _():
        groups[0].fetch(0, refs_1, pos, wo, sem.at[0])
        groups[0].fetch(1, refs_1, pos, wg, sem.at[1])
        groups[1].fetch(0, refs_2, pos, wu, sem.at[2])
        wait_all(wo, sem.at[0])
        for i in range(length // QB):
            rows = slice(i * QB, (i + 1) * QB)
            r1 = x_ref[rows, :].astype(f32) + jnp.concatenate(
                [nn(o_ref[rows, :], two(wo, c)) for c in range(wo.shape[0] // 2)], 1
            )
            r1_ref[rows, :] = r1
            n2 = r1 * lax.rsqrt(jnp.mean(r1 * r1, -1, keepdims=True) + EPS)
            h = n2 * gain_ref[...]
            h_ref[rows, :] = h.astype(bf16)
            ht_ref[:, :, :, rows] = h.T.astype(bf16).reshape(ht_ref.shape[:3] + (QB,))
        wait_all(wg, sem.at[1])
        wait_all(wu, sem.at[2])
        pltpu.make_async_copy(wo, wo_ref, sem.at[3]).start()
        pltpu.make_async_copy(wg, wg_ref, sem.at[4]).start()
        pltpu.make_async_copy(wu, wu_ref, sem.at[5]).start()

    @pl.when(step > 0)
    def _():
        t = step - 1
        wgt, wut = pair_at(wg, t), pair_at(wu, t)
        for i in range(2):
            rows = slice(i * (length // 2), (i + 1) * (length // 2))
            gate = nn(h_ref[rows, :], wgt)
            up = nn(h_ref[rows, :], wut)
            sigma = 1.0 / (1.0 + jnp.exp(-gate))
            silu = gate * sigma
            hid_ref[rows, :] = (silu * up).astype(bf16)
            ga_ref[rows, :] = (up * (sigma + silu * (1.0 - sigma))).astype(bf16)
            ua_ref[rows, :] = silu.astype(bf16)

    @pl.when(step == pl.num_programs(0) - 1)
    def _():
        pltpu.make_async_copy(wo, wo_ref, sem.at[3]).wait()
        pltpu.make_async_copy(wg, wg_ref, sem.at[4]).wait()
        pltpu.make_async_copy(wu, wu_ref, sem.at[5]).wait()


def once(*dims):
    return pl.BlockSpec(dims, lambda i: (0,) * len(dims), pipeline_mode=pl.Buffered(1))


def ffn_up(pos, x, o, gain, groups, hidden):
    length, width = x.shape
    tiles = hidden // (2 * L)
    col = pl.BlockSpec((length, 2 * L), lambda i: (0, jnp.maximum(i - 1, 0)))
    ht_dims = (width // G // 2, 2, G, length)
    square = (width // L, width // G, G, L)
    wide = (hidden // L, width // G, G, L)
    return pl.pallas_call(
        lambda *refs: ffn_up_body(groups, *refs),
        grid=(1 + tiles,),
        in_specs=[SMEM, once(length, width), once(length, width), once(1, width)]
        + groups[0].specs()
        + groups[1].specs(),
        out_specs=[once(length, width), once(length, width), once(*ht_dims), col, col, col, ANY, ANY, ANY],
        out_shape=[
            shape((length, width), f32),
            shape((length, width)),
            shape(ht_dims),
            shape((length, hidden)),
            shape((length, hidden)),
            shape((length, hidden)),
            shape(square),
            shape(wide),
            shape(wide),
        ],
        scratch_shapes=[
            pltpu.VMEM(square, bf16),
            pltpu.VMEM(wide, bf16),
            pltpu.VMEM(wide, bf16),
            pltpu.SemaphoreType.DMA((6,)),
        ],
        compiler_params=params(),
        cost_estimate=cost(4 * length * width * hidden, 40 * length * width),
        name="ffn_up",
    )(pos, x, o, gain, *groups[0].arrays, *groups[1].arrays)


def ffn_down_body(group, pos, ht_ref, df_ref, hid_ref, ga_ref, ua_ref, *rest):
    count = len(group.arrays)
    dg_ref, du_ref, sg_ref, su_ref, sd_ref, wd_ref, wd, dfs, hts, sem = rest[count:]
    step = pl.program_id(0)
    length = df_ref.shape[0]

    @pl.when(step == 0)
    def _():
        group.fetch(0, rest[:count], pos, wd, sem.at[0])
        other = 1 - lax.rem(pos[1], 2)
        dfs[...] = chosen_columns(df_ref, other)
        hts[...] = chosen_rows(ht_ref, other)
        wait_all(wd, sem.at[0])
        pltpu.make_async_copy(wd, wd_ref, sem.at[1]).start()

    wdt = wd_rows(wd, step)
    for i in range(2):
        rows = slice(i * (length // 2), (i + 1) * (length // 2))
        dhid = nt(df_ref[rows, :], wdt)
        dg_ref[rows, :] = (dhid * ga_ref[rows, :].astype(f32)).astype(bf16)
        du_ref[rows, :] = (dhid * ua_ref[rows, :].astype(f32)).astype(bf16)
    gd = tn(hid_ref[...], dfs[...]).astype(bf16)
    for p in range(4):
        sd_ref[:, p] = gd[:, p * L : (p + 1) * L].reshape(8, G, L)
    for ref, grad in ((sg_ref, dg_ref), (su_ref, du_ref)):
        g = nn(hts[...], grad[...]).astype(bf16)
        for c in range(2):
            ref[:, :, c] = g[:, c * L : (c + 1) * L].reshape(4, 4, G, L)

    @pl.when(step == pl.num_programs(0) - 1)
    def _():
        pltpu.make_async_copy(wd, wd_ref, sem.at[1]).wait()


def ffn_down(pos, ht, df, hid, ga, ua, group):
    length, width = df.shape
    hidden = hid.shape[1]
    col = pl.BlockSpec((length, 2 * L), lambda i: (0, i))
    grad_cols = pl.BlockSpec((4, 4, 2, G, L), lambda i: (0, 0, i, 0, 0))
    grad_rows = pl.BlockSpec((8, 4, G, L), lambda i: (i, 0, 0, 0))
    tall = (width // L, hidden // G, G, L)
    return pl.pallas_call(
        lambda *refs: ffn_down_body(group, *refs),
        grid=(hidden // (2 * L),),
        in_specs=[SMEM, once(*ht.shape), once(length, width), col, col, col] + group.specs(),
        out_specs=[col, col, grad_cols, grad_cols, grad_rows, ANY],
        out_shape=[
            shape((length, hidden)),
            shape((length, hidden)),
            shape((4, 4, hidden // L, G, L)),
            shape((4, 4, hidden // L, G, L)),
            shape((hidden // G, 4, G, L)),
            shape(tall),
        ],
        scratch_shapes=[
            pltpu.VMEM(tall, bf16),
            pltpu.VMEM((length, width // 2), bf16),
            pltpu.VMEM((width // 2, length), bf16),
            pltpu.SemaphoreType.DMA((2,)),
        ],
        compiler_params=params(),
        cost_estimate=cost(5 * length * width * hidden, 60 * length * width),
        name="ffn_down",
    )(pos, ht, df, hid, ga, ua, *group.arrays)


def ffn_back_body(pos, r1_ref, df_ref, keep_ref, gain_ref, wo, dg_ref, du_ref, wg, wu, dr_ref, da_ref, do_ref, acc):
    step = pl.program_id(0)
    length = r1_ref.shape[0]
    both = jnp.concatenate([dg_ref[...], du_ref[...]], 1)
    part = nt(both, jnp.concatenate([two(wg, 0), two(wu, 0)], 1))

    @pl.when(step == 0)
    def _():
        acc[...] = part

    @pl.when(step > 0)
    def _():
        acc[...] += part

    @pl.when(step == pl.num_programs(0) - 1)
    def _():
        for i in range(length // QB):
            rows = slice(i * QB, (i + 1) * QB)
            r1 = r1_ref[rows, :]
            rinv = lax.rsqrt(jnp.mean(r1 * r1, -1, keepdims=True) + EPS)
            n2 = r1 * rinv
            dn = acc[rows, :] * gain_ref[...]
            dr = df_ref[rows, :].astype(f32) + rinv * (dn - n2 * jnp.mean(dn * n2, -1, keepdims=True))
            dr_ref[rows, :] = dr
            da = dr.astype(bf16)
            da_ref[rows, :] = da
            do = nt(da, jnp.concatenate([two(wo, c) for c in range(wo.shape[0] // 2)], 1))
            do_ref[rows, :] = (do * keep_ref[rows, :]).astype(bf16)


def ffn_back(pos, r1, df, keep_col, gain, dgate, dup, wo, wg, wu):
    length, width = r1.shape
    hidden = dgate.shape[1]
    col = pl.BlockSpec((length, 2 * L), lambda i: (0, i))
    weight = pl.BlockSpec((2, width // G, G, L), lambda i: (i, 0, 0, 0))
    return pl.pallas_call(
        ffn_back_body,
        grid=(hidden // (2 * L),),
        in_specs=[SMEM, once(length, width), once(length, width), once(length, 1), once(1, width)]
        + [once(*wo.shape), col, col, weight, weight],
        out_specs=[once(length, width)] * 3,
        out_shape=[shape((length, width), f32), shape((length, width)), shape((length, width))],
        scratch_shapes=[pltpu.VMEM((length, width), f32)],
        compiler_params=params(),
        cost_estimate=cost(4 * length * width * hidden, 40 * length * width),
        name="ffn_back",
    )(pos, r1, df, keep_col, gain, wo, dgate, dup, wg, wu)


def bits(pos):
    d = pos[1]
    return lax.rem(d, 2), lax.rem(d // 2, 2), lax.rem(d // 4, 2)


def ffn_grads_body(pos, ht_ref, df_ref, hid_ref, dg_ref, du_ref, rg_ref, ru_ref, rd_ref,
                   sg, kg, su, ku, sa, ka, sb, kb, dfk, htk, tile, tiled):
    step = pl.program_id(0)
    core, b1, b2 = bits(pos)

    @pl.when(step == 0)
    def _():
        dfk[...] = chosen_columns(df_ref, core)
        htk[...] = chosen_rows(ht_ref, core)

    for send, keep, grad, got, by_x in ((sg, kg, dg_ref, rg_ref, True), (su, ku, du_ref, ru_ref, False)):
        g = nn(htk[...], grad[...])
        for c in range(2):
            tile[:, :, c] = (
                g[:, c * L : (c + 1) * L].reshape(4, 4, G, L) + got[:, :, c].astype(f32)
            ).astype(bf16)
        for i in range(2):
            if by_x:
                send[:, i] = tile[:, 2 * i + 1 - b1]
                keep[:, i] = tile[:, 2 * i + b1]
            else:
                send[:, i] = tile[:, 2 * (1 - b2) + i]
                keep[:, i] = tile[:, 2 * b2 + i]
    gd = tn(hid_ref[...], dfk[...])
    for p in range(4):
        tiled[:, p] = (gd[:, p * L : (p + 1) * L].reshape(8, G, L) + rd_ref[:, p].astype(f32)).astype(bf16)
    middle = pl.num_programs(0) // 2

    @pl.when(step <= middle)
    def _():
        for i in range(2):
            sa[:, i] = tiled[:, 2 * i + 1 - b1]
            ka[:, i] = tiled[:, 2 * i + b1]

    @pl.when(step >= middle)
    def _():
        for i in range(2):
            sb[:, i] = tiled[:, 2 * (1 - b2) + i]
            kb[:, i] = tiled[:, 2 * b2 + i]


def ffn_grads(pos, ht, df, hid, dgate, dup, got):
    length, width = df.shape
    hidden = hid.shape[1]
    tiles = hidden // (2 * L)
    middle = tiles // 2
    col = pl.BlockSpec((length, 2 * L), lambda i: (0, i))
    half = pl.BlockSpec((4, 2, 2, G, L), lambda i: (0, 0, i, 0, 0))
    rows_a = pl.BlockSpec((8, 2, G, L), lambda i: (jnp.minimum(i, middle), 0, 0, 0))
    rows_b = pl.BlockSpec((8, 2, G, L), lambda i: (jnp.maximum(i - middle, 0), 0, 0, 0))
    cols = shape((4, 2, hidden // L, G, L))
    rows = shape((8 * (middle + 1), 2, G, L))
    return pl.pallas_call(
        ffn_grads_body,
        grid=(tiles,),
        in_specs=[
            SMEM,
            once(*ht.shape),
            once(length, width),
            col,
            col,
            col,
            pl.BlockSpec((4, 4, 2, G, L), lambda i: (0, 0, i, 0, 0)),
            pl.BlockSpec((4, 4, 2, G, L), lambda i: (0, 0, i, 0, 0)),
            pl.BlockSpec((8, 4, G, L), lambda i: (i, 0, 0, 0)),
        ],
        out_specs=[half] * 4 + [rows_a, rows_a, rows_b, rows_b],
        out_shape=[cols] * 4 + [rows] * 4,
        scratch_shapes=[
            pltpu.VMEM((length, width // 2), bf16),
            pltpu.VMEM((width // 2, length), bf16),
            pltpu.VMEM((4, 4, 2, G, L), bf16),
            pltpu.VMEM((8, 4, G, L), bf16),
        ],
        compiler_params=params(),
        cost_estimate=cost(3 * length * width * hidden, 40 * length * width),
        name="ffn_grads",
    )(pos, ht, df, hid, dgate, dup, *got)


def ffn_out_body(r1_ref, hid_ref, wd, out_ref):
    out_ref[...] = (r1_ref[...] + nn(hid_ref[...], two(wd, 0))).astype(bf16)


def ffn_out(r1, hid, wd):
    length, width = r1.shape
    hidden = hid.shape[1]
    col = pl.BlockSpec((length, 2 * L), lambda i: (0, i))
    return pl.pallas_call(
        ffn_out_body,
        grid=(width // (2 * L),),
        in_specs=[col, once(length, hidden), pl.BlockSpec((2, hidden // G, G, L), lambda i: (i, 0, 0, 0))],
        out_specs=col,
        out_shape=shape((length, width)),
        compiler_params=params(),
        cost_estimate=cost(2 * length * width * hidden, 20 * length * width),
        name="ffn_out",
    )(r1, hid, wd)


def square_send_body(pos, o_ref, ht_ref, da_ref, dq_ref, dk_ref, dv_ref, out_ref, ot, left):
    step = pl.program_id(0)
    length = o_ref.shape[0]
    per = pl.num_programs(0) // 4

    @pl.when(step == 0)
    def _():
        other = 1 - lax.rem(pos[1], 2)
        for i in range(length // QB):
            rows = slice(i * QB, (i + 1) * QB)
            ot[:, :, :, rows] = o_ref[rows, :].astype(f32).T.astype(bf16).reshape(ot.shape[:3] + (QB,))
        left[0] = chosen_rows(ot, other)
        left[1] = chosen_rows(ht_ref, other)

    for i, ref in enumerate((da_ref, dq_ref, dk_ref, dv_ref)):

        @pl.when(step // per == i)
        def _():
            g = nn(left[min(i, 1)], ref[...]).astype(bf16)
            for c in range(2):
                out_ref[:, :, c] = g[:, c * L : (c + 1) * L].reshape(4, 4, G, L)


def square_keep_body(pos, o_ref, ht_ref, da_ref, dq_ref, dk_ref, dv_ref, got, sa, ka, sb, kb, ot, left, tile):
    step = pl.program_id(0)
    length = o_ref.shape[0]
    per = pl.num_programs(0) // 4
    core, b1, b2 = bits(pos)

    @pl.when(step == 0)
    def _():
        for i in range(length // QB):
            rows = slice(i * QB, (i + 1) * QB)
            ot[:, :, :, rows] = o_ref[rows, :].astype(f32).T.astype(bf16).reshape(ot.shape[:3] + (QB,))
        left[0] = chosen_rows(ot, core)
        left[1] = chosen_rows(ht_ref, core)

    for i, ref in enumerate((da_ref, dq_ref, dk_ref, dv_ref)):

        @pl.when(step // per == i)
        def _():
            g = nn(left[min(i, 1)], ref[...])
            for c in range(2):
                tile[:, :, c] = (
                    g[:, c * L : (c + 1) * L].reshape(4, 4, G, L) + got[:, :, c].astype(f32)
                ).astype(bf16)
            for j in range(2):
                if i < 2:
                    sa[:, j] = tile[:, 2 * j + 1 - b1]
                    ka[:, j] = tile[:, 2 * j + b1]
                else:
                    sb[:, j] = tile[:, 2 * (1 - b2) + j]
                    kb[:, j] = tile[:, 2 * b2 + j]


def square_grads(pos, o, ht, grads, got):
    length, width = o.shape
    per = width // (2 * L)
    tiles = 4 * per

    def quarter(which):
        return pl.BlockSpec((length, 2 * L), lambda i: (0, jnp.clip(i - which * per, 0, per - 1)))

    common = [SMEM, once(length, width), once(*ht.shape)] + [quarter(i) for i in range(4)]
    whole = pl.BlockSpec((4, 4, 2, G, L), lambda i: (0, 0, i, 0, 0))
    scratch = [pltpu.VMEM(ht.shape, bf16), pltpu.VMEM((2, width // 2, length), bf16)]
    estimate = cost(4 * length * width * width, 24 * length * width)
    if got is None:
        return pl.pallas_call(
            square_send_body,
            grid=(tiles,),
            in_specs=common,
            out_specs=whole,
            out_shape=shape((4, 4, 4 * width // L, G, L)),
            scratch_shapes=scratch,
            compiler_params=params(),
            cost_estimate=estimate,
            name="square_send",
        )(pos, o, ht, *grads)
    first = pl.BlockSpec((4, 2, 2, G, L), lambda i: (0, 0, jnp.minimum(i, 2 * per - 1), 0, 0))
    second = pl.BlockSpec((4, 2, 2, G, L), lambda i: (0, 0, jnp.maximum(i - 2 * per, 0), 0, 0))
    half = shape((4, 2, 2 * width // L, G, L))
    return pl.pallas_call(
        square_keep_body,
        grid=(tiles,),
        in_specs=common + [whole],
        out_specs=[first, first, second, second],
        out_shape=[half] * 4,
        scratch_shapes=scratch + [pltpu.VMEM((4, 4, 2, G, L), bf16)],
        compiler_params=params(),
        cost_estimate=estimate,
        name="square_keep",
    )(pos, o, ht, *grads, got)


def input_grad_body(x_ref, gain_ref, dr_ref, dq_ref, dk_ref, dv_ref, wq, wk, wv, out_ref, acc):
    step = pl.program_id(0)
    length = x_ref.shape[0]
    both = jnp.concatenate([dq_ref[...], dk_ref[...], dv_ref[...]], 1)
    part = nt(both, jnp.concatenate([two(w, 0) for w in (wq, wk, wv)], 1))

    @pl.when(step == 0)
    def _():
        acc[...] = part

    @pl.when(step > 0)
    def _():
        acc[...] += part

    @pl.when(step == pl.num_programs(0) - 1)
    def _():
        for i in range(length // QB):
            rows = slice(i * QB, (i + 1) * QB)
            x = x_ref[rows, :].astype(f32)
            rinv = lax.rsqrt(jnp.mean(x * x, -1, keepdims=True) + EPS)
            n1 = x * rinv
            dn = acc[rows, :] * gain_ref[...]
            out_ref[rows, :] = dr_ref[rows, :] + rinv * (dn - n1 * jnp.mean(dn * n1, -1, keepdims=True))


def input_grad(x, gain, dr1, dq, dk, dv, weights):
    length, width = x.shape
    col = pl.BlockSpec((length, 2 * L), lambda i: (0, i))
    weight = pl.BlockSpec((2, width // G, G, L), lambda i: (i, 0, 0, 0))
    return pl.pallas_call(
        input_grad_body,
        grid=(width // (2 * L),),
        in_specs=[once(length, width), once(1, width), once(length, width), col, col, col] + [weight] * 3,
        out_specs=once(length, width),
        out_shape=shape((length, width), f32),
        scratch_shapes=[pltpu.VMEM((length, width), f32)],
        compiler_params=params(),
        cost_estimate=cost(6 * length * width * width, 24 * length * width),
        name="input_grad",
    )(x, gain, dr1, dq, dk, dv, *weights)


def place_body(pos, *refs):
    pieces, outs = refs[:10], refs[10:]
    d = pos[1]
    for array, mask, low, size in piece_sources(pieces[0].shape[1]):
        rows = pl.ds(pl.multiple_of((d ^ mask) * G, G), G)
        for c in range(size):
            which, at = 0, low + c
            while at >= outs[which].shape[1] // L:
                at -= outs[which].shape[1] // L
                which += 1
            outs[which][rows, at * L : (at + 1) * L] = pieces[array][0, c].astype(f32)


def place(pos, arrays, widths, rows):
    vmem = pl.BlockSpec(memory_space=pltpu.VMEM)
    return pl.pallas_call(
        place_body,
        in_specs=[SMEM] + [vmem] * 10,
        out_specs=[vmem] * len(widths),
        out_shape=[shape((rows, w), f32) for w in widths],
        compiler_params=params(),
        name="place",
    )(pos, *arrays)


def layout(lengths, length):
    position = jnp.arange(length, dtype=jnp.int32)
    ends = jnp.cumsum(lengths).astype(jnp.int32)
    seg = jnp.sum((position[:, None] >= ends[None, :]).astype(jnp.int32), 1)
    onehot = seg[:, None] == jnp.arange(lengths.shape[0], dtype=jnp.int32)[None, :]
    first = jnp.sum(jnp.where(onehot, (ends - lengths)[None, :], 0), 1)
    last = jnp.sum(jnp.where(onehot, ends[None, :], 0), 1)
    rel = (position - first).astype(f32)
    inverse = 10000.0 ** (-jnp.arange(HEAD_DIM // 2, dtype=f32) * 2.0 / HEAD_DIM)
    angle = rel[:, None] * inverse[None, :]
    keep = (seg < lengths.shape[0] - 1).astype(f32)
    cos, sin = jnp.cos(angle), jnp.sin(angle)
    cos_w = jnp.concatenate([cos] * 4, 1)
    sin_w = jnp.concatenate([-sin, sin] * 2, 1)
    return cos_w, sin_w, first[None, :], last[None, :], keep[:, None]


def add(*terms):
    total = terms[0].astype(f32)
    for t in terms[1:]:
        total = total + t.astype(f32)
    return total


def halve(kept, got, bit):
    picked = []
    for at in (1 - bit, bit):
        parts = [lax.dynamic_index_in_dim(x, at, 1, keepdims=False) for x in (kept, got)]
        picked.append(add(*parts).astype(bf16))
    return picked


def in_parts(sums):
    parts = []
    for _ in range(3):
        part = lax.reduce_precision(sums, 8, 7)
        parts.append(part)
        sums = sums - part
    return jnp.pad(jnp.stack(parts).astype(bf16), ((0, G - 3), (0, L - 2)))


def from_parts(block):
    parts = block[..., :3, :2].astype(f32)
    return parts[..., 0, :] + parts[..., 1, :] + parts[..., 2, :]


def over_fsdp(total, z, extra=None):
    terms = [lax.dynamic_index_in_dim(total, z, 0, keepdims=False)]
    extras = [extra]
    for s in (1, 2, 3):
        away = lax.dynamic_index_in_dim(total, lax.rem(z + s, 4), 0, keepdims=False)
        if extra is not None:
            away = jnp.concatenate([away, extra[None]])
        came = fsdp_shift(away, s)
        if extra is not None:
            extras.append(came[-1])
            came = came[:-1]
        terms.append(came)
    sums = None
    if extra is not None:
        numbers = jnp.stack([from_parts(e) for e in extras])
        for shard in range(4):
            term = lax.dynamic_index_in_dim(numbers, lax.rem(z + 4 - shard, 4), 0, keepdims=False)
            sums = term if sums is None else sums + term
    return add(*terms).astype(bf16), sums


def unfold_rows(w):
    return w.transpose(0, 2, 1, 3).reshape(w.shape[0] * G, w.shape[1] * L)


def sum_whole(grad):
    part = lax.psum_scatter(grad.astype(bf16), "fsdp", scatter_dimension=0, tiled=True)
    return lax.psum(part, "dp").astype(f32)


def local(
    layer_in, first_values, first_values_grad, cotangent, doc_lengths, norm1_gain,
    w_query, w_key, w_value, w_out, norm2_gain, w_gate, w_up, w_down,
):
    rows, length, width = layer_in.shape
    hidden = w_gate.shape[1]
    dp, fsdp = lax.axis_size("dp"), lax.axis_size("fsdp")
    fast = fast_mesh(dp, fsdp, w_query.shape[0])
    z, d = lax.axis_index("fsdp"), lax.axis_index("dp")
    b1, b2 = lax.rem(d // 2, 2), lax.rem(d // 4, 2)
    x, v1 = layer_in[0], first_values[0]
    df = cotangent[0]
    gains = jnp.stack([norm1_gain, norm2_gain])
    c, h = width // L, hidden // L
    members = (
        ((w_query, w_key, w_value), ((c, True),) * 3),
        ((w_out, w_gate), ((c, True), (h, True))),
        ((w_up,), ((h, True),)),
        ((w_down,), ((w_down.shape[0] // G, False),)),
    )
    if fast:
        pos = jnp.stack([z, d]).astype(jnp.int32)
        extra = jnp.pad(gains.reshape(-1, L), ((0, G - gains.size // L), (0, 0)))
        mines, owns = [], []
        for weights, tensors in members:
            pieces, owned = [], []
            for w, (_, by_rows) in zip(weights, tensors):
                if by_rows:
                    pieces.append(row_pieces(lax.dynamic_slice_in_dim(w, d * G, G, 0), 1)[0])
                    owned.append(row_pieces(w, 8))
                else:
                    pieces.append(column_pieces(lax.dynamic_slice_in_dim(w, d * L, L, 1), 1)[0])
                    owned.append(column_pieces(w, 8))
            mines.append(jnp.concatenate(pieces) if len(pieces) > 1 else pieces[0])
            owns.append(jnp.concatenate(owned, 1) if len(owned) > 1 else owned[0])
        g1 = Gather(mines[0], extra)
        far = jnp.stack([e[: gains.size // L].reshape(gains.shape) for e in g1.extras])
        g1.near()
        g2 = Gather(after(mines[1], g1.start))
        g1.corner()
        g1.core()
        g1.core_corner()
        g2.near()
        g3 = Gather(after(mines[2], g2.start))
        groups = [Group(members[0][1], [owns[0]] + g1.arrays(), False)]
        whole_gains = jnp.concatenate(
            [lax.dynamic_index_in_dim(far, lax.rem(z + 4 - j, 4), 0, keepdims=False) for j in range(4)], 1
        )
    else:
        pos = jnp.zeros((2,), jnp.int32)

        def blocks(w, by_rows):
            full = lax.all_gather(w, "fsdp", axis=0, tiled=True)
            return row_pieces(full, full.shape[0] // G).transpose(1, 0, 2, 3) if by_rows else column_pieces(full, c)

        whole_gains = lax.all_gather(gains, "fsdp", axis=1, tiled=True)
        groups = [
            Group(tensors, [blocks(w, t[1]) for w, t in zip(weights, tensors)], True)
            for weights, tensors in members
        ]
    whole_gains = whole_gains.astype(f32)
    gain_1, gain_2 = whole_gains[:1], whole_gains[1:]
    cos_w, sin_w, first_row, last_row, keep_col = layout(doc_lengths[0], length)

    q, k, vm, h1, h1t, sums, wq, wk, wv = qkv(pos, x, v1, gain_1, cos_w, sin_w, groups[0])
    squares = jnp.sum(sums, (1, 2))
    entries = rows * length * width * dp * fsdp
    if fast:
        g2.corner(q)
        g3.near(q)
        g4 = Gather(after(mines[3], g3.start, q))
    o, lse_1 = attend_fwd(q, k, vm, last_row, keep_col, 0, 3)
    if fast:
        g2.core(o)
        g2.core_corner(o)
        g3.corner(o)
    o, lse_2 = attend_fwd(q, k, vm, last_row, keep_col, 3, 3, o)
    if fast:
        g3.core(o)
        g4.near(o)
    o, lse_3 = attend_fwd(q, k, vm, last_row, keep_col, 6, 2, o)
    if fast:
        g3.core_corner(o)
        g4.corner(o)
        g4.core(o)
        groups += [Group(members[i][1], [owns[i]] + g.arrays(), False) for i, g in ((1, g2), (2, g3))]
    r1, h2, h2t, hid, ga, ua, wo, wg, wu = ffn_up(pos, x, o, gain_2, groups[1:3], hidden)
    if fast:
        g4.core_corner(r1)
        groups.append(Group(members[3][1], [owns[3]] + g4.arrays(), False))
    dgate, dup, sg, su, sd, wd = ffn_down(pos, h2t, df, hid, ga, ua, groups[3])
    if fast:
        got = [dp_swap(g, 1) for g in (sg, su, sd)]
    else:
        got = [jnp.zeros_like(g) for g in (sg, su, sd)]
    dr1, da, do = ffn_back(pos, r1, df, keep_col, gain_2, dgate, dup, wo, wg, wu)
    tg, kg, tu, ku, ta, ka, tb, kb = ffn_grads(pos, h2t, df, hid, dgate, dup, after(got, da))
    if fast:
        ng, na, nu, nb = dp_swap(tg, 2), dp_swap(ta, 2), dp_swap(tu, 4), dp_swap(tb, 4)
    back = (first_row, cos_w, -sin_w, first_values_grad[0])
    results = attend_bwd(q, k, vm, after(do, tg), lse_1.T, *back, 0, 3)
    results = attend_bwd(q, k, vm, do, lse_2.T, *back, 3, 3, results)
    dq, dk, dv, first_out = attend_bwd(q, k, vm, do, lse_3.T, *back, 6, 2, results)
    grads = (da, dq, dk, dv)
    if fast:
        ng, na, nu, nb = after((ng, na, nu, nb), dq)
        tg, kg = halve(kg, ng, b2)
        ta, ka = halve(ka, na, b2)
        tu, ku = halve(ku, nu, b1)
        tb, kb = halve(kb, nb, b1)
        mg, ma, mu, mb = dp_swap(tg, 4), dp_swap(ta, 4), dp_swap(tu, 2), dp_swap(tb, 2)
    send = square_grads(pos, o, h1t, grads, None)
    swapped = dp_swap(send, 1) if fast else jnp.zeros_like(send)
    d_x = input_grad(after(x, send), gain_1, dr1, dq, dk, dv, (wq, wk, wv))
    swapped = after(swapped, d_x)
    if fast:
        mg, ma, mu, mb = after((mg, ma, mu, mb), d_x)
        total_g = add(kg, mg).astype(bf16)
        total_a = add(ka, ma).astype(bf16)
        total_u = add(ku, mu).astype(bf16)
        total_b = add(kb, mb).astype(bf16)
        count = hidden // G
        edge = count // 2
        skip = count - total_b.shape[0]
        total_d = jnp.concatenate([total_a[:edge], total_b[edge - skip :]]).reshape(4, count // 4, G, L)
        reduced, sums_z = over_fsdp(jnp.concatenate([total_g, total_u, total_d], 1), z, in_parts(squares))
        wide = lax.all_gather(jnp.concatenate([reduced, in_parts(sums_z)[None]]), "dp")
        squares = jnp.sum(from_parts(wide[:, -1]), 0)
        wide = wide[:, :-1].astype(f32)
        n = hidden // L
        grad_wg, grad_wu = unfold_rows(wide[:, :n]), unfold_rows(wide[:, n : 2 * n])
        grad_wd = wide[:, 2 * n :].transpose(1, 2, 0, 3).reshape(hidden // 4, width)

    ts, ks, tt, kt = square_grads(pos, o, h1t, grads, swapped)
    if fast:
        ns, n_t = dp_swap(ts, 2), dp_swap(tt, 4)
    out = ffn_out(r1, after(hid, ts), wd)
    if fast:
        ns, n_t = after((ns, n_t), out)
        ts, ks = halve(ks, ns, b2)
        tt, kt = halve(kt, n_t, b1)
        total_s = add(ks, dp_swap(ts, 4)).astype(bf16)
        total_t = add(kt, dp_swap(tt, 2)).astype(bf16)
        reduced, _ = over_fsdp(jnp.concatenate([total_s, total_t], 1), z)
        last = Gather.__new__(Gather)
        last.count, last.start = reduced.shape[0], reduced[None]
        last.near()
        last.corner()
        last.core()
        last.core_corner()
        grad_wo, grad_wq, grad_wk, grad_wv = place(pos, last.arrays(), [width] * 4, w_query.shape[0])
    else:
        grad_wg = join(kg, tg, sg, True)
        grad_wu = join(ku, tu, su, False)
        squares = lax.psum(squares, ("dp", "fsdp"))
        count = hidden // G
        edge = count // 2
        skip = count - kb.shape[0]
        even = jnp.concatenate(
            [jnp.stack([ka, ta], 2)[:edge].reshape(edge, 4, G, L), jnp.stack([kb, tb], 1)[edge - skip :].reshape(edge, 4, G, L)]
        )
        grad_wd = jnp.stack([even, sd], 2).reshape(count, 8, G, L).transpose(0, 2, 1, 3).reshape(hidden, width)
        n = width // L
        firsts = join(ks, ts, send[:, :, : 2 * n], True)
        seconds = join(kt, tt, send[:, :, 2 * n :], False)
        grad_wo, grad_wq = firsts[:, :width], firsts[:, width:]
        grad_wk, grad_wv = seconds[:, :width], seconds[:, width:]
        grad_wo, grad_wq, grad_wk, grad_wv, grad_wg, grad_wu, grad_wd = [
            sum_whole(g) for g in (grad_wo, grad_wq, grad_wk, grad_wv, grad_wg, grad_wu, grad_wd)
        ]
    def along(*pairs):
        return sum(jnp.sum(w.astype(f32) * g, 1) for w, g in pairs)

    grad_g1 = along((w_query, grad_wq), (w_key, grad_wk), (w_value, grad_wv)) / norm1_gain.astype(f32)
    grad_g2 = along((w_gate, grad_wg), (w_up, grad_wu)) / norm2_gain.astype(f32)
    return (
        out[None], d_x[None], first_out[None], grad_g1, grad_wq, grad_wk, grad_wv, grad_wo, grad_g2,
        grad_wg, grad_wu, grad_wd, squares / entries,
    )


def join(kept, sent, odd, by_x):
    even = jnp.stack([kept, sent], 2 if by_x else 1)
    even = even.reshape(odd.shape)
    both = jnp.stack([even, odd], 2)
    return unfold_rows(both.reshape((32,) + odd.shape[2:]))


def solution(mesh):
    by_row = P(("dp", "fsdp"), None, None)
    shard = P("fsdp", None)
    return jax.shard_map(
        local,
        mesh=mesh,
        in_specs=(by_row,) * 4
        + (P(("dp", "fsdp"), None), P("fsdp"), shard, shard, shard, shard, P("fsdp"), shard, shard, shard),
        out_specs=(by_row,) * 3
        + (P("fsdp"), shard, shard, shard, shard, P("fsdp"), shard, shard, shard, P()),
        check_vma=False,
    )
```

time: 1320 us -> 623 us (0.47)
  waiting for transfers between devices: 684 us -> 142 us
  matrix products: 342 us -> 0 us
  Pallas kernels: 0 us -> 278 us
  other arithmetic: 139 us -> 38.9 us
  blocking collectives: 83.2 us -> 0 us
  starting transfers between devices: 0.6 us -> 77.7 us
  local copies, waits for them, and re-layouts: 41.1 us -> 59.5 us
    dot_general x33 -> x0, matrix products: 342 us -> none  [the longest x2 45.9 us: attend_backward(): jnp.einsum('qhd,khd->hqk', gblock, value, preferred_element_type=jnp.floa...]
    all_gather x7 -> x1, waiting for transfers between devices: 330 us -> 0.01 us  [local(): lax.all_gather(jnp.concatenate([reduced, in_parts(sums_z)[None]]), 'dp')]
    reduce_scatter x7 -> x0, waiting for transfers between devices: 314 us -> none  [the longest x1 105 us: local(): lax.psum_scatter(grad_wu.astype(jnp.bfloat16), 'fsdp', scatter_dimension=...]
    pallas_call x0 -> x16, Pallas kernels: none -> 278 us  [the longest x3 50.4 us: attend_bwd(): pl.pallas_call(attend_bwd_body, grid=(pairs,), in_specs=[col] * 4 + [whol...]
    ppermute x0 -> x79, waiting for transfers between devices: none -> 142 us  [the longest x18 89.1 us: fsdp_shift(): lax.ppermute(x, 'fsdp', [(i, (i + step) % size) for i in range(size)])]
    ppermute x0 -> x79, starting transfers between devices: none -> 77.6 us  [the longest x61 55.1 us: dp_swap(): lax.ppermute(x, 'dp', [(i, i ^ bit) for i in range(lax.axis_size('dp'))])]
    convert_element_type x18 -> x21, other arithmetic: 75.9 us -> 12.7 us  [the longest x5 4.46 us: halve(): picked.append(add(*parts).astype(bf16))]
    psum x2 -> x0, blocking collectives: 60.3 us -> none  [the longest x1 46.1 us: local(): lax.psum((jnp.sum(vf * vf), jnp.sum(mixed_wide * mixed_wide)), ('dp', 'fs...]
  transfers between devices with their start and end apart: 15 -> 80, of which waited for: 9 -> 19; matrix products, arithmetic and copies ran while one was open for 35% -> 9% of each run, Pallas kernels for 0% -> 38%
where the time goes in v1:
time: 623 us; the launch traced here: 612 us
  Pallas kernels  278 us (45%)
  waiting for transfers between devices  142 us (23%)
  starting transfers between devices  77.7 us (12%)
  local copies, waits for them, and re-layouts  59.5 us (10%)
  other arithmetic  38.9 us (6%)
  between operations  15.7 us (3%)
    ppermute x18, waiting for transfers between devices, fsdp_shift(): lax.ppermute(x, 'fsdp', [(i, (i + step) % size) for i in range(size)])  89.1 us
    ppermute x61, starting transfers between devices, dp_swap(): lax.ppermute(x, 'dp', [(i, i ^ bit) for i in range(lax.axis_size('dp'))])  55.1 us
    ppermute x61, waiting for transfers between devices, dp_swap(): lax.ppermute(x, 'dp', [(i, i ^ bit) for i in range(lax.axis_size('dp'))])  52.9 us
    pallas_call x3, Pallas kernels, attend_bwd(): pl.pallas_call(attend_bwd_body, grid=(pairs,), in_specs=[col] * 4 + [whol...  50.4 us
    pallas_call x3, Pallas kernels, attend_fwd(): pl.pallas_call(attend_fwd_body, grid=(pairs,), in_specs=[col, col, col, p...  34.7 us
    pallas_call x1, Pallas kernels, ffn_back(): pl.pallas_call(ffn_back_body, grid=(hidden // (2 * L),), in_specs=[SMEM,...  30.4 us
    pallas_call x1, Pallas kernels, ffn_up(): pl.pallas_call(lambda *refs: ffn_up_body(groups, *refs), grid=(1 + tiles,...  30.2 us
    pallas_call x1, Pallas kernels, ffn_down(): pl.pallas_call(lambda *refs: ffn_down_body(group, *refs), grid=(hidden //...  27.1 us
  transfers between devices with their start and end apart: 80, of which 19 were waited for; matrix products, arithmetic and copies ran while one was open for 9% of the time, Pallas kernels for 38%

profile of v1, /device:TPU:9, one launch (start us, length us, event | category | flops | bytes accessed | tf_op | source)
XLA Modules:
  0.0 611.6 jit_solution(5283388061430785203)
XLA Ops:
  22.8 4.3 collective-permute-done.1
  28.0 3.4 collective-permute-done
  41.8 10.7 %collective-permute-done.13 = bf16[30,32,128]{2,1,0:T(8,128)(2,1)S(1)} collective-permute-done((bf16[30,32,128]{2,1,0:T(8,128)(2,1)S(1)}, bf16[30,32,128]{2,1,0:T(8,128)(2,1)S(1)}, u32[]{:S(2)}, u32[]{:S(2)}) %collective-permute-start.13) | collective-permute-done | bytes 245792 | tf_op jit(solution)/shard_map/ppermute | solution.py:67
  52.5 5.3 collective-permute-done.12
  68.7 14.0 %collective-permute-done.6.refs_11_ = bf16[3,12,32,128]{3,2,1,0:T(8,128)(2,1)S(1)} collective-permute-done((bf16[3,12,32,128]{3,2,1,0:T(8,128)(2,1)S(1)}, bf16[3,12,32,128]{3,2,1,0:T(8,128)(2,1)S(1)}, u32[]{:S(2)}, u32[]{:S(2)}) %collective-permute-start.6) | collective-permute-done | bytes 294944 | tf_op jit(solution)/shard_map/ppermute | solution.py:58
  95.5 16.1 %qkv.1 = (bf16[1024,1024]{1,0:T(8,128)(2,1)}, bf16[1024,1024]{1,0:T(8,128)(2,1)}, bf16[1024,1024]{1,0:T(8,128)(2,1)}, bf16[1024,1024]{1,0:T(8,128)(2,1)}, bf16[1...) custom-call(s32[2]{0:T(128)} %pad_add_fusion.refs_0_.pos, ...), custom_call_target="tpu_custom_call" | custom-call | flops 6442450944 | bytes 25165824 | tf_op jit(solution)/shard_map/qkv/pallas_call | solution.py:224
  122.4 12.7 %attend_fwd.3 = (bf16[1024,1024]{1,0:T(8,128)(2,1)}, f32[1024,128]{1,0:T(8,128)}) custom-call(bf16[1024,1024]{1,0:T(8,128)(2,1)} %get-tuple-element.115.q_ref, bf16[1024,1024]{1,0:T(8,128)(2,1)} %get-tuple-element.116.k_ref, bf16[1024,1024]{1,0:T(8,128)(2,1)} %get-tuple-element.117.v_ref, s32[1,1024]{1,0:T(1,128)} %bitcast.290, f32[1024,1]{1,0:T(8,128)} %copy.190.keep_ref), custom_call_target="tpu_custom_call" | custom-call | flops 5368709120 | bytes 16777216 | tf_op jit(solution)/shard_map/attend_fwd/pallas_call | solution.py:289
  142.8 12.7 %attend_fwd.4 = (bf16[1024,1024]{1,0:T(8,128)(2,1)}, f32[1024,128]{1,0:T(8,128)}) custom-call(bf16[1024,1024]{1,0:T(8,128)(2,1)} %get-tuple-element.115.q_ref, bf16[1024,1024]{1,0:T(8,128)(2,1)} %get-tuple-element.116.k_ref, bf16[1024,1024]{1,0:T(8,128)(2,1)} %get-tuple-element.117.v_ref, s32[1,1024]{1,0:T(1,128)} %bitcast.291, ...), custom_call_target="tpu_custom_call", output_to_operand_aliasing={{0}: (5, {})} | custom-call | flops 5368709120 | bytes 16777216 | tf_op jit(solution)/shard_map/attend_fwd/pallas_call | solution.py:289
  158.7 9.3 %attend_fwd.5 = (bf16[1024,1024]{1,0:T(8,128)(2,1)}, f32[1024,128]{1,0:T(8,128)}) custom-call(bf16[1024,1024]{1,0:T(8,128)(2,1)} %get-tuple-element.115.q_ref, bf16[1024,1024]{1,0:T(8,128)(2,1)} %get-tuple-element.116.k_ref, bf16[1024,1024]{1,0:T(8,128)(2,1)} %get-tuple-element.117.v_ref, s32[1,1024]{1,0:T(1,128)} %bitcast.292, ...), custom_call_target="tpu_custom_call", output_to_operand_aliasing={{0}: (5, {})} | custom-call | flops 5368709120 | bytes 16777216 | tf_op jit(solution)/shard_map/attend_fwd/pallas_call | solution.py:289
  183.1 30.2 %ffn_up.1 = (f32[1024,1024]{1,0:T(8,128)}, bf16[1024,1024]{1,0:T(8,128)(2,1)}, bf16[16,2,32,1024]{3,2,1,0:T(8,128)(2,1)}, bf16[1024,2816]{1,0:T(8,128)(2,1)}, bf...) custom-call(s32[2]{0:T(128)} %pad_add_fusion.refs_0_.pos, ...), custom_call_target="tpu_custom_call" | custom-call | flops 11811160064 | bytes 41943040 | tf_op jit(solution)/shard_map/ffn_up/pallas_call | solution.py:476
  217.0 27.1 %ffn_down.1 = (bf16[1024,2816]{1,0:T(8,128)(2,1)}, bf16[1024,2816]{1,0:T(8,128)(2,1)}, bf16[4,4,22,32,128]{4,3,2,1,0:T(8,128)(2,1)}, bf16[4,4,22,32,128]{4,3,2,1...) custom-call(s32[2]{0:T(128)} %pad_add_fusion.refs_0_.pos, ...), custom_call_target="tpu_custom_call" | custom-call | flops 14763950080 | bytes 62914560 | tf_op jit(solution)/shard_map/ffn_down/pallas_call | solution.py:547
  248.4 30.4 %ffn_back.1 = (f32[1024,1024]{1,0:T(8,128)}, bf16[1024,1024]{1,0:T(8,128)(2,1)}, bf16[1024,1024]{1,0:T(8,128)(2,1)}) custom-call(s32[2]{0:T(128)} %pad_add_fusion.refs_0_.pos, f32[1024,1024]{1,0:T(8,128)} %get-tuple-element.138.r1_ref, bf16[1024,1024]{1,0:T(8,128)(2,1)} %bitcast.300, f32[1024,1]{1,0:T(8,128)} %copy.190.keep_ref, ...), custom_call_target="tpu_custom_call" | custom-call | flops 11811160064 | bytes 41943040 | tf_op jit(solution)/shard_map/ffn_back/pallas_call | solution.py:607
  278.8 21.2 %ffn_grads.1 = (bf16[4,2,22,32,128]{4,3,2,1,0:T(8,128)(2,1)}, bf16[4,2,22,32,128]{4,3,2,1,0:T(8,128)(2,1)}, bf16[4,2,22,32,128]{4,3,2,1,0:T(8,128)(2,1)}, bf16[4...) custom-call(s32[2]{0:T(128)} %pad_add_fusion.refs_0_.pos, ...), custom_call_target="tpu_custom_call" | custom-call | flops 8858370048 | bytes 41943040 | tf_op jit(solution)/shard_map/ffn_grads/pallas_call | solution.py:678
  307.7 18.4 %attend_bwd.3 = (bf16[1024,1024]{1,0:T(8,128)(2,1)}, bf16[1024,1024]{1,0:T(8,128)(2,1)}, bf16[1024,1024]{1,0:T(8,128)(2,1)}, f32[1024,1024]{1,0:T(8,128)}) custom-call(bf16[1024,1024]{1,0:T(8,128)(2,1)} %get-tuple-element.115.q_ref, bf16[1024,1024]{1,0:T(8,128)(2,1)} %get-tuple-element.116.k_ref, bf16[1024,1024]{1,0:T(8,128)(2,1)} %get-tuple-element.117.v_ref, ...), custom_call_target="tpu_custom_call" | custom-call | flops 12884901888 | bytes 25165824 | tf_op jit(solution)/shard_map/attend_bwd/pallas_call | solution.py:375
  326.2 18.6 %attend_bwd.4 = (bf16[1024,1024]{1,0:T(8,128)(2,1)}, bf16[1024,1024]{1,0:T(8,128)(2,1)}, bf16[1024,1024]{1,0:T(8,128)(2,1)}, f32[1024,1024]{1,0:T(8,128)}) custom-call(bf16[1024,1024]{1,0:T(8,128)(2,1)} %get-tuple-element.115.q_ref, ...), custom_call_target="tpu_custom_call", output_to_operand_aliasing={{0}: (9, {}), {1}: (10, {}), {2}: (11, {}), {3}: (12, {})} | custom-call | flops 12884901888 | bytes 25165824 | tf_op jit(solution)/shard_map/attend_bwd/pallas_call | solution.py:375
  344.8 13.4 %attend_bwd.5 = (bf16[1024,1024]{1,0:T(8,128)(2,1)}, bf16[1024,1024]{1,0:T(8,128)(2,1)}, bf16[1024,1024]{1,0:T(8,128)(2,1)}, f32[1024,1024]{1,0:T(8,128)}) custom-call(bf16[1024,1024]{1,0:T(8,128)(2,1)} %get-tuple-element.115.q_ref, ...), custom_call_target="tpu_custom_call", output_to_operand_aliasing={{0}: (9, {}), {1}: (10, {}), {2}: (11, {}), {3}: (12, {})} | custom-call | flops 12884901888 | bytes 25165824 | tf_op jit(solution)/shard_map/attend_bwd/pallas_call | solution.py:375
  358.1 17.4 %square_send.1 = bf16[4,4,32,32,128]{4,3,2,1,0:T(8,128)(2,1)} custom-call(s32[2]{0:T(128)} %pad_add_fusion.refs_0_.pos, bf16[1024,1024]{1,0:T(8,128)(2,1)} %get-tuple-element.120.refs_2_.o_ref, bf16[16,2,32,1024]{3,2,1,0:T(8,128)(2,1)} %get-tuple-element.140.ht_ref, bf16[1024,1024]{1,0:T(8,128)(2,1)} %get-tuple-element.158.da_ref, ...), custom_call_target="tpu_custom_call" | custom-call | flops 4294967296 | bytes 25165824 | tf_op jit(solution)/shard_map/square_send/pallas_call | solution.py:794
  385.1 16.7 %input_grad.1 = f32[1024,1024]{1,0:T(8,128)} custom-call(bf16[1024,1024]{1,0:T(8,128)(2,1)} %bitcast.304, f32[1,1024]{1,0:T(1,128)} %get-tuple-element.244.refs_3_.gain_ref, f32[1024,1024]{1,0:T(8,128)} %get-tuple-element.183.dr_ref, bf16[1024,1024]{1,0:T(8,128)(2,1)} %get-tuple-element.179.dq_ref, bf16[1024,1024]{1,0:T(8,128)(2,1)} %get-tuple-element.180.dk_ref, ...), custom_call_target="tpu_custom_call" | custom-call | flops 6442450944 | bytes 25165824 | tf_op jit(solution)/shard_map/input_grad/pallas_call | solution.py:850
  415.1 3.2 collective-permute-start.77
  418.4 5.5 collective-permute-done.76
  424.6 32.6 %collective-permute-done.77 = bf16[67,32,128]{2,1,0:T(8,128)(2,1)S(1)} collective-permute-done((bf16[67,32,128]{2,1,0:T(8,128)(2,1)S(1)}, bf16[67,32,128]{2,1,0:T(8,128)(2,1)S(1)}, u32[]{:S(2)}, u32[]{:S(2)}) %collective-permute-start.77) | collective-permute-done | bytes 548896 | tf_op jit(solution)/shard_map/ppermute | solution.py:67
  457.3 6.9 %collective-permute-done.78 = bf16[67,32,128]{2,1,0:T(8,128)(2,1)S(1)} collective-permute-done((bf16[67,32,128]{2,1,0:T(8,128)(2,1)S(1)}, bf16[67,32,128]{2,1,0:T(8,128)(2,1)S(1)}, u32[]{:S(2)}, u32[]{:S(2)}) %collective-permute-start.78) | collective-permute-done | bytes 548896 | tf_op jit(solution)/shard_map/ppermute | solution.py:67
  466.4 18.4 %square_keep.1 = (bf16[4,2,16,32,128]{4,3,2,1,0:T(8,128)(2,1)}, bf16[4,2,16,32,128]{4,3,2,1,0:T(8,128)(2,1)}, bf16[4,2,16,32,128]{4,3,2,1,0:T(8,128)(2,1)}, bf16[4,2,16,32,128]{4,3,2,1,0:T(8,128)(2,1)}) custom-call(s32[2]{0:T(128)} %pad_add_fusion.refs_0_.pos, bf16[1024,1024]{1,0:T(8,128)(2,1)} %get-tuple-element.120.refs_2_.o_ref, ...), custom_call_target="tpu_custom_call" | custom-call | flops 4294967296 | bytes 25165824 | tf_op jit(solution)/shard_map/square_keep/pallas_call | solution.py:808
  488.5 11.3 %ffn_out.1 = bf16[1024,1024]{1,0:T(8,128)(2,1)} custom-call(f32[1024,1024]{1,0:T(8,128)} %get-tuple-element.138.r1_ref, bf16[1024,2816]{1,0:T(8,128)(2,1)} %get-tuple-element.189.refs_3_.hid_ref, bf16[8,88,32,128]{3,2,1,0:T(8,128)(2,1)} %get-tuple-element.190.wd), custom_call_target="tpu_custom_call" | custom-call | flops 5905580032 | bytes 20971520 | tf_op jit(solution)/shard_map/ffn_out/pallas_call | solution.py:714
  499.8 22.4 %collective-permute-done.52 = bf16[4,2,16,32,128]{4,3,2,0,1:T(8,128)(2,1)S(1)} collective-permute-done((bf16[4,2,16,32,128]{4,3,2,0,1:T(8,128)(2,1)}, bf16[4,2,16,32,128]{4,3,2,0,1:T(8,128)(2,1)S(1)}, u32[]{:S(2)}, u32[]{:S(2)}) %collective-permute-start.52) | collective-permute-done | bytes 1048608 | tf_op jit(solution)/shard_map/ppermute | solution.py:58
  524.1 11.1 %collective-permute-done.55 = bf16[4,16,32,128]{3,2,1,0:T(8,128)(2,1)S(1)} collective-permute-done((bf16[4,16,32,128]{3,2,1,0:T(8,128)(2,1)S(1)}, bf16[4,16,32,128]{3,2,1,0:T(8,128)(2,1)S(1)}, u32[]{:S(2)}, u32[]{:S(2)}) %collective-permute-start.55) | collective-permute-done | bytes 524320 | tf_op jit(solution)/shard_map/ppermute | solution.py:58
  539.1 3.1 collective-permute-done.56
  542.2 15.9 %collective-permute-done.57 = bf16[32,32,128]{2,1,0:T(8,128)(2,1)S(1)} collective-permute-done((bf16[32,32,128]{2,1,0:T(8,128)(2,1)S(1)}, bf16[32,32,128]{2,1,0:T(8,128)(2,1)S(1)}, u32[]{:S(2)}, u32[]{:S(2)}) %collective-permute-start.57) | collective-permute-done | bytes 262176 | tf_op jit(solution)/shard_map/ppermute | solution.py:67
  559.8 3.4 collective-permute-start.63
  565.4 5.7 collective-permute-start.65
  577.0 3.8 place.1
  589.3 3.9 slice_bitcast_fusion
  (410 shorter events, 166.7 us)
Async XLA Ops:
  7.2 576.3 %all-gather.3.cloned.1.call-start = ((), (), s32[]{:S(2)}) async-start(), calls=%async_computation | async-start | bytes 4939776 | tf_op jit(solution)/shard_map/all_gather | solution.py:1090
  32.5 26.7 %collective-permute-start.4 = (bf16[3,24,32,128]{3,2,1,0:T(8,128)(2,1)S(1)}, bf16[3,24,32,128]{3,2,1,0:T(8,128)(2,1)}, u32[]{:S(2)}, u32[]{:S(2)}) collective-permute-start(bf16[3,24,32,128]{3,2,1,0:T(8,128)(2,1)S(1)} %pad_maximum_fusion.8.refs_7_), channel_id=1, source_target_pairs={{0,16},{4,20},{8,24},{12,28},{16,0},{20,4},{24,8},{28,12},{1,17},{... | collective-permute-start | bytes 1769480 | tf_op jit(solution)/shard_map/ppermute | solution.py:58
  33.8 27.7 %collective-permute-start.3 = (bf16[3,24,32,128]{3,2,1,0:T(8,128)(2,1)S(1)}, bf16[3,24,32,128]{3,2,1,0:T(8,128)(2,1)}, u32[]{:S(2)}, u32[]{:S(2)}) collective-permute-start(bf16[3,24,32,128]{3,2,1,0:T(8,128)(2,1)S(1)} %pad_maximum_fusion.8.refs_7_), channel_id=1, source_target_pairs={{0,8},{4,12},{8,0},{12,4},{16,24},{20,28},{24,16},{28,20},{1,9},{5... | collective-permute-start | bytes 1769480 | tf_op jit(solution)/shard_map/ppermute | solution.py:58
  58.7 29.3 %collective-permute-start.16 = (bf16[3,30,32,128]{3,2,1,0:T(8,128)(2,1)}, bf16[3,30,32,128]{3,2,1,0:T(8,128)(2,1)}, u32[]{:S(2)}, u32[]{:S(2)}) collective-permute-start(bf16[3,30,32,128]{3,2,1,0:T(8,128)(2,1)} %pad_maximum_fusion.6.refs_5_), channel_id=1, source_target_pairs={{0,16},{4,20},{8,24},{12,28},{16,0},{20,4},{24,8},{28,12},{1,17},{... | collective-permute-start | bytes 2211848 | tf_op jit(solution)/shard_map/ppermute | solution.py:58
  58.9 29.6 %collective-permute-start.15 = (bf16[3,30,32,128]{3,2,1,0:T(8,128)(2,1)}, bf16[3,30,32,128]{3,2,1,0:T(8,128)(2,1)}, u32[]{:S(2)}, u32[]{:S(2)}) collective-permute-start(bf16[3,30,32,128]{3,2,1,0:T(8,128)(2,1)} %pad_maximum_fusion.6.refs_5_), channel_id=1, source_target_pairs={{0,8},{4,12},{8,0},{12,4},{16,24},{20,28},{24,16},{28,20},{1,9},{5... | collective-permute-start | bytes 2211848 | tf_op jit(solution)/shard_map/ppermute | solution.py:58
  60.2 22.5 %collective-permute-start.6 = (bf16[3,12,32,128]{3,2,1,0:T(8,128)(2,1)S(1)}, bf16[3,12,32,128]{3,2,1,0:T(8,128)(2,1)S(1)}, u32[]{:S(2)}, u32[]{:S(2)}) collective-permute-start(bf16[3,12,32,128]{3,2,1,0:T(8,128)(2,1)S(1)} %slice.219), channel_id=1, source_target_pairs={{0,8},{4,12},{8,0},{12,4},{16,24},{20,28},{24,16},{28,20},{1,9},{5... | collective-permute-start | bytes 884744 | tf_op jit(solution)/shard_map/ppermute | solution.py:58
  62.5 21.9 %collective-permute-start.5 = (bf16[3,12,32,128]{3,2,1,0:T(8,128)(2,1)S(1)}, bf16[3,12,32,128]{3,2,1,0:T(8,128)(2,1)S(1)}, u32[]{:S(2)}, u32[]{:S(2)}) collective-permute-start(bf16[3,12,32,128]{3,2,1,0:T(8,128)(2,1)S(1)} %slice.218), channel_id=1, source_target_pairs={{0,16},{4,20},{8,24},{12,28},{16,0},{20,4},{24,8},{28,12},{1,17},{... | collective-permute-start | bytes 884744 | tf_op jit(solution)/shard_map/ppermute | solution.py:58
  67.1 24.2 %collective-permute-start.7 = (bf16[3,24,32,128]{3,2,1,0:T(8,128)(2,1)S(1)}, bf16[3,24,32,128]{3,2,1,0:T(8,128)(2,1)}, u32[]{:S(2)}, u32[]{:S(2)}) collective-permute-start(bf16[3,24,32,128]{3,2,1,0:T(8,128)(2,1)S(1)} %pad_maximum_fusion.8.refs_7_), channel_id=1, source_target_pairs={{0,4},{4,0},{8,12},{12,8},{16,20},{20,16},{24,28},{28,24},{1,5},{5... | collective-permute-start | bytes 1769480 | tf_op jit(solution)/shard_map/ppermute | solution.py:58
  91.3 23.9 %collective-permute-start.26 = (bf16[22,32,128]{2,1,0:T(8,128)(2,1)S(1)}, bf16[22,32,128]{2,1,0:T(8,128)(2,1)S(1)}, u32[]{:S(2)}, u32[]{:S(2)}) collective-permute-start(bf16[22,32,128]{2,1,0:T(8,128)(2,1)S(1)} %bitcast.274), channel_id=1, source_target_pairs={{0,3},{1,0},{2,1},{3,2},{4,7},{5,4},{6,5},{7,6},{8,11},{9,8},{10,9... | collective-permute-start | bytes 540680 | tf_op jit(solution)/shard_map/ppermute | solution.py:67
  92.2 23.0 %collective-permute-start.25 = (bf16[22,32,128]{2,1,0:T(8,128)(2,1)S(1)}, bf16[22,32,128]{2,1,0:T(8,128)(2,1)S(1)}, u32[]{:S(2)}, u32[]{:S(2)}) collective-permute-start(bf16[22,32,128]{2,1,0:T(8,128)(2,1)S(1)} %bitcast.275), channel_id=1, source_target_pairs={{0,2},{1,3},{2,0},{3,1},{4,6},{5,7},{6,4},{7,5},{8,10},{9,11},{10,... | collective-permute-start | bytes 540680 | tf_op jit(solution)/shard_map/ppermute | solution.py:67
  157.0 22.6 %collective-permute-start.31 = (bf16[3,22,32,128]{3,2,1,0:T(8,128)(2,1)}, bf16[3,22,32,128]{3,2,1,0:T(8,128)(2,1)}, u32[]{:S(2)}, u32[]{:S(2)}) collective-permute-start(bf16[3,22,32,128]{3,2,1,0:T(8,128)(2,1)} %pad_maximum_fusion.10.refs_16_), channel_id=1, source_target_pairs={{0,4},{4,0},{8,12},{12,8},{16,20},{20,16},{24,28},{28,24},{1,5},{5... | collective-permute-start | bytes 1622024 | tf_op jit(solution)/shard_map/ppermute | solution.py:58
  158.2 21.9 %collective-permute-start.32 = (bf16[3,22,32,128]{3,2,1,0:T(8,128)(2,1)}, bf16[3,22,32,128]{3,2,1,0:T(8,128)(2,1)}, u32[]{:S(2)}, u32[]{:S(2)}) collective-permute-start(bf16[3,22,32,128]{3,2,1,0:T(8,128)(2,1)} %collective-permute-done.27.refs_17_), channel_id=1, source_target_pairs={{0,4},{4,0},{8,12},{12,8},{16,20},{20,16},{24,28},{28,24},{1,5},{5... | collective-permute-start | bytes 1622024 | tf_op jit(solution)/shard_map/ppermute | solution.py:58
  158.3 22.6 %collective-permute-start.33 = (bf16[3,22,32,128]{3,2,1,0:T(8,128)(2,1)}, bf16[3,22,32,128]{3,2,1,0:T(8,128)(2,1)}, u32[]{:S(2)}, u32[]{:S(2)}) collective-permute-start(bf16[3,22,32,128]{3,2,1,0:T(8,128)(2,1)} %collective-permute-done.28.refs_18_), channel_id=1, source_target_pairs={{0,4},{4,0},{8,12},{12,8},{16,20},{20,16},{24,28},{28,24},{1,5},{5... | collective-permute-start | bytes 1622024 | tf_op jit(solution)/shard_map/ppermute | solution.py:58
  180.1 35.6 %collective-permute-start.43 = (bf16[3,22,32,128]{3,2,1,0:T(8,128)(2,1)S(1)}, bf16[3,22,32,128]{3,2,1,0:T(8,128)(2,1)S(1)}, u32[]{:S(2)}, u32[]{:S(2)}) collective-permute-start(bf16[3,22,32,128]{3,2,1,0:T(8,128)(2,1)S(1)} %copy-done.30), channel_id=1, source_target_pairs={{0,4},{4,0},{8,12},{12,8},{16,20},{20,16},{24,28},{28,24},{1,5},{5... | collective-permute-start | bytes 1622024 | tf_op jit(solution)/shard_map/ppermute | solution.py:58
  180.1 33.2 %collective-permute-start.41 = (bf16[3,11,32,128]{3,2,1,0:T(8,128)(2,1)S(1)}, bf16[3,11,32,128]{3,2,1,0:T(8,128)(2,1)S(1)}, u32[]{:S(2)}, u32[]{:S(2)}) collective-permute-start(bf16[3,11,32,128]{3,2,1,0:T(8,128)(2,1)S(1)} %slice.225), channel_id=1, source_target_pairs={{0,16},{4,20},{8,24},{12,28},{16,0},{20,4},{24,8},{28,12},{1,17},{... | collective-permute-start | bytes 811016 | tf_op jit(solution)/shard_map/ppermute | solution.py:58
  180.9 32.4 %collective-permute-start.42 = (bf16[3,11,32,128]{3,2,1,0:T(8,128)(2,1)S(1)}, bf16[3,11,32,128]{3,2,1,0:T(8,128)(2,1)S(1)}, u32[]{:S(2)}, u32[]{:S(2)}) collective-permute-start(bf16[3,11,32,128]{3,2,1,0:T(8,128)(2,1)S(1)} %slice.226), channel_id=1, source_target_pairs={{0,8},{4,12},{8,0},{12,4},{16,24},{20,28},{24,16},{28,20},{1,9},{5... | collective-permute-start | bytes 811016 | tf_op jit(solution)/shard_map/ppermute | solution.py:58
  182.0 33.8 %collective-permute-start.44 = (bf16[3,22,32,128]{3,2,1,0:T(8,128)(2,1)S(1)}, bf16[3,22,32,128]{3,2,1,0:T(8,128)(2,1)S(1)}, u32[]{:S(2)}, u32[]{:S(2)}) collective-permute-start(bf16[3,22,32,128]{3,2,1,0:T(8,128)(2,1)S(1)} %copy-done.40), channel_id=1, source_target_pairs={{0,4},{4,0},{8,12},{12,8},{16,20},{20,16},{24,28},{28,24},{1,5},{5... | collective-permute-start | bytes 1622024 | tf_op jit(solution)/shard_map/ppermute | solution.py:58
  183.0 32.7 %collective-permute-start.45 = (bf16[3,22,32,128]{3,2,1,0:T(8,128)(2,1)S(1)}, bf16[3,22,32,128]{3,2,1,0:T(8,128)(2,1)S(1)}, u32[]{:S(2)}, u32[]{:S(2)}) collective-permute-start(bf16[3,22,32,128]{3,2,1,0:T(8,128)(2,1)S(1)} %copy-done.38), channel_id=1, source_target_pairs={{0,4},{4,0},{8,12},{12,8},{16,20},{20,16},{24,28},{28,24},{1,5},{5... | collective-permute-start | bytes 1622024 | tf_op jit(solution)/shard_map/ppermute | solution.py:58
  244.2 34.5 %collective-permute-start.48 = (bf16[4,4,22,32,128]{4,3,2,1,0:T(8,128)(2,1)}, bf16[4,4,22,32,128]{4,3,2,1,0:T(8,128)(2,1)}, u32[]{:S(2)}, u32[]{:S(2)}) collective-permute-start(bf16[4,4,22,32,128]{4,3,2,1,0:T(8,128)(2,1)} %get-tuple-element.162), channel_id=1, source_target_pairs={{0,4},{4,0},{8,12},{12,8},{16,20},{20,16},{24,28},{28,24},{1,5},{5... | collective-permute-start | bytes 8650760 | tf_op jit(solution)/shard_map/ppermute | solution.py:58
  244.7 34.1 %collective-permute-start.49 = (bf16[4,4,22,32,128]{4,3,2,1,0:T(8,128)(2,1)}, bf16[4,4,22,32,128]{4,3,2,1,0:T(8,128)(2,1)}, u32[]{:S(2)}, u32[]{:S(2)}) collective-permute-start(bf16[4,4,22,32,128]{4,3,2,1,0:T(8,128)(2,1)} %get-tuple-element.163), channel_id=1, source_target_pairs={{0,4},{4,0},{8,12},{12,8},{16,20},{20,16},{24,28},{28,24},{1,5},{5... | collective-permute-start | bytes 8650760 | tf_op jit(solution)/shard_map/ppermute | solution.py:58
  244.8 34.0 %collective-permute-start.50 = (bf16[88,4,32,128]{3,2,1,0:T(8,128)(2,1)}, bf16[88,4,32,128]{3,2,1,0:T(8,128)(2,1)}, u32[]{:S(2)}, u32[]{:S(2)}) collective-permute-start(bf16[88,4,32,128]{3,2,1,0:T(8,128)(2,1)} %get-tuple-element.164), channel_id=1, source_target_pairs={{0,4},{4,0},{8,12},{12,8},{16,20},{20,16},{24,28},{28,24},{1,5},{5... | collective-permute-start | bytes 8650760 | tf_op jit(solution)/shard_map/ppermute | solution.py:58
  303.4 72.1 %collective-permute-start.71 = (bf16[48,2,32,128]{3,2,0,1:T(8,128)(2,1)}, bf16[48,2,32,128]{3,2,0,1:T(8,128)(2,1)}, u32[]{:S(2)}, u32[]{:S(2)}) collective-permute-start(bf16[48,2,32,128]{3,2,0,1:T(8,128)(2,1)} %copy.212), channel_id=1, source_target_pairs={{0,16},{4,20},{8,24},{12,28},{16,0},{20,4},{24,8},{28,12},{1,17},{... | collective-permute-start | bytes 2359304 | tf_op jit(solution)/shard_map/ppermute | solution.py:58
  304.3 71.2 %collective-permute-start.69 = (bf16[48,2,32,128]{3,2,0,1:T(8,128)(2,1)}, bf16[48,2,32,128]{3,2,0,1:T(8,128)(2,1)}, u32[]{:S(2)}, u32[]{:S(2)}) collective-permute-start(bf16[48,2,32,128]{3,2,0,1:T(8,128)(2,1)} %copy.210), channel_id=1, source_target_pairs={{0,8},{4,12},{8,0},{12,4},{16,24},{20,28},{24,16},{28,20},{1,9},{5... | collective-permute-start | bytes 2359304 | tf_op jit(solution)/shard_map/ppermute | solution.py:58
  306.0 69.5 %collective-permute-start.68 = (bf16[4,2,22,32,128]{4,3,2,0,1:T(8,128)(2,1)S(1)}, bf16[4,2,22,32,128]{4,3,2,0,1:T(8,128)(2,1)S(1)}, u32[]{:S(2)}, u32[]{:S(2)}) collective-permute-start(bf16[4,2,22,32,128]{4,3,2,0,1:T(8,128)(2,1)S(1)} %copy.209), channel_id=1, source_target_pairs={{0,8},{4,12},{8,0},{12,4},{16,24},{20,28},{24,16},{28,20},{1,9},{5... | collective-permute-start | bytes 4325384 | tf_op jit(solution)/shard_map/ppermute | solution.py:58
  307.1 68.4 %collective-permute-start.70 = (bf16[4,2,22,32,128]{4,3,2,0,1:T(8,128)(2,1)}, bf16[4,2,22,32,128]{4,3,2,0,1:T(8,128)(2,1)S(1)}, u32[]{:S(2)}, u32[]{:S(2)}) collective-permute-start(bf16[4,2,22,32,128]{4,3,2,0,1:T(8,128)(2,1)} %copy.211), channel_id=1, source_target_pairs={{0,16},{4,20},{8,24},{12,28},{16,0},{20,4},{24,8},{28,12},{1,17},{... | collective-permute-start | bytes 4325384 | tf_op jit(solution)/shard_map/ppermute | solution.py:58
  377.7 25.4 %collective-permute-start.75 = (bf16[48,32,128]{2,1,0:T(8,128)(2,1)}, bf16[48,32,128]{2,1,0:T(8,128)(2,1)}, u32[]{:S(2)}, u32[]{:S(2)}) collective-permute-start(bf16[48,32,128]{2,1,0:T(8,128)(2,1)} %fusion.23), channel_id=1, source_target_pairs={{0,8},{4,12},{8,0},{12,4},{16,24},{20,28},{24,16},{28,20},{1,9},{5... | collective-permute-start | bytes 1179656 | tf_op jit(solution)/shard_map/ppermute | solution.py:58
  380.7 22.4 %collective-permute-start.73 = (bf16[48,32,128]{2,1,0:T(8,128)(2,1)}, bf16[48,32,128]{2,1,0:T(8,128)(2,1)}, u32[]{:S(2)}, u32[]{:S(2)}) collective-permute-start(bf16[48,32,128]{2,1,0:T(8,128)(2,1)} %get-tuple-element.236), channel_id=1, source_target_pairs={{0,16},{4,20},{8,24},{12,28},{16,0},{20,4},{24,8},{28,12},{1,17},{... | collective-permute-start | bytes 1179656 | tf_op jit(solution)/shard_map/ppermute | solution.py:58
  412.4 54.0 %collective-permute-start.51 = (bf16[4,4,32,32,128]{4,3,2,1,0:T(8,128)(2,1)}, bf16[4,4,32,32,128]{4,3,2,1,0:T(8,128)(2,1)}, u32[]{:S(2)}, u32[]{:S(2)}) collective-permute-start(bf16[4,4,32,32,128]{4,3,2,1,0:T(8,128)(2,1)} %square_send.1), channel_id=1, source_target_pairs={{0,4},{4,0},{8,12},{12,8},{16,20},{20,16},{24,28},{28,24},{1,5},{5... | collective-permute-start | bytes 12582920 | tf_op jit(solution)/shard_map/ppermute | solution.py:58
  415.1 42.1 %collective-permute-start.77 = (bf16[67,32,128]{2,1,0:T(8,128)(2,1)S(1)}, bf16[67,32,128]{2,1,0:T(8,128)(2,1)S(1)}, u32[]{:S(2)}, u32[]{:S(2)}) collective-permute-start(bf16[67,32,128]{2,1,0:T(8,128)(2,1)S(1)} %get-tuple-element.241), channel_id=1, source_target_pairs={{0,2},{1,3},{2,0},{3,1},{4,6},{5,7},{6,4},{7,5},{8,10},{9,11},{10,... | collective-permute-start | bytes 1646600 | tf_op jit(solution)/shard_map/ppermute | solution.py:67
  418.3 45.8 %collective-permute-start.78 = (bf16[67,32,128]{2,1,0:T(8,128)(2,1)S(1)}, bf16[67,32,128]{2,1,0:T(8,128)(2,1)S(1)}, u32[]{:S(2)}, u32[]{:S(2)}) collective-permute-start(bf16[67,32,128]{2,1,0:T(8,128)(2,1)S(1)} %get-tuple-element.242), channel_id=1, source_target_pairs={{0,3},{1,0},{2,1},{3,2},{4,7},{5,4},{6,5},{7,6},{8,11},{9,8},{10,9... | collective-permute-start | bytes 1646600 | tf_op jit(solution)/shard_map/ppermute | solution.py:67
  487.5 34.7 %collective-permute-start.52 = (bf16[4,2,16,32,128]{4,3,2,0,1:T(8,128)(2,1)}, bf16[4,2,16,32,128]{4,3,2,0,1:T(8,128)(2,1)S(1)}, u32[]{:S(2)}, u32[]{:S(2)}) collective-permute-start(bf16[4,2,16,32,128]{4,3,2,0,1:T(8,128)(2,1)} %copy.203), channel_id=1, source_target_pairs={{0,8},{4,12},{8,0},{12,4},{16,24},{20,28},{24,16},{28,20},{1,9},{5... | collective-permute-start | bytes 3145736 | tf_op jit(solution)/shard_map/ppermute | solution.py:58
  487.8 34.4 %collective-permute-start.53 = (bf16[4,2,16,32,128]{4,3,2,0,1:T(8,128)(2,1)S(1)}, bf16[4,2,16,32,128]{4,3,2,0,1:T(8,128)(2,1)S(1)}, u32[]{:S(2)}, u32[]{:S(2)}) collective-permute-start(bf16[4,2,16,32,128]{4,3,2,0,1:T(8,128)(2,1)S(1)} %copy.204), channel_id=1, source_target_pairs={{0,16},{4,20},{8,24},{12,28},{16,0},{20,4},{24,8},{28,12},{1,17},{... | collective-permute-start | bytes 3145736 | tf_op jit(solution)/shard_map/ppermute | solution.py:58
  (110 other events, 1120.3 us)
Sparse Core Ops, SparseCore 0:
  466.5 44.6 all-gather.2

commit v2 on v1

v2 whole, which is shorter than its diff:
```python
import jax
import jax.numpy as jnp
from jax import lax
from jax.experimental import pallas as pl
from jax.experimental.pallas import tpu as pltpu
from jax.sharding import PartitionSpec as P

HEADS = 16
HEAD_DIM = 64
EPS = 1e-06
NEG = -1e30
COST = 4e9
QB = 256
G = 32
L = 128
bf16 = jnp.bfloat16
f32 = jnp.float32
ANY = pl.BlockSpec(memory_space=pl.ANY)
SMEM = pl.BlockSpec(memory_space=pltpu.SMEM)


def params(mib=58):
    return pltpu.CompilerParams(vmem_limit_bytes=mib * 2**20)


def cost(us):
    return pl.CostEstimate(flops=int(us * COST), bytes_accessed=0, transcendentals=0)


def shape(dims, dtype=bf16):
    return jax.ShapeDtypeStruct(dims, dtype)


def nt(a, b):
    return lax.dot_general(a, b, (((1,), (1,)), ((), ())), preferred_element_type=f32)


def nn(a, b):
    return lax.dot_general(a, b, (((1,), (0,)), ((), ())), preferred_element_type=f32)


def tn(a, b):
    return lax.dot_general(a, b, (((0,), (0,)), ((), ())), preferred_element_type=f32)


def fast_mesh(dp, fsdp, shard_rows):
    return dp == 8 and fsdp == 4 and shard_rows == 8 * G


def row_pieces(w, count):
    return w.reshape(count, G, w.shape[1] // L, L).transpose(0, 2, 1, 3)


def column_pieces(w, count):
    return w.reshape(w.shape[0] // G, G, count, L).transpose(2, 0, 1, 3)


def dp_swap(x, bit):
    return lax.ppermute(x, "dp", [(i, i ^ bit) for i in range(lax.axis_size("dp"))])


def after(x, *first):
    return lax.optimization_barrier((x, first))[0]


def fsdp_shift(x, step):
    size = lax.axis_size("fsdp")
    return lax.ppermute(x, "fsdp", [(i, (i + step) % size) for i in range(size)])


class Gather:
    def __init__(self, sent, extra=False):
        self.count = sent.shape[0] - extra
        self.far = [fsdp_shift(sent, s) for s in (1, 2, 3)]
        self.extras = [x[self.count] for x in [sent] + self.far] if extra else None

    def near(self, *gate):
        self.start = jnp.stack([x[: self.count] for x in after(self.far, *gate)])
        self.x, self.y = dp_swap(self.start, 2), dp_swap(self.start, 4)

    def corner(self, *gate):
        cut = self.count // 2
        self.c1 = dp_swap(after(self.x[:, :cut], *gate), 4)
        self.c2 = dp_swap(after(self.y[:, cut:], *gate), 2)

    def core(self, *gate):
        self.other = [dp_swap(after(a, *gate), 1) for a in (self.start, self.x, self.y)]

    def core_corner(self, *gate):
        self.other += [dp_swap(after(a, *gate), 1) for a in (self.c1, self.c2)]

    def arrays(self):
        return [self.start, self.x, self.y, self.c1, self.c2] + self.other


def piece_sources(count):
    cut = count // 2
    found = []
    for core in range(2):
        for i, (mask, low, size) in enumerate(
            ((0, 0, count), (2, 0, count), (4, 0, count), (6, 0, cut), (6, cut, count - cut))
        ):
            found.append((5 * core + i, mask | core, low, size))
    return found


class Group:
    def __init__(self, tensors, owned, arrays, whole):
        self.tensors, self.whole, self.owned = tensors, whole, len(owned)
        self.arrays = list(owned) + list(arrays)

    def specs(self):
        return [ANY] * len(self.arrays)

    def fetch(self, index, refs, pos, scratch, sem):
        if self.whole:
            pltpu.make_async_copy(refs[index], scratch, sem).start()
            return
        z, d = pos[0], pos[1]
        at = sum(t[0] for t in self.tensors[:index])
        blocks, by_rows = self.tensors[index]

        def target(shard, piece, low, size):
            if by_rows:
                return scratch.at[pl.ds(low, size), shard * 8 + piece]
            return scratch.at[piece, pl.ds(shard * blocks + low, size)]

        own = refs[index]
        rows = own.shape[0]
        flat = scratch.reshape(scratch.shape[0], scratch.shape[1] * G, L)
        for c in range(scratch.shape[0]):
            pltpu.make_async_copy(
                own.at[:, pl.ds(c * L, L)], flat.at[c, pl.ds(pl.multiple_of(z * rows, G), rows)], sem
            ).start()
        for array, mask, low, size in piece_sources(sum(t[0] for t in self.tensors)):
            begin, end = max(at, low), min(at + blocks, low + size)
            if end <= begin:
                continue
            for s in range(3):
                pltpu.make_async_copy(
                    refs[self.owned + array].at[s, pl.ds(begin - low, end - begin)],
                    target(lax.rem(z + 3 - s, 4), d ^ mask, begin - at, end - begin),
                    sem,
                ).start()


def cut_body(tensors, gains, pos, *refs):
    count = len(tensors)
    weights, refs = refs[:count], refs[count:]
    if gains:
        gain_ref, refs = refs[0], refs[1:]
    out, stages, sem = refs[0], refs[1:-1], refs[-1]
    d = pos[1]
    copies = []
    for i, (blocks, by_rows) in enumerate(tensors):
        rows = pl.ds(pl.multiple_of(d * G, G), G)
        cols = pl.ds(pl.multiple_of(d * L, L), L)
        part = weights[i].at[rows] if by_rows else weights[i].at[:, cols]
        copies.append(pltpu.make_async_copy(part, stages[i], sem.at[i]))
    for c in copies:
        c.start()
    at = 0
    for i, (blocks, by_rows) in enumerate(tensors):
        copies[i].wait()
        if by_rows:
            for c in range(blocks):
                out[at + c] = stages[i][:, c * L : (c + 1) * L]
        else:
            out[at : at + blocks] = stages[i][...].reshape(blocks, G, L)
        at += blocks
    if gains:
        out[at] = gain_ref[...]


def cut(pos, weights, tensors, gains=None):
    vmem = pl.BlockSpec(memory_space=pltpu.VMEM)
    total = sum(t[0] for t in tensors) + (gains is not None)
    stages = [
        pltpu.VMEM((G, w.shape[1]) if by_rows else (w.shape[0], L), bf16) for w, (_, by_rows) in zip(weights, tensors)
    ]
    return pl.pallas_call(
        lambda *refs: cut_body(tensors, gains is not None, *refs),
        in_specs=[SMEM] + [ANY] * len(weights) + ([] if gains is None else [vmem]),
        out_specs=vmem,
        out_shape=shape((total, G, L)),
        scratch_shapes=stages + [pltpu.SemaphoreType.DMA((len(weights),))],
        compiler_params=params(),
        name="cut",
    )(pos, *weights, *([] if gains is None else [gains]))


def wait_all(scratch, sem):
    pltpu.make_async_copy(scratch, scratch, sem).wait()


def two(w, i):
    rows = w.shape[1] * w.shape[2]
    return jnp.concatenate([w[2 * i].reshape(rows, L), w[2 * i + 1].reshape(rows, L)], 1)


def swap_halves(t):
    lane = lax.broadcasted_iota(jnp.int32, t.shape, 1) % 64
    return jnp.where(lane < 32, pltpu.roll(t, 96, 1), pltpu.roll(t, 32, 1))


def chunked(blocks, size):
    return [(low, min(size, blocks - low)) for low in range(0, blocks, size)]


def beside(w, low, size):
    rows = w.shape[1] * G
    return jnp.concatenate([w[low + c].reshape(rows, L) for c in range(size)], 1)


def like(a):
    return pltpu.VMEM(a.shape, a.dtype)


def qkv_body(group, pos, gain_ref, cos_ref, sin_ref, x_ref, v1_hbm, *rest):
    count = len(group.arrays)
    w_refs = rest[:count]
    (q_out, k_out, v_out, ht_out, sums_ref, wq_out, wk_out, wv_out,
     v1, wq, wk, wv, h, ht, q, k, v, sem) = rest[count:]
    length, width = x_ref.shape
    blocks = width // L
    for i, w in enumerate((wq, wk, wv)):
        group.fetch(i, w_refs, pos, w, sem.at[i])
    get_v1 = pltpu.make_async_copy(v1_hbm, v1, sem.at[3])
    get_v1.start()
    for i in range(length // QB):
        rows = slice(i * QB, (i + 1) * QB)
        x = x_ref[rows, :].astype(f32)
        n = x * lax.rsqrt(jnp.mean(x * x, -1, keepdims=True) + EPS) * gain_ref[...]
        h[rows, :] = n.astype(bf16)
        ht[:, :, :, rows] = n.T.astype(bf16).reshape(ht.shape[:3] + (QB,))
    out = [pltpu.make_async_copy(ht, ht_out, sem.at[4])]
    out[0].start()
    cos, sin = cos_ref[...], sin_ref[...]
    at = 5

    def send(a, b):
        out.append(pltpu.make_async_copy(a, b, sem.at[at + len(out) - 1]))
        out[-1].start()

    sums_ref[...] = jnp.zeros_like(sums_ref)
    for i, (w, w_out, t, t_out) in enumerate(((wq, wq_out, q, q_out), (wk, wk_out, k, k_out), (wv, wv_out, v, v_out))):
        wait_all(w, sem.at[i])
        send(w, w_out)
        if i == 2:
            get_v1.wait()
        for low, size in chunked(blocks, 2):
            cols = slice(low * L, (low + size) * L)
            got = nn(h[...], beside(w, low, size))
            if i == 2:
                first = v1[:, cols].astype(f32)
                mixed = (0.5 * got + 0.5 * first).astype(bf16)
                v[:, cols] = mixed
                mixed = mixed.astype(f32)
                sums_ref[0] += jnp.sum((first * first).reshape(length // 8, 8, size * L), 0)
                sums_ref[1] += jnp.sum((mixed * mixed).reshape(length // 8, 8, size * L), 0)
                continue
            for c in range(size):
                part = got[:, c * L : (c + 1) * L]
                part = (part * cos + swap_halves(part) * sin).astype(bf16)
                if i == 0:
                    part = (part.astype(f32) * 0.125).astype(bf16)
                t[:, (low + c) * L : (low + c + 1) * L] = part
        send(t, t_out)
    for c in out:
        c.wait()


def qkv(pos, x, v1, gain, cos_w, sin_w, group):
    length, width = x.shape
    blocks = width // L
    vmem = pl.BlockSpec(memory_space=pltpu.VMEM)
    weight = shape((blocks, width // G, G, L))
    ht = shape((width // G // 2, 2, G, length))
    return pl.pallas_call(
        lambda *refs: qkv_body(group, *refs),
        in_specs=[SMEM, vmem, vmem, vmem, vmem, ANY] + group.specs(),
        out_specs=[ANY] * 4 + [vmem] + [ANY] * 3,
        out_shape=[shape((length, width))] * 3 + [ht, shape((2, 8, 2 * L), f32)] + [weight] * 3,
        scratch_shapes=[like(a) for a in (v1, weight, weight, weight, x, ht, x, x, x)]
        + [pltpu.SemaphoreType.DMA((12,))],
        compiler_params=params(),
        cost_estimate=cost(15),
        name="qkv",
    )(pos, gain, cos_w, sin_w, x, v1, *group.arrays)


def half_mask(rows, which):
    lane = lax.broadcasted_iota(jnp.int32, (rows, 128), 1)
    return (lane < 64) if which == 0 else (lane >= 64)


def pick(x, which):
    return jnp.where(half_mask(x.shape[0], which), x, jnp.zeros_like(x))


def attend_fwd_body(q_ref, k_ref, v_ref, end_ref, keep_ref, *rest):
    o_ref, lse_ref, bias = rest[-3:]
    pair = pl.program_id(0)
    length = q_ref.shape[0]
    blocks = length // QB

    @pl.when(pair == 0)
    def _():
        for i in range(blocks):
            size = (i + 1) * QB
            q_at = lax.broadcasted_iota(jnp.int32, (QB, size), 0) + i * QB
            k_at = lax.broadcasted_iota(jnp.int32, (QB, size), 1)
            ok = (q_at >= k_at) & (q_at < end_ref[:, :size])
            bias[i * QB : (i + 1) * QB, :size] = jnp.where(ok, 0.0, NEG)

    lane = lax.broadcasted_iota(jnp.int32, (QB, 128), 1)
    for i in range(blocks):
        rows = slice(i * QB, (i + 1) * QB)
        size = (i + 1) * QB
        outs = []
        old = lse_ref[rows, :]
        for h in range(2):
            s = nt(pick(q_ref[rows, :], h), k_ref[:size, :]) + bias[rows, :size]
            top = jnp.max(s, -1, keepdims=True)
            expo = jnp.exp(s - top)
            total = jnp.sum(expo, -1, keepdims=True)
            outs.append(nn(expo.astype(bf16), v_ref[:size, :]) / total)
            old = jnp.where(lane == 2 * pair + h, top + jnp.log(total), old)
        lse_ref[rows, :] = old
        o = jnp.where(lane < 64, outs[0], outs[1]) * keep_ref[rows, :]
        o_ref[rows, :] = o.astype(bf16)


def attend_fwd(q, k, v, end_row, keep_col, first, pairs, before=None):
    length, width = q.shape
    col = pl.BlockSpec((length, 128), lambda p: (0, p + first))
    return pl.pallas_call(
        attend_fwd_body,
        grid=(pairs,),
        in_specs=[
            col,
            col,
            col,
            pl.BlockSpec((1, length), lambda p: (0, 0)),
            pl.BlockSpec((length, 1), lambda p: (0, 0)),
        ]
        + ([] if before is None else [ANY]),
        out_specs=[col, pl.BlockSpec((length, 128), lambda p: (0, 0))],
        out_shape=[
            jax.ShapeDtypeStruct((length, width), bf16),
            jax.ShapeDtypeStruct((length, 128), f32),
        ],
        scratch_shapes=[pltpu.VMEM((length, length), f32)],
        compiler_params=params(),
        cost_estimate=cost(4.2 * pairs),
        input_output_aliases={} if before is None else {5: 0},
        name="attend_fwd",
    )(q, k, v, end_row, keep_col, *([] if before is None else [before]))


def attend_bwd_body(
    q_ref, k_ref, v_ref, do_ref, lse_ref, first_ref, cos_ref, sin_ref, fg_ref, *rest,
):
    dq_ref, dk_ref, dv_ref, fo_ref, bias, dk_acc, dv_acc = rest[-7:]
    pair = pl.program_id(0)
    length = q_ref.shape[0]
    blocks = length // QB

    @pl.when(pair == 0)
    def _():
        for i in range(blocks):
            size = (i + 1) * QB
            k_at = lax.broadcasted_iota(jnp.int32, (size, QB), 0)
            q_at = lax.broadcasted_iota(jnp.int32, (size, QB), 1) + i * QB
            ok = (q_at >= k_at) & (k_at >= first_ref[:, i * QB : (i + 1) * QB])
            bias[:size, i * QB : (i + 1) * QB] = jnp.where(ok, 0.0, NEG)

    k_t = k_ref[...].astype(f32).T.astype(bf16)
    for i in reversed(range(blocks)):
        rows = slice(i * QB, (i + 1) * QB)
        size = (i + 1) * QB
        part_k = None
        part_v = None
        part_q = []
        for h in range(2):
            qh = pick(q_ref[rows, :], h)
            dh = pick(do_ref[rows, :], h)
            lse = lse_ref[pl.ds(2 * pair + h, 1), rows]
            p = jnp.exp(nt(k_ref[:size, :], qh) + bias[:size, rows] - lse)
            dp = nt(v_ref[:size, :], dh)
            delta = jnp.sum(p * dp, 0, keepdims=True)
            ds = (p * (dp - delta)).astype(bf16)
            av = nn(p.astype(bf16), dh)
            ak = nn(ds, qh)
            part_v = av if part_v is None else part_v + av
            part_k = ak if part_k is None else part_k + ak
            part_q.append(nn(k_t[h * 64 : (h + 1) * 64, :size], ds))
        if i == blocks - 1:
            dk_acc[...] = part_k
            dv_acc[...] = part_v
        else:
            dk_acc[:size, :] += part_k
            dv_acc[:size, :] += part_v
        dq = jnp.concatenate(part_q, 0).T * 0.125
        dq = dq * cos_ref[rows, :] + swap_halves(dq) * sin_ref[rows, :]
        dq_ref[rows, :] = dq.astype(bf16)
    dk = dk_acc[...]
    dk_ref[...] = (dk * cos_ref[...] + swap_halves(dk) * sin_ref[...]).astype(bf16)
    dv = dv_acc[...].astype(bf16).astype(f32) * 0.5
    dv_ref[...] = dv.astype(bf16)
    fo_ref[...] = fg_ref[...] + dv


def attend_bwd(q, k, v, do, lse_t, first_row, cos_w, sin_back, fgrad, first, pairs, before=None):
    length, width = q.shape
    col = pl.BlockSpec((length, 128), lambda p: (0, p + first))
    before = [] if before is None else list(before)

    def whole(a):
        return pl.BlockSpec(a.shape, lambda p: (0, 0))

    wide = jax.ShapeDtypeStruct((length, width), bf16)
    return pl.pallas_call(
        attend_bwd_body,
        grid=(pairs,),
        in_specs=[col] * 4 + [whole(lse_t), whole(first_row), whole(cos_w), whole(sin_back), col]
        + [ANY] * len(before),
        out_specs=[col] * 4,
        out_shape=[wide, wide, wide, jax.ShapeDtypeStruct((length, width), f32)],
        scratch_shapes=[
            pltpu.VMEM((length, length), f32),
            pltpu.VMEM((length, 128), f32),
            pltpu.VMEM((length, 128), f32),
        ],
        compiler_params=params(),
        cost_estimate=cost(5.5 * pairs),
        input_output_aliases={9 + i: i for i in range(len(before))},
        name="attend_bwd",
    )(q, k, v, do, lse_t, first_row, cos_w, sin_back, fgrad, *before)


def chosen_columns(ref, parity):
    blocks = ref.shape[1] // L
    return jnp.concatenate(
        [ref[:, pl.ds(pl.multiple_of((2 * p + parity) * L, L), L)] for p in range(blocks // 2)], 1
    )


def chosen_rows(ref, parity):
    return ref[:, parity].reshape(ref.shape[0] * G, ref.shape[3])


def wd_rows(wd, t):
    return jnp.concatenate([wd[c, pl.ds(8 * t, 8)].reshape(8 * G, L) for c in range(wd.shape[0])], 1)


def pair_at(w, t):
    rows = w.shape[1] * G
    return jnp.concatenate([w[2 * t].reshape(rows, L), w[2 * t + 1].reshape(rows, L)], 1)


def once(*dims):
    return pl.BlockSpec(dims, lambda i: (0,) * len(dims), pipeline_mode=pl.Buffered(1))


def ffn_body(groups, pos, x_ref, o_ref, gain_ref, df_hbm, *rest):
    count = [len(g.arrays) for g in groups]
    refs, rest = rest[: sum(count)], rest[sum(count) :]
    of = [refs[: count[0]], refs[count[0] :]]
    (hid_ref, dg_ref, du_ref, sg_ref, su_ref, sd_ref, r1_out, ht_out, ot_out,
     wo_out, wg_out, wu_out, wd_out,
     wo, wg, wu, wd, r1, h2, ht, ot, df, dfs, hts, sem) = rest
    step = pl.program_id(0)
    length = x_ref.shape[0]
    outs = ((r1, r1_out), (ht, ht_out), (ot, ot_out), (wo, wo_out), (wg, wg_out), (wu, wu_out), (wd, wd_out))

    @pl.when(step == 0)
    def _():
        groups[0].fetch(0, of[0], pos, wo, sem.at[0])
        groups[0].fetch(1, of[0], pos, wg, sem.at[1])
        groups[1].fetch(0, of[1], pos, wu, sem.at[2])
        pltpu.make_async_copy(df_hbm, df, sem.at[4]).start()
        groups[1].fetch(1, of[1], pos, wd, sem.at[3])
        other = 1 - lax.rem(pos[1], 2)
        wait_all(wo, sem.at[0])
        w = jnp.concatenate([two(wo, c) for c in range(wo.shape[0] // 2)], 1)
        for i in range(length // QB):
            rows = slice(i * QB, (i + 1) * QB)
            r = x_ref[rows, :].astype(f32) + nn(o_ref[rows, :], w)
            r1[rows, :] = r
            h = r * lax.rsqrt(jnp.mean(r * r, -1, keepdims=True) + EPS) * gain_ref[...]
            h2[rows, :] = h.astype(bf16)
            ht[:, :, :, rows] = h.T.astype(bf16).reshape(ht.shape[:3] + (QB,))
            ot[:, :, :, rows] = o_ref[rows, :].astype(f32).T.astype(bf16).reshape(ht.shape[:3] + (QB,))
        hts[...] = chosen_rows(ht, other)
        wait_all(df, sem.at[4])
        dfs[...] = chosen_columns(df, other)
        wait_all(wg, sem.at[1])
        wait_all(wu, sem.at[2])
        wait_all(wd, sem.at[3])
        for i, (a, b) in enumerate(outs):
            pltpu.make_async_copy(a, b, sem.at[5 + i]).start()

    @pl.when(step > 0)
    def _():
        t = step - 1
        wgt, wut, wdt = pair_at(wg, t), pair_at(wu, t), wd_rows(wd, t)
        for i in range(length // QB):
            rows = slice(i * QB, (i + 1) * QB)
            gate = nn(h2[rows, :], wgt)
            up = nn(h2[rows, :], wut)
            dhid = nt(df[rows, :], wdt)
            sigma = 0.5 + 0.5 * jnp.tanh(0.5 * gate)
            silu = gate * sigma
            hid_ref[rows, :] = (silu * up).astype(bf16)
            dg_ref[rows, :] = (dhid * up * (sigma + silu * (1.0 - sigma))).astype(bf16)
            du_ref[rows, :] = (dhid * silu).astype(bf16)
        gd = tn(hid_ref[...], dfs[...]).astype(bf16)
        for p in range(4):
            sd_ref[:, p] = gd[:, p * L : (p + 1) * L].reshape(8, G, L)
        for ref, grad in ((sg_ref, dg_ref), (su_ref, du_ref)):
            g = nn(hts[...], grad[...]).astype(bf16)
            for c in range(2):
                ref[:, :, c] = g[:, c * L : (c + 1) * L].reshape(4, 4, G, L)

    @pl.when(step == pl.num_programs(0) - 1)
    def _():
        for i, (a, b) in enumerate(outs):
            pltpu.make_async_copy(a, b, sem.at[5 + i]).wait()


def ffn(pos, x, o, df, gain, groups, hidden):
    length, width = x.shape
    tiles = hidden // (2 * L)

    def late(i):
        return jnp.maximum(i - 1, 0)

    col = pl.BlockSpec((length, 2 * L), lambda i: (0, late(i)))
    grad_cols = pl.BlockSpec((4, 4, 2, G, L), lambda i: (0, 0, late(i), 0, 0))
    grad_rows = pl.BlockSpec((8, 4, G, L), lambda i: (late(i), 0, 0, 0))
    ht_dims = (width // G // 2, 2, G, length)
    square, wide = (width // L, width // G, G, L), (hidden // L, width // G, G, L)
    tall = (width // L, hidden // G, G, L)
    kept = [((length, width), f32), (ht_dims, bf16), (ht_dims, bf16)]
    kept += [(square, bf16), (wide, bf16), (wide, bf16), (tall, bf16)]
    vmem = [pltpu.VMEM(*a) for a in kept]
    return pl.pallas_call(
        lambda *refs: ffn_body(groups, *refs),
        grid=(1 + tiles,),
        in_specs=[SMEM, once(length, width), once(length, width), once(1, width), ANY]
        + [s for g in groups for s in g.specs()],
        out_specs=[col, col, col, grad_cols, grad_cols, grad_rows] + [ANY] * 7,
        out_shape=[
            shape((length, hidden)),
            shape((length, hidden)),
            shape((length, hidden)),
            shape((4, 4, hidden // L, G, L)),
            shape((4, 4, hidden // L, G, L)),
            shape((hidden // G, 4, G, L)),
        ]
        + [shape(*a) for a in kept],
        scratch_shapes=vmem[3:]
        + [
            vmem[0],
            pltpu.VMEM((length, width), bf16),
            vmem[1],
            vmem[2],
            pltpu.VMEM((length, width), bf16),
            pltpu.VMEM((length, width // 2), bf16),
            pltpu.VMEM((width // 2, length), bf16),
            pltpu.SemaphoreType.DMA((12,)),
        ],
        compiler_params=params(),
        cost_estimate=cost(46),
        name="ffn",
    )(pos, x, o, gain, df, *[a for g in groups for a in g.arrays])


def ffn_back_body(gain_ref, keep_ref, r1_hbm, df_hbm, wo_hbm, dg_hbm, du_hbm, wg_hbm, wu_hbm,
                  dr_out, da_out, do_out, r1, df, wo, dg, du, wg, wu, acc, da, do, sem):
    length, width = r1.shape
    chunks = chunked(wg.shape[0], 6)
    loads = []
    for i, (low, size) in enumerate(chunks):
        cols = pl.ds(low * L, size * L)
        loads.append(
            [
                pltpu.make_async_copy(a.at[:, cols] if flat else a.at[pl.ds(low, size)],
                                      b.at[:, cols] if flat else b.at[pl.ds(low, size)], sem.at[i])
                for a, b, flat in ((dg_hbm, dg, 1), (wg_hbm, wg, 0), (du_hbm, du, 1), (wu_hbm, wu, 0))
            ]
        )
    last = [pltpu.make_async_copy(a, b, sem.at[len(chunks) + i]) for i, (a, b) in
            enumerate(((r1_hbm, r1), (df_hbm, df), (wo_hbm, wo)))]
    for copies in loads + [last]:
        for c in copies:
            c.start()
    for (low, size), copies in zip(chunks, loads):
        for c in copies:
            c.wait()
        both = jnp.concatenate([a[:, low * L : (low + size) * L] for a in (dg, du)], 1)
        for n in range(width // QB):
            rows = slice(n * QB // G, (n + 1) * QB // G)
            w = jnp.concatenate(
                [a[low + c, rows].reshape(QB, L) for a in (wg, wu) for c in range(size)], 1
            )
            part = nt(both, w)
            if low == 0:
                acc[:, n * QB : (n + 1) * QB] = part
            else:
                acc[:, n * QB : (n + 1) * QB] += part
    for c in last:
        c.wait()
    w = jnp.concatenate([two(wo, c) for c in range(wo.shape[0] // 2)], 1)
    out = []
    for i in range(length // QB):
        rows = slice(i * QB, (i + 1) * QB)
        r = r1[rows, :]
        rinv = lax.rsqrt(jnp.mean(r * r, -1, keepdims=True) + EPS)
        n2 = r * rinv
        dn = acc[rows, :] * gain_ref[...]
        dr = df[rows, :].astype(f32) + rinv * (dn - n2 * jnp.mean(dn * n2, -1, keepdims=True))
        acc[rows, :] = dr
        da[rows, :] = dr.astype(bf16)
        do[rows, :] = (nt(da[rows, :], w) * keep_ref[rows, :]).astype(bf16)
        for k, (a, b) in enumerate(((acc, dr_out), (da, da_out), (do, do_out))):
            c = pltpu.make_async_copy(
                a.at[pl.ds(i * QB, QB)], b.at[pl.ds(i * QB, QB)], sem.at[len(chunks) + 3 + 3 * i + k]
            )
            c.start()
            out.append(c)
    for c in out:
        c.wait()


def ffn_back(r1, df, keep_col, gain, dgate, dup, wo, wg, wu):
    length, width = r1.shape
    hidden = dgate.shape[1]
    vmem = pl.BlockSpec(memory_space=pltpu.VMEM)

    return pl.pallas_call(
        ffn_back_body,
        in_specs=[vmem, vmem] + [ANY] * 7,
        out_specs=[ANY] * 3,
        out_shape=[shape((length, width), f32), shape((length, width)), shape((length, width))],
        scratch_shapes=[like(a) for a in (r1, df, wo, dgate, dup, wg, wu, r1, df, df)]
        + [pltpu.SemaphoreType.DMA((7 + 3 * (length // QB),))],
        compiler_params=params(),
        cost_estimate=cost(22),
        name="ffn_back",
    )(gain, keep_col, r1, df, wo, dgate, dup, wg, wu)


def bits(pos):
    d = pos[1]
    return lax.rem(d, 2), lax.rem(d // 2, 2), lax.rem(d // 4, 2)


def sort_out(out, by_x, value, at, own):
    n = value.shape[1]
    for p in range(4):
        bit, other = (p % 2, p // 2) if by_x else (p // 2, p % 2)
        which = jnp.where(own == bit, 0, 1)
        out[which, other, pl.ds(at, n)] = value[p]


def ffn_grads_body(pos, ht_hbm, df_hbm, hid_hbm, dg_hbm, du_hbm, rg_hbm, ru_hbm, rd_hbm,
                   ka_out, ta_out, kb_out, tb_out,
                   ht, df, hid, dg, du, rg, ru, rd, out_a, out_b, sem):
    core, b1, b2 = bits(pos)
    blocks = rg.shape[2]
    chunks = chunked(blocks, 4)
    first = [pltpu.make_async_copy(ht_hbm.at[:, core], ht, sem.at[0])]
    for p in range(4):
        cols = pl.ds(pl.multiple_of((2 * p + core) * L, L), L)
        first.append(pltpu.make_async_copy(df_hbm.at[:, cols], df.at[:, pl.ds(p * L, L)], sem.at[1 + p]))
    at = 5
    loads = {}
    for name, a, b, ra, rb in (("g", dg_hbm, dg, rg_hbm, rg), ("u", du_hbm, du, ru_hbm, ru), ("d", hid_hbm, hid, rd_hbm, rd)):
        for low, size in chunks:
            cols = pl.ds(low * L, size * L)
            if name == "d":
                some = pl.ds(4 * low, 4 * size)
                pair = (ra.at[some], rb.at[some])
            else:
                some = pl.ds(low, size)
                pair = (ra.at[:, :, some], rb.at[:, :, some])
            loads[name, low] = [
                pltpu.make_async_copy(a.at[:, cols], b.at[:, cols], sem.at[at]),
                pltpu.make_async_copy(*pair, sem.at[at + 1]),
            ]
            at += 2
    for c in first:
        c.start()
    for copies in loads.values():
        for c in copies:
            c.start()
    for c in first:
        c.wait()
    left = ht[...].reshape(ht.shape[0] * G, ht.shape[2])
    targets = ((out_a, ka_out, ta_out), (out_b, kb_out, tb_out))
    sent = []

    def send(which, low, size):
        o, *refs = targets[which]
        some = pl.ds(low, size)
        for i, ref in enumerate(refs):
            sent.append(pltpu.make_async_copy(o.at[i, :, some], ref.at[:, some], sem.at[56 + len(sent)]))
            sent[-1].start()

    for name, grad, got, out, by_x, own in (("g", dg, rg, out_a, True, b1), ("u", du, ru, out_b, False, b2)):
        for low, size in chunks:
            for c in loads[name, low]:
                c.wait()
            g = nn(left, grad[:, low * L : (low + size) * L])
            for s in range(4):
                rows = g[s * 4 * G : (s + 1) * 4 * G].reshape(4, G, size * L)
                value = jnp.stack([rows[:, :, c * L : (c + 1) * L] for c in range(size)], 1)
                value = (value + got[s, :, low : low + size].astype(f32)).astype(bf16)
                sort_out(out, by_x, value, s * blocks + low, own)
        send(0 if by_x else 1, 0, 4 * blocks)
    right = df[...]
    for low, size in chunks:
        for c in loads["d", low]:
            c.wait()
        g = tn(hid[:, low * L : (low + size) * L], right)
        n = 4 * size
        value = jnp.stack([g[:, p * L : (p + 1) * L].reshape(n, G, L) for p in range(4)], 0)
        value = value + jnp.stack([rd[4 * low : 4 * low + n, p].astype(f32) for p in range(4)], 0)
        value = value.astype(bf16)
        edge = min(max(2 * blocks - 4 * low, 0), n)
        if edge:
            sort_out(out_a, True, value[:, :edge], 4 * blocks + 4 * low, b1)
        if edge < n:
            sort_out(out_b, False, value[:, edge:], 4 * blocks + 4 * low + edge - 2 * blocks, b2)
    send(0, 4 * blocks, 2 * blocks)
    send(1, 4 * blocks, 2 * blocks)
    for c in sent:
        c.wait()


def ffn_grads(pos, ht, df, hid, dgate, dup, got):
    length, width = df.shape
    hidden = hid.shape[1]
    half = shape((2, 6 * hidden // L, G, L))
    return pl.pallas_call(
        ffn_grads_body,
        in_specs=[SMEM] + [ANY] * 8,
        out_specs=[ANY] * 4,
        out_shape=[half] * 4,
        scratch_shapes=[
            pltpu.VMEM((ht.shape[0], G, length), bf16),
            pltpu.VMEM((length, width // 2), bf16),
        ]
        + [like(a) for a in (hid, dgate, dup, *got)]
        + [pltpu.VMEM((2,) + half.shape, bf16)] * 2
        + [pltpu.SemaphoreType.DMA((64,))],
        compiler_params=params(),
        cost_estimate=cost(17),
        name="ffn_grads",
    )(pos, ht, df, hid, dgate, dup, *got)


def ffn_out_body(r1_ref, hid_ref, wd, out_ref):
    out_ref[...] = (r1_ref[...] + nn(hid_ref[...], two(wd, 0))).astype(bf16)


def ffn_out(r1, hid, wd):
    length, width = r1.shape
    hidden = hid.shape[1]
    col = pl.BlockSpec((length, 2 * L), lambda i: (0, i))
    return pl.pallas_call(
        ffn_out_body,
        grid=(width // (2 * L),),
        in_specs=[col, once(length, hidden), pl.BlockSpec((2, hidden // G, G, L), lambda i: (i, 0, 0, 0))],
        out_specs=col,
        out_shape=shape((length, width)),
        compiler_params=params(),
        cost_estimate=cost(11),
        name="ffn_out",
    )(r1, hid, wd)


def square_body(keep, pos, ot_hbm, ht_hbm, *rest):
    grads_hbm, rest = rest[:4], rest[4:]
    if keep:
        got_hbm, ka_out, ta_out, kb_out, tb_out, ot, ht, da, dq, dk, dv, got, out_a, out_b, sem = rest
    else:
        out_hbm, ot, ht, da, dq, dk, dv, out, sem = rest
    core, b1, b2 = bits(pos)
    grads = (da, dq, dk, dv)
    mine = core if keep else 1 - core
    blocks = da.shape[1] // L
    loads = [pltpu.make_async_copy(a, b, sem.at[i]) for i, (a, b) in enumerate(zip(grads_hbm, grads))]
    lefts = [pltpu.make_async_copy(a.at[:, mine], b, sem.at[4 + i]) for i, (a, b) in enumerate(((ot_hbm, ot), (ht_hbm, ht)))]
    recv = []
    if keep:
        for i in range(4):
            some = pl.ds(i * blocks, blocks)
            recv.append(pltpu.make_async_copy(got_hbm.at[:, :, some], got.at[:, :, some], sem.at[6 + i]))
            recv[i].start()
    lefts[0].start()
    loads[0].start()
    lefts[1].start()
    for c in loads[1:]:
        c.start()
    sent = []

    def send(a, b):
        sent.append(pltpu.make_async_copy(a, b, sem.at[10 + len(sent)]))
        sent[-1].start()

    for i in range(4):
        if i < 2:
            lefts[i].wait()
        loads[i].wait()
        if keep:
            recv[i].wait()
        ref = (ot, ht, ht, ht)[i]
        left = ref[...].reshape(ref.shape[0] * G, ref.shape[2])
        for low, size in chunked(blocks, 4):
            g = nn(left, grads[i][:, low * L : (low + size) * L])
            for s in range(4):
                rows = g[s * 4 * G : (s + 1) * 4 * G].reshape(4, G, size * L)
                value = jnp.stack([rows[:, :, c * L : (c + 1) * L] for c in range(size)], 1)
                at = i * blocks + low
                if not keep:
                    out[s, :, at : at + size] = value.astype(bf16)
                    continue
                value = (value + got[s, :, at : at + size].astype(f32)).astype(bf16)
                at = s * 2 * blocks + (i % 2) * blocks + low
                sort_out(out_a if i < 2 else out_b, i < 2, value, at, b1 if i < 2 else b2)
        if not keep:
            some = pl.ds(i * blocks, blocks)
            send(out.at[:, :, some], out_hbm.at[:, :, some])
        elif i == 1:
            send(out_a.at[0], ka_out)
            send(out_a.at[1], ta_out)
        elif i == 3:
            send(out_b.at[0], kb_out)
            send(out_b.at[1], tb_out)
    for c in sent:
        c.wait()


def square_grads(pos, ot, ht, grads, got):
    length, width = grads[0].shape
    whole = shape((4, 4, 4 * width // L, G, L))
    half = shape((2, 8 * width // L, G, L))
    keep = got is not None
    left = pltpu.VMEM((ht.shape[0], G, length), bf16)
    return pl.pallas_call(
        lambda *refs: square_body(keep, *refs),
        in_specs=[SMEM] + [ANY] * (7 if keep else 6),
        out_specs=[ANY] * 4 if keep else ANY,
        out_shape=[half] * 4 if keep else whole,
        scratch_shapes=[left, left]
        + [like(a) for a in grads]
        + ([like(whole)] + [pltpu.VMEM((2,) + half.shape, bf16)] * 2 if keep else [like(whole)])
        + [pltpu.SemaphoreType.DMA((14,))],
        compiler_params=params(),
        cost_estimate=cost(10),
        name="square_keep" if keep else "square_send",
    )(pos, ot, ht, *grads, *([got] if keep else []))


def input_grad_body(x_ref, gain_ref, dq_hbm, dk_hbm, dv_hbm, wq_hbm, wk_hbm, wv_hbm, dr_hbm, out_hbm,
                    dq, dk, dv, wq, wk, wv, dr, acc, sem):
    length, width = x_ref.shape
    blocks = width // L
    pairs = ((dq_hbm, dq, wq_hbm, wq), (dk_hbm, dk, wk_hbm, wk), (dv_hbm, dv, wv_hbm, wv))
    loads = [
        (pltpu.make_async_copy(a, b, sem.at[2 * i]), pltpu.make_async_copy(c, d, sem.at[2 * i + 1]))
        for i, (a, b, c, d) in enumerate(pairs)
    ]
    get_dr = pltpu.make_async_copy(dr_hbm, dr, sem.at[6])
    for pair in loads:
        for c in pair:
            c.start()
    get_dr.start()
    for i, (_, grad, _, w) in enumerate(pairs):
        for c in loads[i]:
            c.wait()
        for n in range(width // QB):
            rows = slice(n * QB // G, (n + 1) * QB // G)
            part = nt(grad[...], jnp.concatenate([w[c, rows].reshape(QB, L) for c in range(blocks)], 1))
            if i == 0:
                acc[:, n * QB : (n + 1) * QB] = part
            else:
                acc[:, n * QB : (n + 1) * QB] += part
    get_dr.wait()
    out = []
    for i in range(length // QB):
        rows = slice(i * QB, (i + 1) * QB)
        x = x_ref[rows, :].astype(f32)
        rinv = lax.rsqrt(jnp.mean(x * x, -1, keepdims=True) + EPS)
        n1 = x * rinv
        dn = acc[rows, :] * gain_ref[...]
        acc[rows, :] = dr[rows, :] + rinv * (dn - n1 * jnp.mean(dn * n1, -1, keepdims=True))
        out.append(pltpu.make_async_copy(acc.at[pl.ds(i * QB, QB)], out_hbm.at[pl.ds(i * QB, QB)], sem.at[7 + i]))
        out[-1].start()
    for c in out:
        c.wait()


def input_grad(x, gain, dr1, dq, dk, dv, weights):
    length, width = x.shape
    vmem = pl.BlockSpec(memory_space=pltpu.VMEM)
    return pl.pallas_call(
        input_grad_body,
        in_specs=[vmem, vmem] + [ANY] * 7,
        out_specs=ANY,
        out_shape=shape((length, width), f32),
        scratch_shapes=[like(a) for a in (dq, dk, dv, *weights, dr1, dr1)]
        + [pltpu.SemaphoreType.DMA((7 + length // QB,))],
        compiler_params=params(),
        cost_estimate=cost(14),
        name="input_grad",
    )(x, gain, dq, dk, dv, *weights, dr1)


def place_body(tall, pos, *refs):
    pieces, outs = refs[:10], refs[10:]
    blocks = []
    for which, out in enumerate(outs[:-3] if tall else outs):
        blocks += [(which, c) for c in range(out.shape[1] // L)]
    if tall:
        blocks += [(len(outs) - 3, j) for j in range(outs[-3].shape[0] // G)] + [(None, 0)]
    d = pos[1]
    for array, mask, low, size in piece_sources(pieces[0].shape[1]):
        piece = d ^ mask
        rows = pl.ds(pl.multiple_of(piece * G, G), G)
        cols = pl.ds(pl.multiple_of(piece * L, L), L)
        for c in range(size):
            which, at = blocks[low + c]
            value = pieces[array][0, c].astype(f32)
            if which is None:
                outs[-1][piece] = value
            elif tall and which == len(outs) - 3:
                outs[which][at * G : (at + 1) * G, cols] = value
            else:
                outs[which][rows, at * L : (at + 1) * L] = value
    if tall:
        total = outs[-1][0]
        for piece in range(1, 8):
            total = total + outs[-1][piece]
        outs[-2][...] = total


def place(pos, arrays, widths, rows, tall=None):
    vmem = pl.BlockSpec(memory_space=pltpu.VMEM)
    outs = [shape((rows, w), f32) for w in widths]
    if tall is not None:
        outs += [shape(tall, f32), shape((G, L), f32)]
    return pl.pallas_call(
        lambda *refs: place_body(tall is not None, *refs),
        in_specs=[SMEM] + [vmem] * 10,
        out_specs=[vmem] * len(outs),
        out_shape=outs,
        scratch_shapes=[] if tall is None else [pltpu.VMEM((8, G, L), f32)],
        compiler_params=params(),
        name="place",
    )(pos, *arrays)


def layout(lengths, length):
    position = jnp.arange(length, dtype=jnp.int32)
    ends = jnp.cumsum(lengths).astype(jnp.int32)
    seg = jnp.sum((position[:, None] >= ends[None, :]).astype(jnp.int32), 1)
    onehot = seg[:, None] == jnp.arange(lengths.shape[0], dtype=jnp.int32)[None, :]
    first = jnp.sum(jnp.where(onehot, (ends - lengths)[None, :], 0), 1)
    last = jnp.sum(jnp.where(onehot, ends[None, :], 0), 1)
    rel = (position - first).astype(f32)
    inverse = 10000.0 ** (-jnp.arange(HEAD_DIM // 2, dtype=f32) * 2.0 / HEAD_DIM)
    angle = rel[:, None] * inverse[None, :]
    keep = (seg < lengths.shape[0] - 1).astype(f32)
    cos, sin = jnp.cos(angle), jnp.sin(angle)
    cos_w = jnp.concatenate([cos] * 4, 1)
    sin_w = jnp.concatenate([-sin, sin] * 2, 1)
    return cos_w, sin_w, first[None, :], last[None, :], keep[:, None]


def add(*terms):
    total = terms[0].astype(f32)
    for t in terms[1:]:
        total = total + t.astype(f32)
    return total


def halve(kept, got, bit):
    picked = []
    for at in (1 - bit, bit):
        parts = [lax.dynamic_index_in_dim(x, at, 0, keepdims=False) for x in (kept, got)]
        picked.append(add(*parts).astype(bf16))
    return picked


def in_parts(sums):
    parts = []
    for _ in range(3):
        part = lax.reduce_precision(sums, 8, 7)
        parts.append(part)
        sums = sums - part
    return jnp.pad(jnp.stack(parts).astype(bf16), ((0, G - 3), (0, L - 2)))


def from_parts(block):
    parts = block[..., :3, :2].astype(f32)
    return parts[..., 0, :] + parts[..., 1, :] + parts[..., 2, :]


def to_shards(total, z, extra=None):
    terms = [lax.dynamic_index_in_dim(total, z, 0, keepdims=False)]
    if extra is not None:
        terms[0] = jnp.concatenate([terms[0], extra[None]])
    for s in (1, 2, 3):
        away = lax.dynamic_index_in_dim(total, lax.rem(z + s, 4), 0, keepdims=False)
        if extra is not None:
            away = jnp.concatenate([away, extra[None]])
        terms.append(fsdp_shift(away, s))
    return terms


def sums_over_fsdp(terms, z):
    numbers = jnp.stack([from_parts(t[-1]) for t in terms])
    sums = jnp.zeros_like(numbers[0])
    for shard in range(4):
        sums = sums + lax.dynamic_index_in_dim(numbers, lax.rem(z + 4 - shard, 4), 0, keepdims=False)
    return sums


def back_over_dp(reduced):
    g = Gather.__new__(Gather)
    g.count, g.start = reduced.shape[0], reduced[None]
    g.x, g.y = dp_swap(g.start, 2), dp_swap(g.start, 4)
    return g


def unfold_rows(w):
    return w.transpose(0, 2, 1, 3).reshape(w.shape[0] * G, w.shape[1] * L)


def sum_whole(grad):
    part = lax.psum_scatter(grad.astype(bf16), "fsdp", scatter_dimension=0, tiled=True)
    return lax.psum(part, "dp").astype(f32)


def local(
    layer_in, first_values, first_values_grad, cotangent, doc_lengths, norm1_gain,
    w_query, w_key, w_value, w_out, norm2_gain, w_gate, w_up, w_down,
):
    rows, length, width = layer_in.shape
    hidden = w_gate.shape[1]
    dp, fsdp = lax.axis_size("dp"), lax.axis_size("fsdp")
    fast = fast_mesh(dp, fsdp, w_query.shape[0])
    z, d = lax.axis_index("fsdp"), lax.axis_index("dp")
    b1, b2 = lax.rem(d // 2, 2), lax.rem(d // 4, 2)
    x, v1 = layer_in[0], first_values[0]
    df = cotangent[0]
    gains = jnp.stack([norm1_gain, norm2_gain])
    c, h = width // L, hidden // L
    members = (
        ((w_query, w_key, w_value), ((c, True),) * 3),
        ((w_out, w_gate), ((c, True), (h, True))),
        ((w_up, w_down), ((h, True), (w_down.shape[0] // G, False))),
    )
    if fast:
        pos = jnp.stack([z, d]).astype(jnp.int32)
        extra = jnp.pad(gains.reshape(-1, L), ((0, G - gains.size // L), (0, 0)))
        g1 = Gather(cut(pos, *members[0], extra), True)
        far = jnp.stack([e[: gains.size // L].reshape(gains.shape) for e in g1.extras])
        mines = [cut(after(pos, g1.extras[0]), *m) for m in members[1:]]
        g1.near()
        g2 = Gather(after(mines[0], g1.start))
        g1.corner(*g2.far)
        g2.near()
        g3 = Gather(after(mines[1], g2.start))
        g1.core()
        g1.core_corner()
        groups = [Group(members[0][1], members[0][0], g1.arrays(), False)]
        whole_gains = jnp.concatenate(
            [lax.dynamic_index_in_dim(far, lax.rem(z + 4 - j, 4), 0, keepdims=False) for j in range(4)], 1
        )
    else:
        pos = jnp.zeros((2,), jnp.int32)

        def blocks(w, by_rows):
            full = lax.all_gather(w, "fsdp", axis=0, tiled=True)
            return row_pieces(full, full.shape[0] // G).transpose(1, 0, 2, 3) if by_rows else column_pieces(full, c)

        whole_gains = lax.all_gather(gains, "fsdp", axis=1, tiled=True)
        groups = [
            Group(tensors, [], [blocks(w, t[1]) for w, t in zip(weights, tensors)], True)
            for weights, tensors in members
        ]
    whole_gains = whole_gains.astype(f32)
    gain_1, gain_2 = whole_gains[:1], whole_gains[1:]
    cos_w, sin_w, first_row, last_row, keep_col = layout(doc_lengths[0], length)

    q, k, vm, h1t, sums, wq, wk, wv = qkv(pos, x, v1, gain_1, cos_w, sin_w, groups[0])
    squares = jnp.sum(sums, (1, 2))
    entries = rows * length * width * dp * fsdp
    if fast:
        g2.corner(q)
        q = after(q, g2.x, g2.y)
    o, lse_1 = attend_fwd(q, k, vm, last_row, keep_col, 0, 3)
    if fast:
        g3.near(o)
        g2.core(o)
        o = after(o, g2.c1, g2.c2, g3.start)
    o, lse_2 = attend_fwd(q, k, vm, last_row, keep_col, 3, 5, o)
    if fast:
        g3.corner(o)
        g2.core_corner(o)
        g3.core(o)
        g3.core_corner()
        groups += [Group(members[i][1], members[i][0], g.arrays(), False) for i, g in ((1, g2), (2, g3))]
    hid, dgate, dup, sg, su, sd, r1, h2t, ot, wo, wg, wu, wd = ffn(pos, x, o, df, gain_2, groups[1:], hidden)
    got = [dp_swap(g, 1) if fast else jnp.zeros_like(g) for g in (sg, su, sd)]
    dr1, da, do = ffn_back(r1, df, keep_col, gain_2, dgate, dup, wo, wg, wu)
    ka, ta, kb, tb = ffn_grads(pos, h2t, df, hid, dgate, dup, after(got, da))
    if fast:
        na, nb = dp_swap(ta, 2), dp_swap(tb, 4)
    back = (first_row, cos_w, -sin_w, first_values_grad[0])
    results = attend_bwd(q, k, vm, after(do, ta), lse_1.T, *back, 0, 3)
    dq, dk, dv, first_out = attend_bwd(q, k, vm, do, lse_2.T, *back, 3, 5, results)
    grads = (da, dq, dk, dv)
    if fast:
        na, nb = after((na, nb), dq)
        ta, ka = halve(ka, na, b2)
        tb, kb = halve(kb, nb, b1)
        ma, mb = dp_swap(ta, 4), dp_swap(tb, 2)
        grads = after(grads, ta, tb)
    send = square_grads(pos, ot, h1t, grads, None)
    swapped = dp_swap(send, 1) if fast else jnp.zeros_like(send)
    d_x = input_grad(after(x, send), gain_1, dr1, dq, dk, dv, (wq, wk, wv))
    swapped = after(swapped, d_x)
    if fast:
        ma, mb = after((ma, mb), d_x)
        total_a, total_b = add(ka, ma).astype(bf16), add(kb, mb).astype(bf16)
        n = 4 * hidden // L
        cols_a, cols_b = [t[:n].reshape(4, n // 4, G, L) for t in (total_a, total_b)]
        cols_d = jnp.concatenate([total_a[n:], total_b[n:]]).reshape(4, n // 4, G, L)
        wide_terms = to_shards(jnp.concatenate([cols_a, cols_b, cols_d], 1), z, in_parts(squares))
    ks, ts, kt, tt = square_grads(pos, ot, h1t, grads, swapped)
    if fast:
        ns, n_t = dp_swap(ts, 2), dp_swap(tt, 4)
    out = ffn_out(r1, after(hid, ts), wd)
    if fast:
        ns, n_t = after((ns, n_t), out)
        ts, ks = halve(ks, ns, b2)
        tt, kt = halve(kt, n_t, b1)
        ms, mt = dp_swap(ts, 4), dp_swap(tt, 2)
        wide_terms = after(wide_terms, ts, tt)
        reduced = add(*[t[:-1] for t in wide_terms]).astype(bf16)
        wide = back_over_dp(jnp.concatenate([reduced, in_parts(sums_over_fsdp(wide_terms, z))[None]]))
        total_s, total_t = add(ks, ms).astype(bf16), add(kt, mt).astype(bf16)
        both = [t.reshape((4, -1) + t.shape[1:]) for t in (total_s, total_t)]
        last_terms = to_shards(jnp.concatenate(both, 1), z)
        wide.corner(*both)
        wide.core()
        wide.core_corner()
        grad_wg, grad_wu, grad_wd, squares = place(
            pos, wide.arrays(), [hidden] * 2, w_query.shape[0], (w_down.shape[0], width)
        )
        squares = from_parts(squares)
        last = back_over_dp(add(*last_terms).astype(bf16))
        last.corner()
        last.core()
        last.core_corner()
        grad_wo, grad_wq, grad_wk, grad_wv = place(pos, last.arrays(), [width] * 4, w_query.shape[0])
    else:
        squares = lax.psum(squares, ("dp", "fsdp"))
        n = 4 * hidden // L
        even_a, even_b = jnp.stack([ka, ta], 1), jnp.stack([kb, tb], 0)
        even_a, even_b = [e.reshape((4,) + ka.shape[1:]) for e in (even_a, even_b)]
        grad_wg, grad_wu = join(even_a[:, :n], sg), join(even_b[:, :n], su)
        even_d = jnp.concatenate([even_a[:, n:], even_b[:, n:]], 1).transpose(1, 0, 2, 3)
        grad_wd = jnp.stack([even_d, sd], 2).reshape(n, 8, G, L).transpose(0, 2, 1, 3).reshape(hidden, width)
        n = 2 * width // L
        even_s, even_t = jnp.stack([ks, ts], 1), jnp.stack([kt, tt], 0)
        firsts = join(even_s.reshape((4,) + ks.shape[1:]), send[:, :, :n])
        seconds = join(even_t.reshape((4,) + ks.shape[1:]), send[:, :, n:])
        grad_wo, grad_wq = firsts[:, :width], firsts[:, width:]
        grad_wk, grad_wv = seconds[:, :width], seconds[:, width:]
        grad_wo, grad_wq, grad_wk, grad_wv, grad_wg, grad_wu, grad_wd = [
            sum_whole(g) for g in (grad_wo, grad_wq, grad_wk, grad_wv, grad_wg, grad_wu, grad_wd)
        ]
    def along(*pairs):
        return sum(jnp.sum(w.astype(f32) * g, 1) for w, g in pairs)

    grad_g1 = along((w_query, grad_wq), (w_key, grad_wk), (w_value, grad_wv)) / norm1_gain.astype(f32)
    grad_g2 = along((w_gate, grad_wg), (w_up, grad_wu)) / norm2_gain.astype(f32)
    return (
        out[None], d_x[None], first_out[None], grad_g1, grad_wq, grad_wk, grad_wv, grad_wo, grad_g2,
        grad_wg, grad_wu, grad_wd, squares / entries,
    )


def join(even, odd):
    even = even.reshape((4, 4, -1) + even.shape[2:]).transpose(1, 0, 2, 3, 4)
    both = jnp.stack([even, odd], 2)
    return unfold_rows(both.reshape((32,) + odd.shape[2:]))


def solution(mesh):
    by_row = P(("dp", "fsdp"), None, None)
    shard = P("fsdp", None)
    return jax.shard_map(
        local,
        mesh=mesh,
        in_specs=(by_row,) * 4
        + (P(("dp", "fsdp"), None), P("fsdp"), shard, shard, shard, shard, P("fsdp"), shard, shard, shard),
        out_specs=(by_row,) * 3
        + (P("fsdp"), shard, shard, shard, shard, P("fsdp"), shard, shard, shard, P()),
        check_vma=False,
    )
```

time: 623 us -> 471 us (0.76)
  waiting for transfers between devices: 142 us -> 87 us
  Pallas kernels: 278 us -> 241 us
  local copies, waits for them, and re-layouts: 59.5 us -> 25.7 us
  between operations: 15.7 us -> 2.16 us
  other arithmetic: 38.9 us -> 30.1 us
    ppermute x18 -> x15, waiting for transfers between devices: 89.1 us -> 38.8 us  [fsdp_shift(): lax.ppermute(x, 'fsdp', [(i, (i + step) % size) for i in range(size)])]
    pallas_call x9 -> x12, Pallas kernels: 181 us -> 149 us  [the longest x1 46 us: ffn(): pl.pallas_call(lambda *refs: ffn_body(groups, *refs), grid=(1 + tiles,),...]
    unnamed x136 -> x121, local copies, waits for them, and re-layouts: 14.3 us -> 5.78 us
    reshape x15 -> x0, local copies, waits for them, and re-layouts: 7.52 us -> none  [the longest x14 6.16 us: row_pieces(): return w.reshape(count, G, w.shape[1] // L, L).transpose(0, 2, 1, 3)]
    pallas_call x6 -> x0, local copies, waits for them, and re-layouts: 7.24 us -> none  [the longest x4 4.78 us: ffn_grads(): pl.pallas_call(ffn_grads_body, grid=(tiles,), in_specs=[SMEM, once(*ht.sh...]
    ppermute x61 -> x57, waiting for transfers between devices: 52.9 us -> 48.1 us  [dp_swap(): lax.ppermute(x, 'dp', [(i, i ^ bit) for i in range(lax.axis_size('dp'))])]
    pallas_call x3 -> x2, Pallas kernels: 50.4 us -> 47.6 us  [attend_bwd(): pl.pallas_call(attend_bwd_body, grid=(pairs,), in_specs=[col] * 4 + [whol...]
    ppermute x61 -> x57, starting transfers between devices: 55.1 us -> 57.3 us  [dp_swap(): lax.ppermute(x, 'dp', [(i, i ^ bit) for i in range(lax.axis_size('dp'))])]
  transfers between devices with their start and end apart: 80 -> 72, of which waited for: 19 -> 18; matrix products, arithmetic and copies ran while one was open for 9% -> 8% of each run, Pallas kernels for 38% -> 37%
where the time goes in v2:
time: 471 us; the launch traced here: 465 us
  Pallas kernels  241 us (51%)
  waiting for transfers between devices  87 us (18%)
  starting transfers between devices  79.4 us (17%)
  other arithmetic  30.1 us (6%)
  local copies, waits for them, and re-layouts  25.7 us (5%)
    ppermute x57, starting transfers between devices, dp_swap(): lax.ppermute(x, 'dp', [(i, i ^ bit) for i in range(lax.axis_size('dp'))])  57.3 us
    ppermute x57, waiting for transfers between devices, dp_swap(): lax.ppermute(x, 'dp', [(i, i ^ bit) for i in range(lax.axis_size('dp'))])  48.1 us
    pallas_call x2, Pallas kernels, attend_bwd(): pl.pallas_call(attend_bwd_body, grid=(pairs,), in_specs=[col] * 4 + [whol...  47.6 us
    pallas_call x1, Pallas kernels, ffn(): pl.pallas_call(lambda *refs: ffn_body(groups, *refs), grid=(1 + tiles,),...  46 us
    ppermute x15, waiting for transfers between devices, fsdp_shift(): lax.ppermute(x, 'fsdp', [(i, (i + step) % size) for i in range(size)])  38.8 us
    pallas_call x2, Pallas kernels, attend_fwd(): pl.pallas_call(attend_fwd_body, grid=(pairs,), in_specs=[col, col, col, p...  32.6 us
    ppermute x15, starting transfers between devices, fsdp_shift(): lax.ppermute(x, 'fsdp', [(i, (i + step) % size) for i in range(size)])  22.1 us
    pallas_call x1, Pallas kernels, ffn_back(): pl.pallas_call(ffn_back_body, in_specs=[vmem, vmem] + [ANY] * 7, out_spec...  21.5 us
  transfers between devices with their start and end apart: 72, of which 18 were waited for; matrix products, arithmetic and copies ran while one was open for 8% of the time, Pallas kernels for 37%

profile of v2, /device:TPU:9, one launch (start us, length us, event | category | flops | bytes accessed | tf_op | source)
XLA Modules:
  0.0 465.3 jit_solution(11439451915006595023)
XLA Ops:
  14.9 6.3 %collective-permute-done.1 = bf16[25,32,128]{2,1,0:T(8,128)(2,1)S(1)} collective-permute-done((bf16[25,32,128]{2,1,0:T(8,128)(2,1)}, bf16[25,32,128]{2,1,0:T(8,128)(2,1)S(1)}, u32[]{:S(2)}, u32[]{:S(2)}) %collective-permute-start.1) | collective-permute-done | bytes 204832 | tf_op jit(solution)/shard_map/ppermute | solution.py:68
  21.2 4.4 collective-permute-done
  35.0 9.8 %collective-permute-done.6 = bf16[30,32,128]{2,1,0:T(8,128)(2,1)S(1)} collective-permute-done((bf16[30,32,128]{2,1,0:T(8,128)(2,1)S(1)}, bf16[30,32,128]{2,1,0:T(8,128)(2,1)S(1)}, u32[]{:S(2)}, u32[]{:S(2)}) %collective-permute-start.6) | collective-permute-done | bytes 245792 | tf_op jit(solution)/shard_map/ppermute | solution.py:68
  44.8 5.3 %collective-permute-done.5 = bf16[30,32,128]{2,1,0:T(8,128)(2,1)S(1)} collective-permute-done((bf16[30,32,128]{2,1,0:T(8,128)(2,1)S(1)}, bf16[30,32,128]{2,1,0:T(8,128)(2,1)S(1)}, u32[]{:S(2)}, u32[]{:S(2)}) %collective-permute-start.5) | collective-permute-done | bytes 245792 | tf_op jit(solution)/shard_map/ppermute | solution.py:68
  65.3 8.8 %collective-permute-done.9.refs_13_ = bf16[3,12,32,128]{3,2,1,0:T(8,128)(2,1)} collective-permute-done((bf16[3,12,32,128]{3,2,1,0:T(8,128)(2,1)S(1)}, bf16[3,12,32,128]{3,2,1,0:T(8,128)(2,1)}, u32[]{:S(2)}, u32[]{:S(2)}) %collective-permute-start.9) | collective-permute-done | bytes 294944 | tf_op jit(solution)/shard_map/ppermute | solution.py:59
  84.7 14.6 %qkv.1 = (bf16[1024,1024]{1,0:T(8,128)(2,1)}, bf16[1024,1024]{1,0:T(8,128)(2,1)}, bf16[1024,1024]{1,0:T(8,128)(2,1)}, bf16[16,2,32,1024]{3,2,1,0:T(8,128)(2,1)},...) custom-call(s32[2]{0:T(128)} %pad_add_fusion.refs_0_.pos, ...), custom_call_target="tpu_custom_call" | custom-call | flops 60000002048 | tf_op jit(solution)/shard_map/qkv/pallas_call | solution.py:279
  100.9 12.8 %attend_fwd.2 = (bf16[1024,1024]{1,0:T(8,128)(2,1)}, f32[1024,128]{1,0:T(8,128)}) custom-call(bf16[1024,1024]{1,0:T(8,128)(2,1)} %get-tuple-element.125.q_ref, bf16[1024,1024]{1,0:T(8,128)(2,1)} %get-tuple-element.126.k_ref, bf16[1024,1024]{1,0:T(8,128)(2,1)} %get-tuple-element.127.v_ref, s32[1,1024]{1,0:T(1,128)} %bitcast.137, f32[1024,1]{1,0:T(8,128)} %copy.46.keep_ref), custom_call_target="tpu_custom_call" | custom-call | flops 50400002048 | tf_op jit(solution)/shard_map/attend_fwd/pallas_call | solution.py:337
  117.5 19.7 %attend_fwd.3 = (bf16[1024,1024]{1,0:T(8,128)(2,1)}, f32[1024,128]{1,0:T(8,128)}) custom-call(bf16[1024,1024]{1,0:T(8,128)(2,1)} %get-tuple-element.125.q_ref, bf16[1024,1024]{1,0:T(8,128)(2,1)} %get-tuple-element.126.k_ref, bf16[1024,1024]{1,0:T(8,128)(2,1)} %get-tuple-element.127.v_ref, s32[1,1024]{1,0:T(1,128)} %bitcast.138, ...), custom_call_target="tpu_custom_call", output_to_operand_aliasing={{0}: (5, {})} | custom-call | flops 83999997952 | tf_op jit(solution)/shard_map/attend_fwd/pallas_call | solution.py:337
  141.6 3.0 collective-permute-start.23
  145.2 5.2 %collective-permute-done.30.refs_23_ = bf16[3,22,32,128]{3,2,1,0:T(8,128)(2,1)S(1)} collective-permute-done((bf16[3,22,32,128]{3,2,1,0:T(8,128)(2,1)S(1)}, bf16[3,22,32,128]{3,2,1,0:T(8,128)(2,1)S(1)}, u32[]{:S(2)}, u32[]{:S(2)}) %collective-permute-start.30) | collective-permute-done | bytes 540704 | tf_op jit(solution)/shard_map/ppermute | solution.py:59
  150.4 3.3 collective-permute-start.33
  160.7 46.0 %ffn.1 = (bf16[1024,2816]{1,0:T(8,128)(2,1)}, bf16[1024,2816]{1,0:T(8,128)(2,1)}, bf16[1024,2816]{1,0:T(8,128)(2,1)}, bf16[4,4,22,32,128]{4,3,2,1,0:T(8,128)(2,1...) custom-call(s32[2]{0:T(128)} %pad_add_fusion.refs_0_.pos, ...), custom_call_target="tpu_custom_call" | custom-call | flops 184000004096 | tf_op jit(solution)/shard_map/ffn/pallas_call | solution.py:548
  207.5 21.5 %ffn_back.1 = (f32[1024,1024]{1,0:T(8,128)}, bf16[1024,1024]{1,0:T(8,128)(2,1)}, bf16[1024,1024]{1,0:T(8,128)(2,1)}) custom-call(f32[1,1024]{1,0:T(1,128)} %get-tuple-element.234.refs_3_.gain_ref, f32[1024,1]{1,0:T(8,128)} %copy.46.keep_ref, f32[1024,1024]{1,0:T(8,128)} %get-tuple-element.147.r1_hbm.r1_ref, bf16[1024,1024]{1,0:T(8,128)(2,1)} %bitcast.145, ...), custom_call_target="tpu_custom_call" | custom-call | flops 88000004096 | tf_op jit(solution)/shard_map/ffn_back/pallas_call | solution.py:642
  231.5 17.6 %ffn_grads.1 = (bf16[2,132,32,128]{3,2,1,0:T(8,128)(2,1)}, bf16[2,132,32,128]{3,2,1,0:T(8,128)(2,1)}, bf16[2,132,32,128]{3,2,1,0:T(8,128)(2,1)}, bf16[2,132,32,128]{3,2,1,0:T(8,128)(2,1)}) custom-call(s32[2]{0:T(128)} %pad_add_fusion.refs_0_.pos, bf16[16,2,32,1024]{3,2,1,0:T(8,128)(2,1)} %get-tuple-element.159.ht_hbm, bf16[1024,1024]{1,0:T(8,128)(2,1)} %bitcast.146, ...), custom_call_target="tpu_custom_call" | custom-call | flops 67999997952 | tf_op jit(solution)/shard_map/ffn_grads/pallas_call | solution.py:747
  250.7 18.6 %attend_bwd.2 = (bf16[1024,1024]{1,0:T(8,128)(2,1)}, bf16[1024,1024]{1,0:T(8,128)(2,1)}, bf16[1024,1024]{1,0:T(8,128)(2,1)}, f32[1024,1024]{1,0:T(8,128)}) custom-call(bf16[1024,1024]{1,0:T(8,128)(2,1)} %get-tuple-element.125.q_ref, bf16[1024,1024]{1,0:T(8,128)(2,1)} %get-tuple-element.126.k_ref, bf16[1024,1024]{1,0:T(8,128)(2,1)} %get-tuple-element.127.v_ref, ...), custom_call_target="tpu_custom_call" | custom-call | flops 65999998976 | tf_op jit(solution)/shard_map/attend_bwd/pallas_call | solution.py:423
  269.3 29.0 %attend_bwd.3 = (bf16[1024,1024]{1,0:T(8,128)(2,1)}, bf16[1024,1024]{1,0:T(8,128)(2,1)}, bf16[1024,1024]{1,0:T(8,128)(2,1)}, f32[1024,1024]{1,0:T(8,128)}) custom-call(bf16[1024,1024]{1,0:T(8,128)(2,1)} %get-tuple-element.125.q_ref, ...), custom_call_target="tpu_custom_call", output_to_operand_aliasing={{0}: (9, {}), {1}: (10, {}), {2}: (11, {}), {3}: (12, {})} | custom-call | flops 109999996928 | tf_op jit(solution)/shard_map/attend_bwd/pallas_call | solution.py:423
  305.0 8.7 %square_send.1 = bf16[4,4,32,32,128]{4,3,2,1,0:T(8,128)(2,1)} custom-call(s32[2]{0:T(128)} %pad_add_fusion.refs_0_.pos, bf16[16,2,32,1024]{3,2,1,0:T(8,128)(2,1)} %get-tuple-element.149.refs_1_, bf16[16,2,32,1024]{3,2,1,0:T(8,128)(2,1)} %get-tuple-element.150.refs_2_, bf16[1024,1024]{1,0:T(8,128)(2,1)} %get-tuple-element.181.refs_3_, ...), custom_call_target="tpu_custom_call" | custom-call | flops 40000000000 | tf_op jit(solution)/shard_map/square_send/pallas_call | solution.py:853
  315.6 13.9 %input_grad.1 = f32[1024,1024]{1,0:T(8,128)} custom-call(bf16[1024,1024]{1,0:T(8,128)(2,1)} %bitcast.149, f32[1,1024]{1,0:T(1,128)} %get-tuple-element.235.refs_1_.gain_ref, bf16[1024,1024]{1,0:T(8,128)(2,1)} %get-tuple-element.182.refs_4_.dq_hbm, bf16[1024,1024]{1,0:T(8,128)(2,1)} %get-tuple-element.183.refs_5_.dk_hbm, ...), custom_call_target="tpu_custom_call" | custom-call | flops 56000000000 | tf_op jit(solution)/shard_map/input_grad/pallas_call | solution.py:910
  338.7 3.7 collective-permute-start.61
  342.3 10.3 %square_keep.1 = (bf16[2,64,32,128]{3,2,1,0:T(8,128)(2,1)}, bf16[2,64,32,128]{3,2,1,0:T(8,128)(2,1)}, bf16[2,64,32,128]{3,2,1,0:T(8,128)(2,1)}, bf16[2,64,32,128]{3,2,1,0:T(8,128)(2,1)}) custom-call(s32[2]{0:T(128)} %pad_add_fusion.refs_0_.pos, bf16[16,2,32,1024]{3,2,1,0:T(8,128)(2,1)} %get-tuple-element.149.refs_1_, ...), custom_call_target="tpu_custom_call" | custom-call | flops 40000000000 | tf_op jit(solution)/shard_map/square_keep/pallas_call | solution.py:853
  354.1 11.3 %ffn_out.1 = bf16[1024,1024]{1,0:T(8,128)(2,1)} custom-call(f32[1024,1024]{1,0:T(8,128)} %get-tuple-element.147.r1_hbm.r1_ref, bf16[1024,2816]{1,0:T(8,128)(2,1)} %get-tuple-element.192.hid_hbm.hid_ref, bf16[8,88,32,128]{3,2,1,0:T(8,128)(2,1)} %get-tuple-element.193.wd), custom_call_target="tpu_custom_call" | custom-call | flops 44000002048 | tf_op jit(solution)/shard_map/ffn_out/pallas_call | solution.py:773
  365.4 10.5 %collective-permute-done.43 = bf16[2,64,32,128]{3,2,1,0:T(8,128)(2,1)S(1)} collective-permute-done((bf16[2,64,32,128]{3,2,1,0:T(8,128)(2,1)}, bf16[2,64,32,128]{3,2,1,0:T(8,128)(2,1)S(1)}, u32[]{:S(2)}, u32[]{:S(2)}) %collective-permute-start.43) | collective-permute-done | bytes 1048608 | tf_op jit(solution)/shard_map/ppermute | solution.py:59
  376.3 8.7 %collective-permute-done.61 = bf16[67,32,128]{2,1,0:T(8,128)(2,1)} collective-permute-done((bf16[67,32,128]{2,1,0:T(8,128)(2,1)S(1)}, bf16[67,32,128]{2,1,0:T(8,128)(2,1)}, u32[]{:S(2)}, u32[]{:S(2)}) %collective-permute-start.61) | collective-permute-done | bytes 548896 | tf_op jit(solution)/shard_map/ppermute | solution.py:68
  392.3 8.6 %collective-permute-done.45 = bf16[64,32,128]{2,1,0:T(8,128)(2,1)S(1)} collective-permute-done((bf16[64,32,128]{2,1,0:T(8,128)(2,1)S(1)}, bf16[64,32,128]{2,1,0:T(8,128)(2,1)S(1)}, u32[]{:S(2)}, u32[]{:S(2)}) %collective-permute-start.45) | collective-permute-done | bytes 524320 | tf_op jit(solution)/shard_map/ppermute | solution.py:59
  402.7 3.3 collective-permute-start.47
  407.4 6.7 %collective-permute-done.64.refs_3_ = bf16[1,67,32,128]{3,2,1,0:T(8,128)(2,1)S(1)} collective-permute-done((bf16[1,67,32,128]{3,2,1,0:T(8,128)(2,1)S(1)}, bf16[1,67,32,128]{3,2,1,0:T(8,128)(2,1)S(1)}, u32[]{:S(2)}, u32[]{:S(2)}) %collective-permute-start.64) | collective-permute-done | bytes 548896 | tf_op jit(solution)/shard_map/ppermute | solution.py:59
  414.4 9.4 %collective-permute-start.67 = (bf16[1,67,32,128]{3,2,1,0:T(8,128)(2,1)S(1)}, bf16[1,67,32,128]{3,2,1,0:T(8,128)(2,1)S(1)}, u32[]{:S(2)}, u32[]{:S(2)}) collective-permute-start(bf16[1,67,32,128]{3,2,1,0:T(8,128)(2,1)S(1)} %maximum_bitcast_fusion.refs_1_), channel_id=1, source_target_pairs={{0,4},{4,0},{8,12},{12,8},{16,20},{20,16},{24,28},{28,24},{1,5},{5... | collective-permute-start | bytes 1646600 | tf_op jit(solution)/shard_map/ppermute | solution.py:59
  423.8 2.8 collective-permute-start.69
  426.6 3.0 collective-permute-done.48
  432.0 6.3 %collective-permute-done.50.refs_3_ = bf16[1,32,32,128]{3,2,1,0:T(8,128)(2,1)S(1)} collective-permute-done((bf16[1,32,32,128]{3,2,1,0:T(8,128)(2,1)S(1)}, bf16[1,32,32,128]{3,2,1,0:T(8,128)(2,1)S(1)}, u32[]{:S(2)}, u32[]{:S(2)}) %collective-permute-start.50) | collective-permute-done | bytes 262176 | tf_op jit(solution)/shard_map/ppermute | solution.py:59
  444.9 5.9 %place.3 = (f32[256,2816]{1,0:T(8,128)}, f32[256,2816]{1,0:T(8,128)}, f32[704,1024]{1,0:T(8,128)}, f32[32,128]{1,0:T(8,128)}) custom-call(s32[2]{0:T(128)} %pad_add_fusion.refs_0_.pos, bf16[1,67,32,128]{3,2,1,0:T(8,128)(2,1)} %copy-done.4, bf16[1,67,32,128]{3,2,1,0:T(8,128)(2,1)} %copy-done.11, bf16[1,67,32,128]{3,2,1,0:T(8,128)(2,1)} %copy-done.10, ...), custom_call_target="tpu_custom_call" | custom-call | tf_op jit(solution)/shard_map/place/pallas_call | solution.py:956
  458.3 3.8 place.2
  (344 shorter events, 120.3 us)
Async XLA Ops:
  25.7 26.9 %collective-permute-start.4 = (bf16[3,24,32,128]{3,2,1,0:T(8,128)(2,1)S(1)}, bf16[3,24,32,128]{3,2,1,0:T(8,128)(2,1)}, u32[]{:S(2)}, u32[]{:S(2)}) collective-permute-start(bf16[3,24,32,128]{3,2,1,0:T(8,128)(2,1)S(1)} %pad_maximum_fusion.8.refs_9_), channel_id=1, source_target_pairs={{0,16},{4,20},{8,24},{12,28},{16,0},{20,4},{24,8},{28,12},{1,17},{... | collective-permute-start | bytes 1769480 | tf_op jit(solution)/shard_map/ppermute | solution.py:59
  27.1 27.9 %collective-permute-start.3 = (bf16[3,24,32,128]{3,2,1,0:T(8,128)(2,1)S(1)}, bf16[3,24,32,128]{3,2,1,0:T(8,128)(2,1)}, u32[]{:S(2)}, u32[]{:S(2)}) collective-permute-start(bf16[3,24,32,128]{3,2,1,0:T(8,128)(2,1)S(1)} %pad_maximum_fusion.8.refs_9_), channel_id=1, source_target_pairs={{0,8},{4,12},{8,0},{12,4},{16,24},{20,28},{24,16},{28,20},{1,9},{5... | collective-permute-start | bytes 1769480 | tf_op jit(solution)/shard_map/ppermute | solution.py:59
  31.6 18.4 %collective-permute-start.5 = (bf16[30,32,128]{2,1,0:T(8,128)(2,1)S(1)}, bf16[30,32,128]{2,1,0:T(8,128)(2,1)S(1)}, u32[]{:S(2)}, u32[]{:S(2)}) collective-permute-start(bf16[30,32,128]{2,1,0:T(8,128)(2,1)S(1)} %copy-done.35), channel_id=1, source_target_pairs={{0,1},{1,2},{2,3},{3,0},{4,5},{5,6},{6,7},{7,4},{8,9},{9,10},{10,1... | collective-permute-start | bytes 737288 | tf_op jit(solution)/shard_map/ppermute | solution.py:68
  50.1 26.4 %collective-permute-start.16 = (bf16[3,30,32,128]{3,2,1,0:T(8,128)(2,1)S(1)}, bf16[3,30,32,128]{3,2,1,0:T(8,128)(2,1)}, u32[]{:S(2)}, u32[]{:S(2)}) collective-permute-start(bf16[3,30,32,128]{3,2,1,0:T(8,128)(2,1)S(1)} %pad_maximum_fusion.6.refs_7_), channel_id=1, source_target_pairs={{0,16},{4,20},{8,24},{12,28},{16,0},{20,4},{24,8},{28,12},{1,17},{... | collective-permute-start | bytes 2211848 | tf_op jit(solution)/shard_map/ppermute | solution.py:59
  50.4 26.7 %collective-permute-start.15 = (bf16[3,30,32,128]{3,2,1,0:T(8,128)(2,1)S(1)}, bf16[3,30,32,128]{3,2,1,0:T(8,128)(2,1)}, u32[]{:S(2)}, u32[]{:S(2)}) collective-permute-start(bf16[3,30,32,128]{3,2,1,0:T(8,128)(2,1)S(1)} %pad_maximum_fusion.6.refs_7_), channel_id=1, source_target_pairs={{0,8},{4,12},{8,0},{12,4},{16,24},{20,28},{24,16},{28,20},{1,9},{5... | collective-permute-start | bytes 2211848 | tf_op jit(solution)/shard_map/ppermute | solution.py:59
  53.7 20.4 %collective-permute-start.9 = (bf16[3,12,32,128]{3,2,1,0:T(8,128)(2,1)S(1)}, bf16[3,12,32,128]{3,2,1,0:T(8,128)(2,1)}, u32[]{:S(2)}, u32[]{:S(2)}) collective-permute-start(bf16[3,12,32,128]{3,2,1,0:T(8,128)(2,1)S(1)} %slice.222), channel_id=1, source_target_pairs={{0,8},{4,12},{8,0},{12,4},{16,24},{20,28},{24,16},{28,20},{1,9},{5... | collective-permute-start | bytes 884744 | tf_op jit(solution)/shard_map/ppermute | solution.py:59
  55.9 19.8 %collective-permute-start.8 = (bf16[3,12,32,128]{3,2,1,0:T(8,128)(2,1)S(1)}, bf16[3,12,32,128]{3,2,1,0:T(8,128)(2,1)}, u32[]{:S(2)}, u32[]{:S(2)}) collective-permute-start(bf16[3,12,32,128]{3,2,1,0:T(8,128)(2,1)S(1)} %slice.221), channel_id=1, source_target_pairs={{0,16},{4,20},{8,24},{12,28},{16,0},{20,4},{24,8},{28,12},{1,17},{... | collective-permute-start | bytes 884744 | tf_op jit(solution)/shard_map/ppermute | solution.py:59
  79.8 33.9 %collective-permute-start.21 = (bf16[44,32,128]{2,1,0:T(8,128)(2,1)S(1)}, bf16[44,32,128]{2,1,0:T(8,128)(2,1)S(1)}, u32[]{:S(2)}, u32[]{:S(2)}) collective-permute-start(bf16[44,32,128]{2,1,0:T(8,128)(2,1)S(1)} %copy-done.30), channel_id=1, source_target_pairs={{0,3},{1,0},{2,1},{3,2},{4,7},{5,4},{6,5},{7,6},{8,11},{9,8},{10,9... | collective-permute-start | bytes 1081352 | tf_op jit(solution)/shard_map/ppermute | solution.py:68
  81.7 32.0 %collective-permute-start.20 = (bf16[44,32,128]{2,1,0:T(8,128)(2,1)S(1)}, bf16[44,32,128]{2,1,0:T(8,128)(2,1)S(1)}, u32[]{:S(2)}, u32[]{:S(2)}) collective-permute-start(bf16[44,32,128]{2,1,0:T(8,128)(2,1)S(1)} %copy-done.30), channel_id=1, source_target_pairs={{0,2},{1,3},{2,0},{3,1},{4,6},{5,7},{6,4},{7,5},{8,10},{9,11},{10,... | collective-permute-start | bytes 1081352 | tf_op jit(solution)/shard_map/ppermute | solution.py:68
  83.3 30.4 %collective-permute-start.19 = (bf16[44,32,128]{2,1,0:T(8,128)(2,1)S(1)}, bf16[44,32,128]{2,1,0:T(8,128)(2,1)S(1)}, u32[]{:S(2)}, u32[]{:S(2)}) collective-permute-start(bf16[44,32,128]{2,1,0:T(8,128)(2,1)S(1)} %copy-done.30), channel_id=1, source_target_pairs={{0,1},{1,2},{2,3},{3,0},{4,5},{5,6},{6,7},{7,4},{8,9},{9,10},{10,1... | collective-permute-start | bytes 1081352 | tf_op jit(solution)/shard_map/ppermute | solution.py:68
  113.8 24.0 %collective-permute-start.28 = (bf16[3,44,32,128]{3,2,1,0:T(8,128)(2,1)S(1)}, bf16[3,44,32,128]{3,2,1,0:T(8,128)(2,1)}, u32[]{:S(2)}, u32[]{:S(2)}) collective-permute-start(bf16[3,44,32,128]{3,2,1,0:T(8,128)(2,1)S(1)} %pad_maximum_fusion.5.refs_19_), channel_id=1, source_target_pairs={{0,16},{4,20},{8,24},{12,28},{16,0},{20,4},{24,8},{28,12},{1,17},{... | collective-permute-start | bytes 3244040 | tf_op jit(solution)/shard_map/ppermute | solution.py:59
  114.2 26.0 %collective-permute-start.27 = (bf16[3,44,32,128]{3,2,1,0:T(8,128)(2,1)S(1)}, bf16[3,44,32,128]{3,2,1,0:T(8,128)(2,1)}, u32[]{:S(2)}, u32[]{:S(2)}) collective-permute-start(bf16[3,44,32,128]{3,2,1,0:T(8,128)(2,1)S(1)} %pad_maximum_fusion.5.refs_19_), channel_id=1, source_target_pairs={{0,8},{4,12},{8,0},{12,4},{16,24},{20,28},{24,16},{28,20},{1,9},{5... | collective-permute-start | bytes 3244040 | tf_op jit(solution)/shard_map/ppermute | solution.py:59
  115.4 29.3 %collective-permute-start.22 = (bf16[3,30,32,128]{3,2,1,0:T(8,128)(2,1)S(1)}, bf16[3,30,32,128]{3,2,1,0:T(8,128)(2,1)S(1)}, u32[]{:S(2)}, u32[]{:S(2)}) collective-permute-start(bf16[3,30,32,128]{3,2,1,0:T(8,128)(2,1)S(1)} %pad_maximum_fusion.6.refs_7_), channel_id=1, source_target_pairs={{0,4},{4,0},{8,12},{12,8},{16,20},{20,16},{24,28},{28,24},{1,5},{5... | collective-permute-start | bytes 2211848 | tf_op jit(solution)/shard_map/ppermute | solution.py:59
  206.7 22.3 %collective-permute-start.36 = (bf16[4,4,22,32,128]{4,3,2,1,0:T(8,128)(2,1)}, bf16[4,4,22,32,128]{4,3,2,1,0:T(8,128)(2,1)S(1)}, u32[]{:S(2)}, u32[]{:S(2)}) collective-permute-start(bf16[4,4,22,32,128]{4,3,2,1,0:T(8,128)(2,1)} %get-tuple-element.160), channel_id=1, source_target_pairs={{0,4},{4,0},{8,12},{12,8},{16,20},{20,16},{24,28},{28,24},{1,5},{5... | collective-permute-start | bytes 8650760 | tf_op jit(solution)/shard_map/ppermute | solution.py:59
  207.0 22.0 %collective-permute-start.37 = (bf16[4,4,22,32,128]{4,3,2,1,0:T(8,128)(2,1)}, bf16[4,4,22,32,128]{4,3,2,1,0:T(8,128)(2,1)S(1)}, u32[]{:S(2)}, u32[]{:S(2)}) collective-permute-start(bf16[4,4,22,32,128]{4,3,2,1,0:T(8,128)(2,1)} %get-tuple-element.161), channel_id=1, source_target_pairs={{0,4},{4,0},{8,12},{12,8},{16,20},{20,16},{24,28},{28,24},{1,5},{5... | collective-permute-start | bytes 8650760 | tf_op jit(solution)/shard_map/ppermute | solution.py:59
  207.3 21.7 %collective-permute-start.38 = (bf16[88,4,32,128]{3,2,1,0:T(8,128)(2,1)}, bf16[88,4,32,128]{3,2,1,0:T(8,128)(2,1)}, u32[]{:S(2)}, u32[]{:S(2)}) collective-permute-start(bf16[88,4,32,128]{3,2,1,0:T(8,128)(2,1)} %get-tuple-element.162), channel_id=1, source_target_pairs={{0,4},{4,0},{8,12},{12,8},{16,20},{20,16},{24,28},{28,24},{1,5},{5... | collective-permute-start | bytes 8650760 | tf_op jit(solution)/shard_map/ppermute | solution.py:59
  249.1 49.3 %collective-permute-start.39 = (bf16[2,132,32,128]{3,2,1,0:T(8,128)(2,1)}, bf16[2,132,32,128]{3,2,1,0:T(8,128)(2,1)}, u32[]{:S(2)}, u32[]{:S(2)}) collective-permute-start(bf16[2,132,32,128]{3,2,1,0:T(8,128)(2,1)} %get-tuple-element.166), channel_id=1, source_target_pairs={{0,8},{4,12},{8,0},{12,4},{16,24},{20,28},{24,16},{28,20},{1,9},{5... | collective-permute-start | bytes 6488072 | tf_op jit(solution)/shard_map/ppermute | solution.py:59
  249.8 48.6 %collective-permute-start.40 = (bf16[2,132,32,128]{3,2,1,0:T(8,128)(2,1)}, bf16[2,132,32,128]{3,2,1,0:T(8,128)(2,1)}, u32[]{:S(2)}, u32[]{:S(2)}) collective-permute-start(bf16[2,132,32,128]{3,2,1,0:T(8,128)(2,1)} %get-tuple-element.177), channel_id=1, source_target_pairs={{0,16},{4,20},{8,24},{12,28},{16,0},{20,4},{24,8},{28,12},{1,17},{... | collective-permute-start | bytes 6488072 | tf_op jit(solution)/shard_map/ppermute | solution.py:59
  301.1 28.5 %collective-permute-start.59 = (bf16[132,32,128]{2,1,0:T(8,128)(2,1)}, bf16[132,32,128]{2,1,0:T(8,128)(2,1)S(1)}, u32[]{:S(2)}, u32[]{:S(2)}) collective-permute-start(bf16[132,32,128]{2,1,0:T(8,128)(2,1)} %fusion.3), channel_id=1, source_target_pairs={{0,8},{4,12},{8,0},{12,4},{16,24},{20,28},{24,16},{28,20},{1,9},{5... | collective-permute-start | bytes 3244040 | tf_op jit(solution)/shard_map/ppermute | solution.py:59
  304.1 25.4 %collective-permute-start.58 = (bf16[132,32,128]{2,1,0:T(8,128)(2,1)}, bf16[132,32,128]{2,1,0:T(8,128)(2,1)}, u32[]{:S(2)}, u32[]{:S(2)}) collective-permute-start(bf16[132,32,128]{2,1,0:T(8,128)(2,1)} %fusion.2), channel_id=1, source_target_pairs={{0,16},{4,20},{8,24},{12,28},{16,0},{20,4},{24,8},{28,12},{1,17},{... | collective-permute-start | bytes 3244040 | tf_op jit(solution)/shard_map/ppermute | solution.py:59
  313.7 28.6 %collective-permute-start.41 = (bf16[4,4,32,32,128]{4,3,2,1,0:T(8,128)(2,1)}, bf16[4,4,32,32,128]{4,3,2,1,0:T(8,128)(2,1)}, u32[]{:S(2)}, u32[]{:S(2)}) collective-permute-start(bf16[4,4,32,32,128]{4,3,2,1,0:T(8,128)(2,1)} %square_send.1), channel_id=1, source_target_pairs={{0,4},{4,0},{8,12},{12,8},{16,20},{20,16},{24,28},{28,24},{1,5},{5... | collective-permute-start | bytes 12582920 | tf_op jit(solution)/shard_map/ppermute | solution.py:59
  336.9 39.3 %collective-permute-start.62 = (bf16[67,32,128]{2,1,0:T(8,128)(2,1)}, bf16[67,32,128]{2,1,0:T(8,128)(2,1)}, u32[]{:S(2)}, u32[]{:S(2)}) collective-permute-start(bf16[67,32,128]{2,1,0:T(8,128)(2,1)} %get-tuple-element.230), channel_id=1, source_target_pairs={{0,3},{1,0},{2,1},{3,2},{4,7},{5,4},{6,5},{7,6},{8,11},{9,8},{10,9... | collective-permute-start | bytes 1646600 | tf_op jit(solution)/shard_map/ppermute | solution.py:68
  338.5 37.8 %collective-permute-start.60 = (bf16[67,32,128]{2,1,0:T(8,128)(2,1)}, bf16[67,32,128]{2,1,0:T(8,128)(2,1)}, u32[]{:S(2)}, u32[]{:S(2)}) collective-permute-start(bf16[67,32,128]{2,1,0:T(8,128)(2,1)} %get-tuple-element.231), channel_id=1, source_target_pairs={{0,1},{1,2},{2,3},{3,0},{4,5},{5,6},{6,7},{7,4},{8,9},{9,10},{10,1... | collective-permute-start | bytes 1646600 | tf_op jit(solution)/shard_map/ppermute | solution.py:68
  338.7 46.3 %collective-permute-start.61 = (bf16[67,32,128]{2,1,0:T(8,128)(2,1)S(1)}, bf16[67,32,128]{2,1,0:T(8,128)(2,1)}, u32[]{:S(2)}, u32[]{:S(2)}) collective-permute-start(bf16[67,32,128]{2,1,0:T(8,128)(2,1)S(1)} %get-tuple-element.232), channel_id=1, source_target_pairs={{0,2},{1,3},{2,0},{3,1},{4,6},{5,7},{6,4},{7,5},{8,10},{9,11},{10,... | collective-permute-start | bytes 1646600 | tf_op jit(solution)/shard_map/ppermute | solution.py:68
  352.7 23.2 %collective-permute-start.42 = (bf16[2,64,32,128]{3,2,1,0:T(8,128)(2,1)}, bf16[2,64,32,128]{3,2,1,0:T(8,128)(2,1)S(1)}, u32[]{:S(2)}, u32[]{:S(2)}) collective-permute-start(bf16[2,64,32,128]{3,2,1,0:T(8,128)(2,1)} %get-tuple-element.191), channel_id=1, source_target_pairs={{0,8},{4,12},{8,0},{12,4},{16,24},{20,28},{24,16},{28,20},{1,9},{5... | collective-permute-start | bytes 3145736 | tf_op jit(solution)/shard_map/ppermute | solution.py:59
  353.4 22.5 %collective-permute-start.43 = (bf16[2,64,32,128]{3,2,1,0:T(8,128)(2,1)}, bf16[2,64,32,128]{3,2,1,0:T(8,128)(2,1)S(1)}, u32[]{:S(2)}, u32[]{:S(2)}) collective-permute-start(bf16[2,64,32,128]{3,2,1,0:T(8,128)(2,1)} %get-tuple-element.196), channel_id=1, source_target_pairs={{0,16},{4,20},{8,24},{12,28},{16,0},{20,4},{24,8},{28,12},{1,17},{... | collective-permute-start | bytes 3145736 | tf_op jit(solution)/shard_map/ppermute | solution.py:59
  390.9 23.2 %collective-permute-start.64 = (bf16[1,67,32,128]{3,2,1,0:T(8,128)(2,1)S(1)}, bf16[1,67,32,128]{3,2,1,0:T(8,128)(2,1)S(1)}, u32[]{:S(2)}, u32[]{:S(2)}) collective-permute-start(bf16[1,67,32,128]{3,2,1,0:T(8,128)(2,1)S(1)} %maximum_bitcast_fusion.refs_1_), channel_id=1, source_target_pairs={{0,16},{4,20},{8,24},{12,28},{16,0},{20,4},{24,8},{28,12},{1,17},{... | collective-permute-start | bytes 1646600 | tf_op jit(solution)/shard_map/ppermute | solution.py:59
  392.3 21.9 %collective-permute-start.63 = (bf16[1,67,32,128]{3,2,1,0:T(8,128)(2,1)S(1)}, bf16[1,67,32,128]{3,2,1,0:T(8,128)(2,1)S(1)}, u32[]{:S(2)}, u32[]{:S(2)}) collective-permute-start(bf16[1,67,32,128]{3,2,1,0:T(8,128)(2,1)S(1)} %maximum_bitcast_fusion.refs_1_), channel_id=1, source_target_pairs={{0,8},{4,12},{8,0},{12,4},{16,24},{20,28},{24,16},{28,20},{1,9},{5... | collective-permute-start | bytes 1646600 | tf_op jit(solution)/shard_map/ppermute | solution.py:59
  402.7 21.1 %collective-permute-start.47 = (bf16[32,32,128]{2,1,0:T(8,128)(2,1)S(1)}, bf16[32,32,128]{2,1,0:T(8,128)(2,1)S(1)}, u32[]{:S(2)}, u32[]{:S(2)}) collective-permute-start(bf16[32,32,128]{2,1,0:T(8,128)(2,1)S(1)} %get-tuple-element.228), channel_id=1, source_target_pairs={{0,2},{1,3},{2,0},{3,1},{4,6},{5,7},{6,4},{7,5},{8,10},{9,11},{10,... | collective-permute-start | bytes 786440 | tf_op jit(solution)/shard_map/ppermute | solution.py:68
  406.0 23.6 %collective-permute-start.48 = (bf16[32,32,128]{2,1,0:T(8,128)(2,1)S(1)}, bf16[32,32,128]{2,1,0:T(8,128)(2,1)S(1)}, u32[]{:S(2)}, u32[]{:S(2)}) collective-permute-start(bf16[32,32,128]{2,1,0:T(8,128)(2,1)S(1)} %get-tuple-element.229), channel_id=1, source_target_pairs={{0,3},{1,0},{2,1},{3,2},{4,7},{5,4},{6,5},{7,6},{8,11},{9,8},{10,9... | collective-permute-start | bytes 786440 | tf_op jit(solution)/shard_map/ppermute | solution.py:68
  414.4 26.2 %collective-permute-start.67 = (bf16[1,67,32,128]{3,2,1,0:T(8,128)(2,1)S(1)}, bf16[1,67,32,128]{3,2,1,0:T(8,128)(2,1)S(1)}, u32[]{:S(2)}, u32[]{:S(2)}) collective-permute-start(bf16[1,67,32,128]{3,2,1,0:T(8,128)(2,1)S(1)} %maximum_bitcast_fusion.refs_1_), channel_id=1, source_target_pairs={{0,4},{4,0},{8,12},{12,8},{16,20},{20,16},{24,28},{28,24},{1,5},{5... | collective-permute-start | bytes 1646600 | tf_op jit(solution)/shard_map/ppermute | solution.py:59
  423.8 18.7 %collective-permute-start.69 = (bf16[1,67,32,128]{3,2,1,0:T(8,128)(2,1)S(1)}, bf16[1,67,32,128]{3,2,1,0:T(8,128)(2,1)S(1)}, u32[]{:S(2)}, u32[]{:S(2)}) collective-permute-start(bf16[1,67,32,128]{3,2,1,0:T(8,128)(2,1)S(1)} %collective-permute-done.64.refs_3_), channel_id=1, source_target_pairs={{0,4},{4,0},{8,12},{12,8},{16,20},{20,16},{24,28},{28,24},{1,5},{5... | collective-permute-start | bytes 1646600 | tf_op jit(solution)/shard_map/ppermute | solution.py:59
  (100 other events, 1128.1 us)

commit v3 on v2

--- a/solution.py
+++ b/solution.py
@@ -294,44 +294,60 @@
     return (lane < 64) if which == 0 else (lane >= 64)
 
 
-def pick(x, which):
-    return jnp.where(half_mask(x.shape[0], which), x, jnp.zeros_like(x))
-
-
-def attend_fwd_body(q_ref, k_ref, v_ref, end_ref, keep_ref, *rest):
-    o_ref, lse_ref, bias = rest[-3:]
+def pick(x, which, other=None):
+    return jnp.where(half_mask(x.shape[0], which), x, jnp.zeros_like(x) if other is None else other)
+
+
+def marks(seg, docs):
+    lane = jnp.arange(128, dtype=jnp.int32)[None, :] % 64
+    same = lane == seg[:, None]
+    return jnp.where((lane < docs) & ~same, NEG, 0.0).astype(bf16), same.astype(bf16)
+
+
+def key_blocks(length):
+    return length // 2 // QB + 1
+
+
+def attend_fwd_body(q_ref, k_ref, v_ref, qm_ref, km_ref, keep_ref, *rest):
+    o_ref, lse_ref = rest[-2:]
     pair = pl.program_id(0)
     length = q_ref.shape[0]
     blocks = length // QB
-
-    @pl.when(pair == 0)
-    def _():
-        for i in range(blocks):
-            size = (i + 1) * QB
-            q_at = lax.broadcasted_iota(jnp.int32, (QB, size), 0) + i * QB
-            k_at = lax.broadcasted_iota(jnp.int32, (QB, size), 1)
-            ok = (q_at >= k_at) & (q_at < end_ref[:, :size])
-            bias[i * QB : (i + 1) * QB, :size] = jnp.where(ok, 0.0, NEG)
-
+    most = key_blocks(length)
+    row, col = [lax.broadcasted_iota(jnp.int32, (QB, QB), a) for a in (0, 1)]
+    causal = jnp.where(row >= col, 0.0, NEG)
+    keys = [pick(k_ref[...], h, km_ref[...]) for h in range(2)]
     lane = lax.broadcasted_iota(jnp.int32, (QB, 128), 1)
-    for i in range(blocks):
+
+    work = [(i, h) for i in range(blocks) for h in range(2)]
+
+    def span(i):
+        return slice(max(0, i + 1 - most) * QB, (i + 1) * QB)
+
+    def scores(i, h):
         rows = slice(i * QB, (i + 1) * QB)
-        size = (i + 1) * QB
-        outs = []
-        old = lse_ref[rows, :]
-        for h in range(2):
-            s = nt(pick(q_ref[rows, :], h), k_ref[:size, :]) + bias[rows, :size]
-            top = jnp.max(s, -1, keepdims=True)
-            expo = jnp.exp(s - top)
-            total = jnp.sum(expo, -1, keepdims=True)
-            outs.append(nn(expo.astype(bf16), v_ref[:size, :]) / total)
-            old = jnp.where(lane == 2 * pair + h, top + jnp.log(total), old)
-        lse_ref[rows, :] = old
-        o = jnp.where(lane < 64, outs[0], outs[1]) * keep_ref[rows, :]
-        o_ref[rows, :] = o.astype(bf16)
-
-
-def attend_fwd(q, k, v, end_row, keep_col, first, pairs, before=None):
+        return nt(pick(q_ref[rows, :], h, qm_ref[rows, :]), keys[h][span(i), :])
+
+    ahead = scores(*work[0])
+    outs, stats = {}, {}
+    for at, (i, h) in enumerate(work):
+        rows = slice(i * QB, (i + 1) * QB)
+        s = ahead + causal if i == 0 else jnp.concatenate([ahead[:, :-QB], ahead[:, -QB:] + causal], 1)
+        if at + 1 < len(work):
+            ahead = scores(*work[at + 1])
+        top = jnp.max(s, -1, keepdims=True)
+        expo = jnp.exp(s - top)
+        total = jnp.sum(expo, -1, keepdims=True)
+        outs[h] = nn(expo.astype(bf16), v_ref[span(i), :]) / total
+        stats[h] = top + jnp.log(total)
+        if h == 1:
+            old = jnp.where(lane == 2 * pair, stats[0], lse_ref[rows, :])
+            lse_ref[rows, :] = jnp.where(lane == 2 * pair + 1, stats[1], old)
+            o = jnp.where(lane < 64, outs[0], outs[1]) * keep_ref[rows, :]
+            o_ref[rows, :] = o.astype(bf16)
+
+
+def attend_fwd(q, k, v, q_mark, k_mark, keep_col, first, pairs, before=None):
     length, width = q.shape
     col = pl.BlockSpec((length, 128), lambda p: (0, p + first))
     return pl.pallas_call(
@@ -341,7 +357,8 @@
             col,
             col,
             col,
-            pl.BlockSpec((1, length), lambda p: (0, 0)),
+            pl.BlockSpec((length, 128), lambda p: (0, 0)),
+            pl.BlockSpec((length, 128), lambda p: (0, 0)),
             pl.BlockSpec((length, 1), lambda p: (0, 0)),
         ]
         + ([] if before is None else [ANY]),
@@ -350,60 +367,59 @@
             jax.ShapeDtypeStruct((length, width), bf16),
             jax.ShapeDtypeStruct((length, 128), f32),
         ],
-        scratch_shapes=[pltpu.VMEM((length, length), f32)],
         compiler_params=params(),
         cost_estimate=cost(4.2 * pairs),
-        input_output_aliases={} if before is None else {5: 0},
+        input_output_aliases={} if before is None else {6: 0},
         name="attend_fwd",
-    )(q, k, v, end_row, keep_col, *([] if before is None else [before]))
+    )(q, k, v, q_mark, k_mark, keep_col, *([] if before is None else [before]))
 
 
 def attend_bwd_body(
-    q_ref, k_ref, v_ref, do_ref, lse_ref, first_ref, cos_ref, sin_ref, fg_ref, *rest,
+    q_ref, k_ref, v_ref, do_ref, lse_ref, qm_ref, km_ref, cos_ref, sin_ref, fg_ref, *rest,
 ):
-    dq_ref, dk_ref, dv_ref, fo_ref, bias, dk_acc, dv_acc = rest[-7:]
+    dq_ref, dk_ref, dv_ref, fo_ref, dk_acc, dv_acc = rest[-6:]
     pair = pl.program_id(0)
     length = q_ref.shape[0]
     blocks = length // QB
-
-    @pl.when(pair == 0)
-    def _():
-        for i in range(blocks):
-            size = (i + 1) * QB
-            k_at = lax.broadcasted_iota(jnp.int32, (size, QB), 0)
-            q_at = lax.broadcasted_iota(jnp.int32, (size, QB), 1) + i * QB
-            ok = (q_at >= k_at) & (k_at >= first_ref[:, i * QB : (i + 1) * QB])
-            bias[:size, i * QB : (i + 1) * QB] = jnp.where(ok, 0.0, NEG)
-
+    most = key_blocks(length)
+    row, col = [lax.broadcasted_iota(jnp.int32, (QB, QB), a) for a in (0, 1)]
+    causal = jnp.where(row <= col, 0.0, NEG)
+    marked = [pick(k_ref[...], h, km_ref[...]) for h in range(2)]
     k_t = k_ref[...].astype(f32).T.astype(bf16)
-    for i in reversed(range(blocks)):
+    dk_acc[...] = jnp.zeros_like(dk_acc)
+    dv_acc[...] = jnp.zeros_like(dv_acc)
+
+    work = [(i, h) for i in reversed(range(blocks)) for h in range(2)]
+
+    def products(i, h):
         rows = slice(i * QB, (i + 1) * QB)
-        size = (i + 1) * QB
-        part_k = None
-        part_v = None
-        part_q = []
-        for h in range(2):
-            qh = pick(q_ref[rows, :], h)
-            dh = pick(do_ref[rows, :], h)
-            lse = lse_ref[pl.ds(2 * pair + h, 1), rows]
-            p = jnp.exp(nt(k_ref[:size, :], qh) + bias[:size, rows] - lse)
-            dp = nt(v_ref[:size, :], dh)
-            delta = jnp.sum(p * dp, 0, keepdims=True)
-            ds = (p * (dp - delta)).astype(bf16)
-            av = nn(p.astype(bf16), dh)
-            ak = nn(ds, qh)
-            part_v = av if part_v is None else part_v + av
-            part_k = ak if part_k is None else part_k + ak
-            part_q.append(nn(k_t[h * 64 : (h + 1) * 64, :size], ds))
-        if i == blocks - 1:
-            dk_acc[...] = part_k
-            dv_acc[...] = part_v
-        else:
-            dk_acc[:size, :] += part_k
-            dv_acc[:size, :] += part_v
-        dq = jnp.concatenate(part_q, 0).T * 0.125
-        dq = dq * cos_ref[rows, :] + swap_halves(dq) * sin_ref[rows, :]
-        dq_ref[rows, :] = dq.astype(bf16)
+        keys = slice(max(0, i + 1 - most) * QB, (i + 1) * QB)
+        qh = pick(q_ref[rows, :], h)
+        dh = pick(do_ref[rows, :], h)
+        qm = pick(q_ref[rows, :], h, qm_ref[rows, :])
+        return qh, dh, nt(marked[h][keys, :], qm), nt(v_ref[keys, :], dh)
+
+    ahead = products(*work[0])
+    part_q = []
+    for at, (i, h) in enumerate(work):
+        rows = slice(i * QB, (i + 1) * QB)
+        keys = slice(max(0, i + 1 - most) * QB, (i + 1) * QB)
+        qh, dh, s, dp = ahead
+        if at + 1 < len(work):
+            ahead = products(*work[at + 1])
+        lse = lse_ref[pl.ds(2 * pair + h, 1), rows]
+        s = s + causal if i == 0 else jnp.concatenate([s[:-QB], s[-QB:] + causal], 0)
+        p = jnp.exp(s - lse)
+        delta = jnp.sum(p * dp, 0, keepdims=True)
+        ds = (p * (dp - delta)).astype(bf16)
+        dv_acc[keys, :] += nn(p.astype(bf16), dh)
+        dk_acc[keys, :] += nn(ds, qh)
+        part_q.append(nn(k_t[h * 64 : (h + 1) * 64, keys], ds))
+        if h == 1:
+            dq = jnp.concatenate(part_q, 0).T * 0.125
+            part_q = []
+            dq = dq * cos_ref[rows, :] + swap_halves(dq) * sin_ref[rows, :]
+            dq_ref[rows, :] = dq.astype(bf16)
     dk = dk_acc[...]
     dk_ref[...] = (dk * cos_ref[...] + swap_halves(dk) * sin_ref[...]).astype(bf16)
     dv = dv_acc[...].astype(bf16).astype(f32) * 0.5
@@ -411,7 +427,7 @@
     fo_ref[...] = fg_ref[...] + dv
 
 
-def attend_bwd(q, k, v, do, lse_t, first_row, cos_w, sin_back, fgrad, first, pairs, before=None):
+def attend_bwd(q, k, v, do, lse_t, q_mark, k_mark, cos_w, sin_back, fgrad, first, pairs, before=None):
     length, width = q.shape
     col = pl.BlockSpec((length, 128), lambda p: (0, p + first))
     before = [] if before is None else list(before)
@@ -423,20 +439,19 @@
     return pl.pallas_call(
         attend_bwd_body,
         grid=(pairs,),
-        in_specs=[col] * 4 + [whole(lse_t), whole(first_row), whole(cos_w), whole(sin_back), col]
+        in_specs=[col] * 4 + [whole(lse_t), whole(q_mark), whole(k_mark), whole(cos_w), whole(sin_back), col]
         + [ANY] * len(before),
         out_specs=[col] * 4,
         out_shape=[wide, wide, wide, jax.ShapeDtypeStruct((length, width), f32)],
         scratch_shapes=[
-            pltpu.VMEM((length, length), f32),
             pltpu.VMEM((length, 128), f32),
             pltpu.VMEM((length, 128), f32),
         ],
         compiler_params=params(),
         cost_estimate=cost(5.5 * pairs),
-        input_output_aliases={9 + i: i for i in range(len(before))},
+        input_output_aliases={10 + i: i for i in range(len(before))},
         name="attend_bwd",
-    )(q, k, v, do, lse_t, first_row, cos_w, sin_back, fgrad, *before)
+    )(q, k, v, do, lse_t, q_mark, k_mark, cos_w, sin_back, fgrad, *before)
 
 
 def chosen_columns(ref, parity):
@@ -960,6 +975,7 @@
         out_shape=outs,
         scratch_shapes=[] if tall is None else [pltpu.VMEM((8, G, L), f32)],
         compiler_params=params(),
+        cost_estimate=cost(5),
         name="place",
     )(pos, *arrays)
 
@@ -970,7 +986,6 @@
     seg = jnp.sum((position[:, None] >= ends[None, :]).astype(jnp.int32), 1)
     onehot = seg[:, None] == jnp.arange(lengths.shape[0], dtype=jnp.int32)[None, :]
     first = jnp.sum(jnp.where(onehot, (ends - lengths)[None, :], 0), 1)
-    last = jnp.sum(jnp.where(onehot, ends[None, :], 0), 1)
     rel = (position - first).astype(f32)
     inverse = 10000.0 ** (-jnp.arange(HEAD_DIM // 2, dtype=f32) * 2.0 / HEAD_DIM)
     angle = rel[:, None] * inverse[None, :]
@@ -978,7 +993,7 @@
     cos, sin = jnp.cos(angle), jnp.sin(angle)
     cos_w = jnp.concatenate([cos] * 4, 1)
     sin_w = jnp.concatenate([-sin, sin] * 2, 1)
-    return cos_w, sin_w, first[None, :], last[None, :], keep[:, None]
+    return cos_w, sin_w, marks(seg, lengths.shape[0]), keep[:, None]
 
 
 def add(*terms):
@@ -1073,8 +1088,8 @@
         mines = [cut(after(pos, g1.extras[0]), *m) for m in members[1:]]
         g1.near()
         g2 = Gather(after(mines[0], g1.start))
-        g1.corner(*g2.far)
-        g2.near()
+        g1.corner(g2.far[0], g2.far[2])
+        g2.near(g1.c1, g1.c2)
         g3 = Gather(after(mines[1], g2.start))
         g1.core()
         g1.core_corner()
@@ -1096,7 +1111,7 @@
         ]
     whole_gains = whole_gains.astype(f32)
     gain_1, gain_2 = whole_gains[:1], whole_gains[1:]
-    cos_w, sin_w, first_row, last_row, keep_col = layout(doc_lengths[0], length)
+    cos_w, sin_w, mark, keep_col = layout(doc_lengths[0], length)
 
     q, k, vm, h1t, sums, wq, wk, wv = qkv(pos, x, v1, gain_1, cos_w, sin_w, groups[0])
     squares = jnp.sum(sums, (1, 2))
@@ -1104,12 +1119,12 @@
     if fast:
         g2.corner(q)
         q = after(q, g2.x, g2.y)
-    o, lse_1 = attend_fwd(q, k, vm, last_row, keep_col, 0, 3)
+    o, lse_1 = attend_fwd(q, k, vm, *mark, keep_col, 0, 3)
     if fast:
         g3.near(o)
         g2.core(o)
         o = after(o, g2.c1, g2.c2, g3.start)
-    o, lse_2 = attend_fwd(q, k, vm, last_row, keep_col, 3, 5, o)
+    o, lse_2 = attend_fwd(q, k, vm, *mark, keep_col, 3, 5, o)
     if fast:
         g3.corner(o)
         g2.core_corner(o)
@@ -1118,55 +1133,59 @@
         groups += [Group(members[i][1], members[i][0], g.arrays(), False) for i, g in ((1, g2), (2, g3))]
     hid, dgate, dup, sg, su, sd, r1, h2t, ot, wo, wg, wu, wd = ffn(pos, x, o, df, gain_2, groups[1:], hidden)
     got = [dp_swap(g, 1) if fast else jnp.zeros_like(g) for g in (sg, su, sd)]
-    dr1, da, do = ffn_back(r1, df, keep_col, gain_2, dgate, dup, wo, wg, wu)
-    ka, ta, kb, tb = ffn_grads(pos, h2t, df, hid, dgate, dup, after(got, da))
+    out = ffn_out(r1, hid, wd)
+    ka, ta, kb, tb = ffn_grads(pos, h2t, df, hid, dgate, dup, after(got, out))
     if fast:
         na, nb = dp_swap(ta, 2), dp_swap(tb, 4)
-    back = (first_row, cos_w, -sin_w, first_values_grad[0])
-    results = attend_bwd(q, k, vm, after(do, ta), lse_1.T, *back, 0, 3)
-    dq, dk, dv, first_out = attend_bwd(q, k, vm, do, lse_2.T, *back, 3, 5, results)
-    grads = (da, dq, dk, dv)
+        dgate = after(dgate, ta)
+    dr1, da, do = ffn_back(r1, df, keep_col, gain_2, dgate, dup, wo, wg, wu)
+    back = (*mark, cos_w, -sin_w, first_values_grad[0])
+    results = attend_bwd(q, k, vm, do, lse_2.T, *back, 3, 5)
     if fast:
-        na, nb = after((na, nb), dq)
+        na, nb = after((na, nb), results)
         ta, ka = halve(ka, na, b2)
         tb, kb = halve(kb, nb, b1)
         ma, mb = dp_swap(ta, 4), dp_swap(tb, 2)
-        grads = after(grads, ta, tb)
+        results = after(results, ta, tb)
+    dq, dk, dv, first_out = attend_bwd(q, k, vm, do, lse_1.T, *back, 0, 3, results)
+    grads = (da, dq, dk, dv)
+    if fast:
+        grads = after(grads, ma, mb)
     send = square_grads(pos, ot, h1t, grads, None)
     swapped = dp_swap(send, 1) if fast else jnp.zeros_like(send)
-    d_x = input_grad(after(x, send), gain_1, dr1, dq, dk, dv, (wq, wk, wv))
-    swapped = after(swapped, d_x)
     if fast:
-        ma, mb = after((ma, mb), d_x)
+        ma, mb = after((ma, mb), send)
         total_a, total_b = add(ka, ma).astype(bf16), add(kb, mb).astype(bf16)
         n = 4 * hidden // L
         cols_a, cols_b = [t[:n].reshape(4, n // 4, G, L) for t in (total_a, total_b)]
         cols_d = jnp.concatenate([total_a[n:], total_b[n:]]).reshape(4, n // 4, G, L)
         wide_terms = to_shards(jnp.concatenate([cols_a, cols_b, cols_d], 1), z, in_parts(squares))
+        swapped = after(swapped, wide_terms[0])
     ks, ts, kt, tt = square_grads(pos, ot, h1t, grads, swapped)
     if fast:
         ns, n_t = dp_swap(ts, 2), dp_swap(tt, 4)
-    out = ffn_out(r1, after(hid, ts), wd)
+    d_x = input_grad(after(x, ts), gain_1, dr1, dq, dk, dv, (wq, wk, wv))
     if fast:
-        ns, n_t = after((ns, n_t), out)
+        ns, n_t = after((ns, n_t), d_x)
         ts, ks = halve(ks, ns, b2)
         tt, kt = halve(kt, n_t, b1)
         ms, mt = dp_swap(ts, 4), dp_swap(tt, 2)
-        wide_terms = after(wide_terms, ts, tt)
-        reduced = add(*[t[:-1] for t in wide_terms]).astype(bf16)
-        wide = back_over_dp(jnp.concatenate([reduced, in_parts(sums_over_fsdp(wide_terms, z))[None]]))
+        ms, mt, wide_terms = after((ms, mt, wide_terms), ts)
         total_s, total_t = add(ks, ms).astype(bf16), add(kt, mt).astype(bf16)
         both = [t.reshape((4, -1) + t.shape[1:]) for t in (total_s, total_t)]
         last_terms = to_shards(jnp.concatenate(both, 1), z)
-        wide.corner(*both)
+        wide_terms = after(wide_terms, *both)
+        reduced = add(*[t[:-1] for t in wide_terms]).astype(bf16)
+        wide = back_over_dp(jnp.concatenate([reduced, in_parts(sums_over_fsdp(wide_terms, z))[None]]))
+        wide.corner()
+        last = back_over_dp(after(add(*last_terms).astype(bf16), wide.c1, wide.c2))
         wide.core()
         wide.core_corner()
+        last.corner(*wide.other)
         grad_wg, grad_wu, grad_wd, squares = place(
             pos, wide.arrays(), [hidden] * 2, w_query.shape[0], (w_down.shape[0], width)
         )
         squares = from_parts(squares)
-        last = back_over_dp(add(*last_terms).astype(bf16))
-        last.corner()
         last.core()
         last.core_corner()
         grad_wo, grad_wq, grad_wk, grad_wv = place(pos, last.arrays(), [width] * 4, w_query.shape[0])

time: 471 us -> 439 us (0.932)
  Pallas kernels: 241 us -> 221 us
  local copies, waits for them, and re-layouts: 25.7 us -> 19 us
    ppermute x15, waiting for transfers between devices: 38.8 us -> 23.1 us  [fsdp_shift(): lax.ppermute(x, 'fsdp', [(i, (i + step) % size) for i in range(size)])]
    ppermute x57, waiting for transfers between devices: 48.1 us -> 61.4 us  [dp_swap(): lax.ppermute(x, 'dp', [(i, i ^ bit) for i in range(lax.axis_size('dp'))])]
    pallas_call x2, Pallas kernels: 47.6 us -> 37.3 us  [attend_bwd(): pl.pallas_call(attend_bwd_body, grid=(pairs,), in_specs=[col] * 4 + [whol...]
    pallas_call x2, Pallas kernels: 32.6 us -> 23 us  [attend_fwd(): pl.pallas_call(attend_fwd_body, grid=(pairs,), in_specs=[col, col, col, p...]
  transfers between devices with their start and end apart: 72 -> 72, of which waited for: 18 -> 26; matrix products, arithmetic and copies ran while one was open for 8% -> 7% of each run, Pallas kernels for 37% -> 33%
where the time goes in v3:
time: 439 us; the launch traced here: 434 us
  Pallas kernels  221 us (50%)
  waiting for transfers between devices  84.5 us (19%)
  starting transfers between devices  78.6 us (18%)
  other arithmetic  28.7 us (7%)
  local copies, waits for them, and re-layouts  19 us (4%)
    ppermute x57, waiting for transfers between devices, dp_swap(): lax.ppermute(x, 'dp', [(i, i ^ bit) for i in range(lax.axis_size('dp'))])  61.4 us
    ppermute x57, starting transfers between devices, dp_swap(): lax.ppermute(x, 'dp', [(i, i ^ bit) for i in range(lax.axis_size('dp'))])  56.8 us
    pallas_call x1, Pallas kernels, ffn(): pl.pallas_call(lambda *refs: ffn_body(groups, *refs), grid=(1 + tiles,),...  45.9 us
    pallas_call x2, Pallas kernels, attend_bwd(): pl.pallas_call(attend_bwd_body, grid=(pairs,), in_specs=[col] * 4 + [whol...  37.3 us
    ppermute x15, waiting for transfers between devices, fsdp_shift(): lax.ppermute(x, 'fsdp', [(i, (i + step) % size) for i in range(size)])  23.1 us
    pallas_call x2, Pallas kernels, attend_fwd(): pl.pallas_call(attend_fwd_body, grid=(pairs,), in_specs=[col, col, col, p...  23 us
    ppermute x15, starting transfers between devices, fsdp_shift(): lax.ppermute(x, 'fsdp', [(i, (i + step) % size) for i in range(size)])  21.8 us
    pallas_call x1, Pallas kernels, ffn_back(): pl.pallas_call(ffn_back_body, in_specs=[vmem, vmem] + [ANY] * 7, out_spec...  21.7 us
  transfers between devices with their start and end apart: 72, of which 26 were waited for; matrix products, arithmetic and copies ran while one was open for 7% of the time, Pallas kernels for 33%

profile of v3, /device:TPU:9, one launch (start us, length us, event | category | flops | bytes accessed | tf_op | source)
XLA Modules:
  0.0 433.8 jit_solution(9920568928281417714)
XLA Ops:
  16.6 4.6 %collective-permute-done.1 = bf16[25,32,128]{2,1,0:T(8,128)(2,1)S(1)} collective-permute-done((bf16[25,32,128]{2,1,0:T(8,128)(2,1)}, bf16[25,32,128]{2,1,0:T(8,128)(2,1)S(1)}, u32[]{:S(2)}, u32[]{:S(2)}) %collective-permute-start.1) | collective-permute-done | bytes 204832 | tf_op jit(solution)/shard_map/ppermute | solution.py:68
  21.2 4.4 %collective-permute-done = bf16[25,32,128]{2,1,0:T(8,128)(2,1)S(1)} collective-permute-done((bf16[25,32,128]{2,1,0:T(8,128)(2,1)}, bf16[25,32,128]{2,1,0:T(8,128)(2,1)S(1)}, u32[]{:S(2)}, u32[]{:S(2)}) %collective-permute-start) | collective-permute-done | bytes 204832 | tf_op jit(solution)/shard_map/ppermute | solution.py:68
  42.6 2.9 collective-permute-start.14
  48.7 3.2 collective-permute-done.8.refs_13_
  54.7 3.8 collective-permute-start.13
  64.1 14.6 %qkv.1 = (bf16[1024,1024]{1,0:T(8,128)(2,1)}, bf16[1024,1024]{1,0:T(8,128)(2,1)}, bf16[1024,1024]{1,0:T(8,128)(2,1)}, bf16[16,2,32,1024]{3,2,1,0:T(8,128)(2,1)},...) custom-call(s32[2]{0:T(128)} %pad_add_fusion.refs_0_.pos, ...), custom_call_target="tpu_custom_call" | custom-call | flops 60000002048 | tf_op jit(solution)/shard_map/qkv/pallas_call | solution.py:279
  81.9 9.5 %attend_fwd.2 = (bf16[1024,1024]{1,0:T(8,128)(2,1)}, f32[1024,128]{1,0:T(8,128)}) custom-call(bf16[1024,1024]{1,0:T(8,128)(2,1)} %get-tuple-element.135.q_ref, bf16[1024,1024]{1,0:T(8,128)(2,1)} %get-tuple-element.136.k_ref, bf16[1024,1024]{1,0:T(8,128)(2,1)} %get-tuple-element.137.v_ref, bf16[1024,128]{1,0:T(8,128)(2,1)} %select_convert_fusion.qm_ref, ...), custom_call_target="tpu_custom_call" | custom-call | flops 50400002048 | tf_op jit(solution)/shard_map/attend_fwd/pallas_call | solution.py:353
  96.5 13.5 %attend_fwd.3 = (bf16[1024,1024]{1,0:T(8,128)(2,1)}, f32[1024,128]{1,0:T(8,128)}) custom-call(bf16[1024,1024]{1,0:T(8,128)(2,1)} %get-tuple-element.135.q_ref, bf16[1024,1024]{1,0:T(8,128)(2,1)} %get-tuple-element.136.k_ref, bf16[1024,1024]{1,0:T(8,128)(2,1)} %get-tuple-element.137.v_ref, ...), custom_call_target="tpu_custom_call", output_to_operand_aliasing={{0}: (6, {})} | custom-call | flops 83999997952 | tf_op jit(solution)/shard_map/attend_fwd/pallas_call | solution.py:353
  110.6 6.6 %collective-permute-done.28.refs_21_ = bf16[3,44,32,128]{3,2,1,0:T(8,128)(2,1)} collective-permute-done((bf16[3,44,32,128]{3,2,1,0:T(8,128)(2,1)S(1)}, bf16[3,44,32,128]{3,2,1,0:T(8,128)(2,1)}, u32[]{:S(2)}, u32[]{:S(2)}) %collective-permute-start.28) | collective-permute-done | bytes 1081376 | tf_op jit(solution)/shard_map/ppermute | solution.py:59
  119.8 3.4 collective-permute-start.23
  123.9 6.0 %collective-permute-done.30.refs_23_ = bf16[3,22,32,128]{3,2,1,0:T(8,128)(2,1)S(1)} collective-permute-done((bf16[3,22,32,128]{3,2,1,0:T(8,128)(2,1)S(1)}, bf16[3,22,32,128]{3,2,1,0:T(8,128)(2,1)S(1)}, u32[]{:S(2)}, u32[]{:S(2)}) %collective-permute-start.30) | collective-permute-done | bytes 540704 | tf_op jit(solution)/shard_map/ppermute | solution.py:59
  129.9 3.2 collective-permute-start.33
  139.0 45.9 %ffn.1 = (bf16[1024,2816]{1,0:T(8,128)(2,1)}, bf16[1024,2816]{1,0:T(8,128)(2,1)}, bf16[1024,2816]{1,0:T(8,128)(2,1)}, bf16[4,4,22,32,128]{4,3,2,1,0:T(8,128)(2,1...) custom-call(s32[2]{0:T(128)} %pad_add_fusion.refs_0_.pos, ...), custom_call_target="tpu_custom_call" | custom-call | flops 184000004096 | tf_op jit(solution)/shard_map/ffn/pallas_call | solution.py:563
  186.0 11.3 %ffn_out.1 = bf16[1024,1024]{1,0:T(8,128)(2,1)} custom-call(f32[1024,1024]{1,0:T(8,128)} %get-tuple-element.157.r1_ref.r1_hbm, bf16[1024,2816]{1,0:T(8,128)(2,1)} %get-tuple-element.158.hid_ref.hid_hbm, bf16[8,88,32,128]{3,2,1,0:T(8,128)(2,1)} %get-tuple-element.159.wd), custom_call_target="tpu_custom_call" | custom-call | flops 44000002048 | tf_op jit(solution)/shard_map/ffn_out/pallas_call | solution.py:788
  200.4 17.2 %ffn_grads.1 = (bf16[2,132,32,128]{3,2,1,0:T(8,128)(2,1)}, bf16[2,132,32,128]{3,2,1,0:T(8,128)(2,1)}, bf16[2,132,32,128]{3,2,1,0:T(8,128)(2,1)}, bf16[2,132,32,128]{3,2,1,0:T(8,128)(2,1)}) custom-call(s32[2]{0:T(128)} %pad_add_fusion.refs_0_.pos, bf16[16,2,32,1024]{3,2,1,0:T(8,128)(2,1)} %get-tuple-element.164.ht_hbm, bf16[1024,1024]{1,0:T(8,128)(2,1)} %bitcast.141, ...), custom_call_target="tpu_custom_call" | custom-call | flops 67999997952 | tf_op jit(solution)/shard_map/ffn_grads/pallas_call | solution.py:762
  219.3 21.7 %ffn_back.1 = (f32[1024,1024]{1,0:T(8,128)}, bf16[1024,1024]{1,0:T(8,128)(2,1)}, bf16[1024,1024]{1,0:T(8,128)(2,1)}) custom-call(f32[1,1024]{1,0:T(1,128)} %get-tuple-element.252.refs_3_.gain_ref, f32[1024,1]{1,0:T(8,128)} %copy.46.keep_ref, f32[1024,1024]{1,0:T(8,128)} %get-tuple-element.157.r1_ref.r1_hbm, bf16[1024,1024]{1,0:T(8,128)(2,1)} %bitcast.142, ...), custom_call_target="tpu_custom_call" | custom-call | flops 88000004096 | tf_op jit(solution)/shard_map/ffn_back/pallas_call | solution.py:657
  241.0 22.3 %attend_bwd.2 = (bf16[1024,1024]{1,0:T(8,128)(2,1)}, bf16[1024,1024]{1,0:T(8,128)(2,1)}, bf16[1024,1024]{1,0:T(8,128)(2,1)}, f32[1024,1024]{1,0:T(8,128)}) custom-call(bf16[1024,1024]{1,0:T(8,128)(2,1)} %get-tuple-element.135.q_ref, bf16[1024,1024]{1,0:T(8,128)(2,1)} %get-tuple-element.136.k_ref, bf16[1024,1024]{1,0:T(8,128)(2,1)} %get-tuple-element.137.v_ref, ...), custom_call_target="tpu_custom_call" | custom-call | flops 109999996928 | tf_op jit(solution)/shard_map/attend_bwd/pallas_call | solution.py:439
  263.3 4.0 collective-permute-done.40
  271.9 14.9 %attend_bwd.3 = (bf16[1024,1024]{1,0:T(8,128)(2,1)}, bf16[1024,1024]{1,0:T(8,128)(2,1)}, bf16[1024,1024]{1,0:T(8,128)(2,1)}, f32[1024,1024]{1,0:T(8,128)}) custom-call(bf16[1024,1024]{1,0:T(8,128)(2,1)} %get-tuple-element.135.q_ref, ...), custom_call_target="tpu_custom_call", output_to_operand_aliasing={{0}: (10, {}), {1}: (11, {}), {2}: (12, {}), {3}: (13, {})} | custom-call | flops 65999998976 | tf_op jit(solution)/shard_map/attend_bwd/pallas_call | solution.py:439
  286.9 5.8 %collective-permute-done.42 = bf16[132,32,128]{2,1,0:T(8,128)(2,1)S(1)} collective-permute-done((bf16[132,32,128]{2,1,0:T(8,128)(2,1)S(1)}, bf16[132,32,128]{2,1,0:T(8,128)(2,1)S(1)}, u32[]{:S(2)}, u32[]{:S(2)}) %collective-permute-start.42) | collective-permute-done | bytes 1081376 | tf_op jit(solution)/shard_map/ppermute | solution.py:59
  292.7 3.0 collective-permute-done.41
  295.7 8.8 %square_send.1 = bf16[4,4,32,32,128]{4,3,2,1,0:T(8,128)(2,1)} custom-call(s32[2]{0:T(128)} %pad_add_fusion.refs_0_.pos, bf16[16,2,32,1024]{3,2,1,0:T(8,128)(2,1)} %get-tuple-element.160.refs_1_, bf16[16,2,32,1024]{3,2,1,0:T(8,128)(2,1)} %get-tuple-element.161.refs_2_, bf16[1024,1024]{1,0:T(8,128)(2,1)} %get-tuple-element.196.refs_3_, ...), custom_call_target="tpu_custom_call" | custom-call | flops 40000000000 | tf_op jit(solution)/shard_map/square_send/pallas_call | solution.py:868
  319.3 10.3 %square_keep.1 = (bf16[2,64,32,128]{3,2,1,0:T(8,128)(2,1)}, bf16[2,64,32,128]{3,2,1,0:T(8,128)(2,1)}, bf16[2,64,32,128]{3,2,1,0:T(8,128)(2,1)}, bf16[2,64,32,128]{3,2,1,0:T(8,128)(2,1)}) custom-call(s32[2]{0:T(128)} %pad_add_fusion.refs_0_.pos, bf16[16,2,32,1024]{3,2,1,0:T(8,128)(2,1)} %get-tuple-element.160.refs_1_, ...), custom_call_target="tpu_custom_call" | custom-call | flops 40000000000 | tf_op jit(solution)/shard_map/square_keep/pallas_call | solution.py:868
  330.9 14.1 %input_grad.1 = f32[1024,1024]{1,0:T(8,128)} custom-call(bf16[1024,1024]{1,0:T(8,128)(2,1)} %bitcast.145, f32[1,1024]{1,0:T(1,128)} %get-tuple-element.253.refs_1_.gain_ref, bf16[1024,1024]{1,0:T(8,128)(2,1)} %get-tuple-element.197.refs_4_.dq_hbm, bf16[1024,1024]{1,0:T(8,128)(2,1)} %get-tuple-element.198.refs_5_.dk_hbm, ...), custom_call_target="tpu_custom_call" | custom-call | flops 56000000000 | tf_op jit(solution)/shard_map/input_grad/pallas_call | solution.py:925
  345.0 9.8 %collective-permute-done.45 = bf16[2,64,32,128]{3,2,1,0:T(8,128)(2,1)S(1)} collective-permute-done((bf16[2,64,32,128]{3,2,1,0:T(8,128)(2,1)}, bf16[2,64,32,128]{3,2,1,0:T(8,128)(2,1)S(1)}, u32[]{:S(2)}, u32[]{:S(2)}) %collective-permute-start.45) | collective-permute-done | bytes 1048608 | tf_op jit(solution)/shard_map/ppermute | solution.py:59
  355.9 7.9 %collective-permute-done.49 = bf16[67,32,128]{2,1,0:T(8,128)(2,1)} collective-permute-done((bf16[67,32,128]{2,1,0:T(8,128)(2,1)S(1)}, bf16[67,32,128]{2,1,0:T(8,128)(2,1)}, u32[]{:S(2)}, u32[]{:S(2)}) %collective-permute-start.49) | collective-permute-done | bytes 548896 | tf_op jit(solution)/shard_map/ppermute | solution.py:68
  363.8 2.9 collective-permute-done.47
  376.1 6.6 %collective-permute-done.56.refs_3_ = bf16[1,67,32,128]{3,2,1,0:T(8,128)(2,1)S(1)} collective-permute-done((bf16[1,67,32,128]{3,2,1,0:T(8,128)(2,1)S(1)}, bf16[1,67,32,128]{3,2,1,0:T(8,128)(2,1)S(1)}, u32[]{:S(2)}, u32[]{:S(2)}) %collective-permute-start.56) | collective-permute-done | bytes 548896 | tf_op jit(solution)/shard_map/ppermute | solution.py:59
  384.1 9.5 %collective-permute-start.60 = (bf16[1,67,32,128]{3,2,1,0:T(8,128)(2,1)S(1)}, bf16[1,67,32,128]{3,2,1,0:T(8,128)(2,1)S(1)}, u32[]{:S(2)}, u32[]{:S(2)}) collective-permute-start(bf16[1,67,32,128]{3,2,1,0:T(8,128)(2,1)S(1)} %maximum_bitcast_fusion.refs_1_), channel_id=1, source_target_pairs={{0,4},{4,0},{8,12},{12,8},{16,20},{20,16},{24,28},{28,24},{1,5},{5... | collective-permute-start | bytes 1646600 | tf_op jit(solution)/shard_map/ppermute | solution.py:59
  401.8 6.2 %collective-permute-done.59.refs_3_ = bf16[1,32,32,128]{3,2,1,0:T(8,128)(2,1)S(1)} collective-permute-done((bf16[1,32,32,128]{3,2,1,0:T(8,128)(2,1)S(1)}, bf16[1,32,32,128]{3,2,1,0:T(8,128)(2,1)S(1)}, u32[]{:S(2)}, u32[]{:S(2)}) %collective-permute-start.59) | collective-permute-done | bytes 262176 | tf_op jit(solution)/shard_map/ppermute | solution.py:59
  413.1 5.9 %place.3 = (f32[256,2816]{1,0:T(8,128)}, f32[256,2816]{1,0:T(8,128)}, f32[704,1024]{1,0:T(8,128)}, f32[32,128]{1,0:T(8,128)}) custom-call(s32[2]{0:T(128)} %pad_add_fusion.refs_0_.pos, bf16[1,67,32,128]{3,2,1,0:T(8,128)(2,1)} %copy-done.17, bf16[1,67,32,128]{3,2,1,0:T(8,128)(2,1)} %copy-done.28, bf16[1,67,32,128]{3,2,1,0:T(8,128)(2,1)} %copy-done.27, ...), custom_call_target="tpu_custom_call" | custom-call | flops 20000000000 | tf_op jit(solution)/shard_map/place/pallas_call | solution.py:971
  427.0 3.8 place.2
  (338 shorter events, 124.3 us)
Async XLA Ops:
  5.6 15.6 %collective-permute-start.1 = (bf16[25,32,128]{2,1,0:T(8,128)(2,1)}, bf16[25,32,128]{2,1,0:T(8,128)(2,1)S(1)}, u32[]{:S(2)}, u32[]{:S(2)}) collective-permute-start(bf16[25,32,128]{2,1,0:T(8,128)(2,1)} %cut.3), channel_id=1, source_target_pairs={{0,2},{1,3},{2,0},{3,1},{4,6},{5,7},{6,4},{7,5},{8,10},{9,11},{10,... | collective-permute-start | bytes 614408 | tf_op jit(solution)/shard_map/ppermute | solution.py:68
  8.1 17.5 %collective-permute-start = (bf16[25,32,128]{2,1,0:T(8,128)(2,1)}, bf16[25,32,128]{2,1,0:T(8,128)(2,1)S(1)}, u32[]{:S(2)}, u32[]{:S(2)}) collective-permute-start(bf16[25,32,128]{2,1,0:T(8,128)(2,1)} %cut.3), channel_id=1, source_target_pairs={{0,1},{1,2},{2,3},{3,0},{4,5},{5,6},{6,7},{7,4},{8,9},{9,10},{10,1... | collective-permute-start | bytes 614408 | tf_op jit(solution)/shard_map/ppermute | solution.py:68
  32.4 14.9 %collective-permute-start.3 = (bf16[3,24,32,128]{3,2,1,0:T(8,128)(2,1)S(1)}, bf16[3,24,32,128]{3,2,1,0:T(8,128)(2,1)}, u32[]{:S(2)}, u32[]{:S(2)}) collective-permute-start(bf16[3,24,32,128]{3,2,1,0:T(8,128)(2,1)S(1)} %pad_maximum_fusion.8.refs_9_), channel_id=1, source_target_pairs={{0,8},{4,12},{8,0},{12,4},{16,24},{20,28},{24,16},{28,20},{1,9},{5... | collective-permute-start | bytes 1769480 | tf_op jit(solution)/shard_map/ppermute | solution.py:59
  42.6 15.8 %collective-permute-start.14 = (bf16[30,32,128]{2,1,0:T(8,128)(2,1)S(1)}, bf16[30,32,128]{2,1,0:T(8,128)(2,1)S(1)}, u32[]{:S(2)}, u32[]{:S(2)}) collective-permute-start(bf16[30,32,128]{2,1,0:T(8,128)(2,1)S(1)} %copy-done.22), channel_id=1, source_target_pairs={{0,2},{1,3},{2,0},{3,1},{4,6},{5,7},{6,4},{7,5},{8,10},{9,11},{10,... | collective-permute-start | bytes 737288 | tf_op jit(solution)/shard_map/ppermute | solution.py:68
  47.3 15.6 %collective-permute-start.11 = (bf16[3,24,32,128]{3,2,1,0:T(8,128)(2,1)S(1)}, bf16[3,24,32,128]{3,2,1,0:T(8,128)(2,1)}, u32[]{:S(2)}, u32[]{:S(2)}) collective-permute-start(bf16[3,24,32,128]{3,2,1,0:T(8,128)(2,1)S(1)} %collective-permute-done.4.refs_11_), channel_id=1, source_target_pairs={{0,4},{4,0},{8,12},{12,8},{16,20},{20,16},{24,28},{28,24},{1,5},{5... | collective-permute-start | bytes 1769480 | tf_op jit(solution)/shard_map/ppermute | solution.py:59
  59.2 32.2 %collective-permute-start.21 = (bf16[44,32,128]{2,1,0:T(8,128)(2,1)S(1)}, bf16[44,32,128]{2,1,0:T(8,128)(2,1)S(1)}, u32[]{:S(2)}, u32[]{:S(2)}) collective-permute-start(bf16[44,32,128]{2,1,0:T(8,128)(2,1)S(1)} %copy-done.20), channel_id=1, source_target_pairs={{0,3},{1,0},{2,1},{3,2},{4,7},{5,4},{6,5},{7,6},{8,11},{9,8},{10,9... | collective-permute-start | bytes 1081352 | tf_op jit(solution)/shard_map/ppermute | solution.py:68
  60.3 31.2 %collective-permute-start.20 = (bf16[44,32,128]{2,1,0:T(8,128)(2,1)S(1)}, bf16[44,32,128]{2,1,0:T(8,128)(2,1)S(1)}, u32[]{:S(2)}, u32[]{:S(2)}) collective-permute-start(bf16[44,32,128]{2,1,0:T(8,128)(2,1)S(1)} %copy-done.20), channel_id=1, source_target_pairs={{0,2},{1,3},{2,0},{3,1},{4,6},{5,7},{6,4},{7,5},{8,10},{9,11},{10,... | collective-permute-start | bytes 1081352 | tf_op jit(solution)/shard_map/ppermute | solution.py:68
  62.9 30.1 %collective-permute-start.19 = (bf16[44,32,128]{2,1,0:T(8,128)(2,1)S(1)}, bf16[44,32,128]{2,1,0:T(8,128)(2,1)S(1)}, u32[]{:S(2)}, u32[]{:S(2)}) collective-permute-start(bf16[44,32,128]{2,1,0:T(8,128)(2,1)S(1)} %copy-done.20), channel_id=1, source_target_pairs={{0,1},{1,2},{2,3},{3,0},{4,5},{5,6},{6,7},{7,4},{8,9},{9,10},{10,1... | collective-permute-start | bytes 1081352 | tf_op jit(solution)/shard_map/ppermute | solution.py:68
  63.4 17.2 %collective-permute-start.16 = (bf16[3,30,32,128]{3,2,1,0:T(8,128)(2,1)S(1)}, bf16[3,30,32,128]{3,2,1,0:T(8,128)(2,1)S(1)}, u32[]{:S(2)}, u32[]{:S(2)}) collective-permute-start(bf16[3,30,32,128]{3,2,1,0:T(8,128)(2,1)S(1)} %pad_maximum_fusion.6.refs_7_), channel_id=1, source_target_pairs={{0,16},{4,20},{8,24},{12,28},{16,0},{20,4},{24,8},{28,12},{1,17},{... | collective-permute-start | bytes 2211848 | tf_op jit(solution)/shard_map/ppermute | solution.py:59
  63.7 17.0 %collective-permute-start.15 = (bf16[3,30,32,128]{3,2,1,0:T(8,128)(2,1)S(1)}, bf16[3,30,32,128]{3,2,1,0:T(8,128)(2,1)S(1)}, u32[]{:S(2)}, u32[]{:S(2)}) collective-permute-start(bf16[3,30,32,128]{3,2,1,0:T(8,128)(2,1)S(1)} %pad_maximum_fusion.6.refs_7_), channel_id=1, source_target_pairs={{0,8},{4,12},{8,0},{12,4},{16,24},{20,28},{24,16},{28,20},{1,9},{5... | collective-permute-start | bytes 2211848 | tf_op jit(solution)/shard_map/ppermute | solution.py:59
  80.7 15.8 %collective-permute-start.17 = (bf16[3,15,32,128]{3,2,1,0:T(8,128)(2,1)S(1)}, bf16[3,15,32,128]{3,2,1,0:T(8,128)(2,1)}, u32[]{:S(2)}, u32[]{:S(2)}) collective-permute-start(bf16[3,15,32,128]{3,2,1,0:T(8,128)(2,1)S(1)} %slice.223), channel_id=1, source_target_pairs={{0,16},{4,20},{8,24},{12,28},{16,0},{20,4},{24,8},{28,12},{1,17},{... | collective-permute-start | bytes 1105928 | tf_op jit(solution)/shard_map/ppermute | solution.py:59
  93.2 24.1 %collective-permute-start.28 = (bf16[3,44,32,128]{3,2,1,0:T(8,128)(2,1)S(1)}, bf16[3,44,32,128]{3,2,1,0:T(8,128)(2,1)}, u32[]{:S(2)}, u32[]{:S(2)}) collective-permute-start(bf16[3,44,32,128]{3,2,1,0:T(8,128)(2,1)S(1)} %pad_maximum_fusion.5.refs_19_), channel_id=1, source_target_pairs={{0,16},{4,20},{8,24},{12,28},{16,0},{20,4},{24,8},{28,12},{1,17},{... | collective-permute-start | bytes 3244040 | tf_op jit(solution)/shard_map/ppermute | solution.py:59
  93.5 24.9 %collective-permute-start.27 = (bf16[3,44,32,128]{3,2,1,0:T(8,128)(2,1)S(1)}, bf16[3,44,32,128]{3,2,1,0:T(8,128)(2,1)}, u32[]{:S(2)}, u32[]{:S(2)}) collective-permute-start(bf16[3,44,32,128]{3,2,1,0:T(8,128)(2,1)S(1)} %pad_maximum_fusion.5.refs_19_), channel_id=1, source_target_pairs={{0,8},{4,12},{8,0},{12,4},{16,24},{20,28},{24,16},{28,20},{1,9},{5... | collective-permute-start | bytes 3244040 | tf_op jit(solution)/shard_map/ppermute | solution.py:59
  93.9 29.4 %collective-permute-start.22 = (bf16[3,30,32,128]{3,2,1,0:T(8,128)(2,1)S(1)}, bf16[3,30,32,128]{3,2,1,0:T(8,128)(2,1)S(1)}, u32[]{:S(2)}, u32[]{:S(2)}) collective-permute-start(bf16[3,30,32,128]{3,2,1,0:T(8,128)(2,1)S(1)} %pad_maximum_fusion.6.refs_7_), channel_id=1, source_target_pairs={{0,4},{4,0},{8,12},{12,8},{16,20},{20,16},{24,28},{28,24},{1,5},{5... | collective-permute-start | bytes 2211848 | tf_op jit(solution)/shard_map/ppermute | solution.py:59
  123.4 14.8 %collective-permute-start.31 = (bf16[3,44,32,128]{3,2,1,0:T(8,128)(2,1)S(1)}, bf16[3,44,32,128]{3,2,1,0:T(8,128)(2,1)}, u32[]{:S(2)}, u32[]{:S(2)}) collective-permute-start(bf16[3,44,32,128]{3,2,1,0:T(8,128)(2,1)S(1)} %pad_maximum_fusion.5.refs_19_), channel_id=1, source_target_pairs={{0,4},{4,0},{8,12},{12,8},{16,20},{20,16},{24,28},{28,24},{1,5},{5... | collective-permute-start | bytes 3244040 | tf_op jit(solution)/shard_map/ppermute | solution.py:59
  217.6 49.7 %collective-permute-start.39 = (bf16[2,132,32,128]{3,2,1,0:T(8,128)(2,1)}, bf16[2,132,32,128]{3,2,1,0:T(8,128)(2,1)}, u32[]{:S(2)}, u32[]{:S(2)}) collective-permute-start(bf16[2,132,32,128]{3,2,1,0:T(8,128)(2,1)} %get-tuple-element.172), channel_id=1, source_target_pairs={{0,8},{4,12},{8,0},{12,4},{16,24},{20,28},{24,16},{28,20},{1,9},{5... | collective-permute-start | bytes 6488072 | tf_op jit(solution)/shard_map/ppermute | solution.py:59
  219.1 48.2 %collective-permute-start.40 = (bf16[2,132,32,128]{3,2,1,0:T(8,128)(2,1)}, bf16[2,132,32,128]{3,2,1,0:T(8,128)(2,1)}, u32[]{:S(2)}, u32[]{:S(2)}) collective-permute-start(bf16[2,132,32,128]{3,2,1,0:T(8,128)(2,1)} %get-tuple-element.185), channel_id=1, source_target_pairs={{0,16},{4,20},{8,24},{12,28},{16,0},{20,4},{24,8},{28,12},{1,17},{... | collective-permute-start | bytes 6488072 | tf_op jit(solution)/shard_map/ppermute | solution.py:59
  268.8 23.9 %collective-permute-start.42 = (bf16[132,32,128]{2,1,0:T(8,128)(2,1)S(1)}, bf16[132,32,128]{2,1,0:T(8,128)(2,1)S(1)}, u32[]{:S(2)}, u32[]{:S(2)}) collective-permute-start(bf16[132,32,128]{2,1,0:T(8,128)(2,1)S(1)} %fusion.3), channel_id=1, source_target_pairs={{0,8},{4,12},{8,0},{12,4},{16,24},{20,28},{24,16},{28,20},{1,9},{5... | collective-permute-start | bytes 3244040 | tf_op jit(solution)/shard_map/ppermute | solution.py:59
  271.7 24.0 %collective-permute-start.41 = (bf16[132,32,128]{2,1,0:T(8,128)(2,1)}, bf16[132,32,128]{2,1,0:T(8,128)(2,1)S(1)}, u32[]{:S(2)}, u32[]{:S(2)}) collective-permute-start(bf16[132,32,128]{2,1,0:T(8,128)(2,1)} %fusion.2), channel_id=1, source_target_pairs={{0,16},{4,20},{8,24},{12,28},{16,0},{20,4},{24,8},{28,12},{1,17},{... | collective-permute-start | bytes 3244040 | tf_op jit(solution)/shard_map/ppermute | solution.py:59
  304.6 14.7 %collective-permute-start.43 = (bf16[4,4,32,32,128]{4,3,2,1,0:T(8,128)(2,1)}, bf16[4,4,32,32,128]{4,3,2,1,0:T(8,128)(2,1)}, u32[]{:S(2)}, u32[]{:S(2)}) collective-permute-start(bf16[4,4,32,32,128]{4,3,2,1,0:T(8,128)(2,1)} %square_send.1), channel_id=1, source_target_pairs={{0,4},{4,0},{8,12},{12,8},{16,20},{20,16},{24,28},{28,24},{1,5},{5... | collective-permute-start | bytes 12582920 | tf_op jit(solution)/shard_map/ppermute | solution.py:59
  314.5 41.4 %collective-permute-start.50 = (bf16[67,32,128]{2,1,0:T(8,128)(2,1)}, bf16[67,32,128]{2,1,0:T(8,128)(2,1)}, u32[]{:S(2)}, u32[]{:S(2)}) collective-permute-start(bf16[67,32,128]{2,1,0:T(8,128)(2,1)} %get-tuple-element.248), channel_id=1, source_target_pairs={{0,3},{1,0},{2,1},{3,2},{4,7},{5,4},{6,5},{7,6},{8,11},{9,8},{10,9... | collective-permute-start | bytes 1646600 | tf_op jit(solution)/shard_map/ppermute | solution.py:68
  316.1 39.8 %collective-permute-start.48 = (bf16[67,32,128]{2,1,0:T(8,128)(2,1)S(1)}, bf16[67,32,128]{2,1,0:T(8,128)(2,1)}, u32[]{:S(2)}, u32[]{:S(2)}) collective-permute-start(bf16[67,32,128]{2,1,0:T(8,128)(2,1)S(1)} %get-tuple-element.249), channel_id=1, source_target_pairs={{0,1},{1,2},{2,3},{3,0},{4,5},{5,6},{6,7},{7,4},{8,9},{9,10},{10,1... | collective-permute-start | bytes 1646600 | tf_op jit(solution)/shard_map/ppermute | solution.py:68
  318.0 45.8 %collective-permute-start.49 = (bf16[67,32,128]{2,1,0:T(8,128)(2,1)S(1)}, bf16[67,32,128]{2,1,0:T(8,128)(2,1)}, u32[]{:S(2)}, u32[]{:S(2)}) collective-permute-start(bf16[67,32,128]{2,1,0:T(8,128)(2,1)S(1)} %get-tuple-element.250), channel_id=1, source_target_pairs={{0,2},{1,3},{2,0},{3,1},{4,6},{5,7},{6,4},{7,5},{8,10},{9,11},{10,... | collective-permute-start | bytes 1646600 | tf_op jit(solution)/shard_map/ppermute | solution.py:68
  329.6 25.2 %collective-permute-start.44 = (bf16[2,64,32,128]{3,2,1,0:T(8,128)(2,1)}, bf16[2,64,32,128]{3,2,1,0:T(8,128)(2,1)S(1)}, u32[]{:S(2)}, u32[]{:S(2)}) collective-permute-start(bf16[2,64,32,128]{3,2,1,0:T(8,128)(2,1)} %get-tuple-element.204), channel_id=1, source_target_pairs={{0,8},{4,12},{8,0},{12,4},{16,24},{20,28},{24,16},{28,20},{1,9},{5... | collective-permute-start | bytes 3145736 | tf_op jit(solution)/shard_map/ppermute | solution.py:59
  330.7 24.1 %collective-permute-start.45 = (bf16[2,64,32,128]{3,2,1,0:T(8,128)(2,1)}, bf16[2,64,32,128]{3,2,1,0:T(8,128)(2,1)S(1)}, u32[]{:S(2)}, u32[]{:S(2)}) collective-permute-start(bf16[2,64,32,128]{3,2,1,0:T(8,128)(2,1)} %get-tuple-element.212), channel_id=1, source_target_pairs={{0,16},{4,20},{8,24},{12,28},{16,0},{20,4},{24,8},{28,12},{1,17},{... | collective-permute-start | bytes 3145736 | tf_op jit(solution)/shard_map/ppermute | solution.py:59
  373.0 20.6 %collective-permute-start.52 = (bf16[32,32,128]{2,1,0:T(8,128)(2,1)S(1)}, bf16[32,32,128]{2,1,0:T(8,128)(2,1)S(1)}, u32[]{:S(2)}, u32[]{:S(2)}) collective-permute-start(bf16[32,32,128]{2,1,0:T(8,128)(2,1)S(1)} %get-tuple-element.246), channel_id=1, source_target_pairs={{0,2},{1,3},{2,0},{3,1},{4,6},{5,7},{6,4},{7,5},{8,10},{9,11},{10,... | collective-permute-start | bytes 786440 | tf_op jit(solution)/shard_map/ppermute | solution.py:68
  375.8 23.3 %collective-permute-start.53 = (bf16[32,32,128]{2,1,0:T(8,128)(2,1)S(1)}, bf16[32,32,128]{2,1,0:T(8,128)(2,1)S(1)}, u32[]{:S(2)}, u32[]{:S(2)}) collective-permute-start(bf16[32,32,128]{2,1,0:T(8,128)(2,1)S(1)} %get-tuple-element.247), channel_id=1, source_target_pairs={{0,3},{1,0},{2,1},{3,2},{4,7},{5,4},{6,5},{7,6},{8,11},{9,8},{10,9... | collective-permute-start | bytes 786440 | tf_op jit(solution)/shard_map/ppermute | solution.py:68
  382.7 17.3 %collective-permute-start.57 = (bf16[1,34,32,128]{3,2,1,0:T(8,128)(2,1)S(1)}, bf16[1,34,32,128]{3,2,1,0:T(8,128)(2,1)S(1)}, u32[]{:S(2)}, u32[]{:S(2)}) collective-permute-start(bf16[1,34,32,128]{3,2,1,0:T(8,128)(2,1)S(1)} %slice.237), channel_id=1, source_target_pairs={{0,8},{4,12},{8,0},{12,4},{16,24},{20,28},{24,16},{28,20},{1,9},{5... | collective-permute-start | bytes 835592 | tf_op jit(solution)/shard_map/ppermute | solution.py:59
  383.8 16.2 %collective-permute-start.55 = (bf16[1,33,32,128]{3,2,1,0:T(8,128)(2,1)S(1)}, bf16[1,33,32,128]{3,2,1,0:T(8,128)(2,1)S(1)}, u32[]{:S(2)}, u32[]{:S(2)}) collective-permute-start(bf16[1,33,32,128]{3,2,1,0:T(8,128)(2,1)S(1)} %slice.236), channel_id=1, source_target_pairs={{0,16},{4,20},{8,24},{12,28},{16,0},{20,4},{24,8},{28,12},{1,17},{... | collective-permute-start | bytes 811016 | tf_op jit(solution)/shard_map/ppermute | solution.py:59
  384.1 26.0 %collective-permute-start.60 = (bf16[1,67,32,128]{3,2,1,0:T(8,128)(2,1)S(1)}, bf16[1,67,32,128]{3,2,1,0:T(8,128)(2,1)S(1)}, u32[]{:S(2)}, u32[]{:S(2)}) collective-permute-start(bf16[1,67,32,128]{3,2,1,0:T(8,128)(2,1)S(1)} %maximum_bitcast_fusion.refs_1_), channel_id=1, source_target_pairs={{0,4},{4,0},{8,12},{12,8},{16,20},{20,16},{24,28},{28,24},{1,5},{5... | collective-permute-start | bytes 1646600 | tf_op jit(solution)/shard_map/ppermute | solution.py:59
  393.6 18.0 %collective-permute-start.62 = (bf16[1,67,32,128]{3,2,1,0:T(8,128)(2,1)S(1)}, bf16[1,67,32,128]{3,2,1,0:T(8,128)(2,1)S(1)}, u32[]{:S(2)}, u32[]{:S(2)}) collective-permute-start(bf16[1,67,32,128]{3,2,1,0:T(8,128)(2,1)S(1)} %collective-permute-done.56.refs_3_), channel_id=1, source_target_pairs={{0,4},{4,0},{8,12},{12,8},{16,20},{20,16},{24,28},{28,24},{1,5},{5... | collective-permute-start | bytes 1646600 | tf_op jit(solution)/shard_map/ppermute | solution.py:59
  410.1 15.0 %collective-permute-start.67 = (bf16[1,32,32,128]{3,2,1,0:T(8,128)(2,1)S(1)}, bf16[1,32,32,128]{3,2,1,0:T(8,128)(2,1)}, u32[]{:S(2)}, u32[]{:S(2)}) collective-permute-start(bf16[1,32,32,128]{3,2,1,0:T(8,128)(2,1)S(1)} %bitcast.130), channel_id=1, source_target_pairs={{0,4},{4,0},{8,12},{12,8},{16,20},{20,16},{24,28},{28,24},{1,5},{5... | collective-permute-start | bytes 786440 | tf_op jit(solution)/shard_map/ppermute | solution.py:59
  (95 other events, 1017.1 us)

commit v4 on v3

--- a/solution.py
+++ b/solution.py
@@ -685,7 +685,7 @@
                    ht, df, hid, dg, du, rg, ru, rd, out_a, out_b, sem):
     core, b1, b2 = bits(pos)
     blocks = rg.shape[2]
-    chunks = chunked(blocks, 4)
+    chunks = chunked(blocks, 8)
     first = [pltpu.make_async_copy(ht_hbm.at[:, core], ht, sem.at[0])]
     for p in range(4):
         cols = pl.ds(pl.multiple_of((2 * p + core) * L, L), L)

time: 439 us -> 438 us (level)
  no operation moved by 1% of the time
where the time goes in v4:
time: 438 us; the launch traced here: 433 us
  Pallas kernels  220 us (50%)
  waiting for transfers between devices  85.4 us (19%)
  starting transfers between devices  77.8 us (18%)
  other arithmetic  28.7 us (7%)
  local copies, waits for them, and re-layouts  19 us (4%)
    ppermute x57, waiting for transfers between devices, dp_swap(): lax.ppermute(x, 'dp', [(i, i ^ bit) for i in range(lax.axis_size('dp'))])  62.3 us
    ppermute x57, starting transfers between devices, dp_swap(): lax.ppermute(x, 'dp', [(i, i ^ bit) for i in range(lax.axis_size('dp'))])  56.2 us
    pallas_call x1, Pallas kernels, ffn(): pl.pallas_call(lambda *refs: ffn_body(groups, *refs), grid=(1 + tiles,),...  45.9 us
    pallas_call x2, Pallas kernels, attend_bwd(): pl.pallas_call(attend_bwd_body, grid=(pairs,), in_specs=[col] * 4 + [whol...  37.3 us
    ppermute x15, waiting for transfers between devices, fsdp_shift(): lax.ppermute(x, 'fsdp', [(i, (i + step) % size) for i in range(size)])  23.1 us
    pallas_call x2, Pallas kernels, attend_fwd(): pl.pallas_call(attend_fwd_body, grid=(pairs,), in_specs=[col, col, col, p...  22.9 us
    pallas_call x1, Pallas kernels, ffn_back(): pl.pallas_call(ffn_back_body, in_specs=[vmem, vmem] + [ANY] * 7, out_spec...  21.7 us
    ppermute x15, starting transfers between devices, fsdp_shift(): lax.ppermute(x, 'fsdp', [(i, (i + step) % size) for i in range(size)])  21.6 us
  transfers between devices with their start and end apart: 72, of which 26 were waited for; matrix products, arithmetic and copies ran while one was open for 7% of the time, Pallas kernels for 33%

profile of v4, /device:TPU:9, one launch (start us, length us, event | category | flops | bytes accessed | tf_op | source)
XLA Modules:
  0.0 432.6 jit_solution(3058761447974354102)
XLA Ops:
  16.6 4.6 %collective-permute-done.1 = bf16[25,32,128]{2,1,0:T(8,128)(2,1)S(1)} collective-permute-done((bf16[25,32,128]{2,1,0:T(8,128)(2,1)}, bf16[25,32,128]{2,1,0:T(8,128)(2,1)S(1)}, u32[]{:S(2)}, u32[]{:S(2)}) %collective-permute-start.1) | collective-permute-done | bytes 204832 | tf_op jit(solution)/shard_map/ppermute | solution.py:68
  21.2 4.4 %collective-permute-done = bf16[25,32,128]{2,1,0:T(8,128)(2,1)S(1)} collective-permute-done((bf16[25,32,128]{2,1,0:T(8,128)(2,1)}, bf16[25,32,128]{2,1,0:T(8,128)(2,1)S(1)}, u32[]{:S(2)}, u32[]{:S(2)}) %collective-permute-start) | collective-permute-done | bytes 204832 | tf_op jit(solution)/shard_map/ppermute | solution.py:68
  42.6 2.9 collective-permute-start.14
  48.7 3.2 collective-permute-done.8.refs_13_
  54.7 3.8 collective-permute-start.13
  64.1 14.6 %qkv.1 = (bf16[1024,1024]{1,0:T(8,128)(2,1)}, bf16[1024,1024]{1,0:T(8,128)(2,1)}, bf16[1024,1024]{1,0:T(8,128)(2,1)}, bf16[16,2,32,1024]{3,2,1,0:T(8,128)(2,1)},...) custom-call(s32[2]{0:T(128)} %pad_add_fusion.refs_0_.pos, ...), custom_call_target="tpu_custom_call" | custom-call | flops 60000002048 | tf_op jit(solution)/shard_map/qkv/pallas_call | solution.py:279
  81.8 9.4 %attend_fwd.2 = (bf16[1024,1024]{1,0:T(8,128)(2,1)}, f32[1024,128]{1,0:T(8,128)}) custom-call(bf16[1024,1024]{1,0:T(8,128)(2,1)} %get-tuple-element.135.q_ref, bf16[1024,1024]{1,0:T(8,128)(2,1)} %get-tuple-element.136.k_ref, bf16[1024,1024]{1,0:T(8,128)(2,1)} %get-tuple-element.137.v_ref, bf16[1024,128]{1,0:T(8,128)(2,1)} %select_convert_fusion.qm_ref, ...), custom_call_target="tpu_custom_call" | custom-call | flops 50400002048 | tf_op jit(solution)/shard_map/attend_fwd/pallas_call | solution.py:353
  96.3 13.5 %attend_fwd.3 = (bf16[1024,1024]{1,0:T(8,128)(2,1)}, f32[1024,128]{1,0:T(8,128)}) custom-call(bf16[1024,1024]{1,0:T(8,128)(2,1)} %get-tuple-element.135.q_ref, bf16[1024,1024]{1,0:T(8,128)(2,1)} %get-tuple-element.136.k_ref, bf16[1024,1024]{1,0:T(8,128)(2,1)} %get-tuple-element.137.v_ref, ...), custom_call_target="tpu_custom_call", output_to_operand_aliasing={{0}: (6, {})} | custom-call | flops 83999997952 | tf_op jit(solution)/shard_map/attend_fwd/pallas_call | solution.py:353
  110.4 7.0 %collective-permute-done.28.refs_21_ = bf16[3,44,32,128]{3,2,1,0:T(8,128)(2,1)} collective-permute-done((bf16[3,44,32,128]{3,2,1,0:T(8,128)(2,1)S(1)}, bf16[3,44,32,128]{3,2,1,0:T(8,128)(2,1)}, u32[]{:S(2)}, u32[]{:S(2)}) %collective-permute-start.28) | collective-permute-done | bytes 1081376 | tf_op jit(solution)/shard_map/ppermute | solution.py:59
  120.0 3.2 collective-permute-start.23
  123.9 6.4 %collective-permute-done.30.refs_23_ = bf16[3,22,32,128]{3,2,1,0:T(8,128)(2,1)S(1)} collective-permute-done((bf16[3,22,32,128]{3,2,1,0:T(8,128)(2,1)S(1)}, bf16[3,22,32,128]{3,2,1,0:T(8,128)(2,1)S(1)}, u32[]{:S(2)}, u32[]{:S(2)}) %collective-permute-start.30) | collective-permute-done | bytes 540704 | tf_op jit(solution)/shard_map/ppermute | solution.py:59
  130.3 3.0 collective-permute-start.33
  139.2 45.9 %ffn.1 = (bf16[1024,2816]{1,0:T(8,128)(2,1)}, bf16[1024,2816]{1,0:T(8,128)(2,1)}, bf16[1024,2816]{1,0:T(8,128)(2,1)}, bf16[4,4,22,32,128]{4,3,2,1,0:T(8,128)(2,1...) custom-call(s32[2]{0:T(128)} %pad_add_fusion.refs_0_.pos, ...), custom_call_target="tpu_custom_call" | custom-call | flops 184000004096 | tf_op jit(solution)/shard_map/ffn/pallas_call | solution.py:563
  186.1 11.3 %ffn_out.1 = bf16[1024,1024]{1,0:T(8,128)(2,1)} custom-call(f32[1024,1024]{1,0:T(8,128)} %get-tuple-element.157.r1_ref.r1_hbm, bf16[1024,2816]{1,0:T(8,128)(2,1)} %get-tuple-element.158.hid_ref.hid_hbm, bf16[8,88,32,128]{3,2,1,0:T(8,128)(2,1)} %get-tuple-element.159.wd), custom_call_target="tpu_custom_call" | custom-call | flops 44000002048 | tf_op jit(solution)/shard_map/ffn_out/pallas_call | solution.py:788
  200.6 16.0 %ffn_grads.1 = (bf16[2,132,32,128]{3,2,1,0:T(8,128)(2,1)}, bf16[2,132,32,128]{3,2,1,0:T(8,128)(2,1)}, bf16[2,132,32,128]{3,2,1,0:T(8,128)(2,1)}, bf16[2,132,32,128]{3,2,1,0:T(8,128)(2,1)}) custom-call(s32[2]{0:T(128)} %pad_add_fusion.refs_0_.pos, bf16[16,2,32,1024]{3,2,1,0:T(8,128)(2,1)} %get-tuple-element.164.ht_hbm, bf16[1024,1024]{1,0:T(8,128)(2,1)} %bitcast.141, ...), custom_call_target="tpu_custom_call" | custom-call | flops 67999997952 | tf_op jit(solution)/shard_map/ffn_grads/pallas_call | solution.py:762
  218.4 21.7 %ffn_back.1 = (f32[1024,1024]{1,0:T(8,128)}, bf16[1024,1024]{1,0:T(8,128)(2,1)}, bf16[1024,1024]{1,0:T(8,128)(2,1)}) custom-call(f32[1,1024]{1,0:T(1,128)} %get-tuple-element.252.refs_3_.gain_ref, f32[1024,1]{1,0:T(8,128)} %copy.46.keep_ref, f32[1024,1024]{1,0:T(8,128)} %get-tuple-element.157.r1_ref.r1_hbm, bf16[1024,1024]{1,0:T(8,128)(2,1)} %bitcast.142, ...), custom_call_target="tpu_custom_call" | custom-call | flops 88000004096 | tf_op jit(solution)/shard_map/ffn_back/pallas_call | solution.py:657
  240.0 22.3 %attend_bwd.2 = (bf16[1024,1024]{1,0:T(8,128)(2,1)}, bf16[1024,1024]{1,0:T(8,128)(2,1)}, bf16[1024,1024]{1,0:T(8,128)(2,1)}, f32[1024,1024]{1,0:T(8,128)}) custom-call(bf16[1024,1024]{1,0:T(8,128)(2,1)} %get-tuple-element.135.q_ref, bf16[1024,1024]{1,0:T(8,128)(2,1)} %get-tuple-element.136.k_ref, bf16[1024,1024]{1,0:T(8,128)(2,1)} %get-tuple-element.137.v_ref, ...), custom_call_target="tpu_custom_call" | custom-call | flops 109999996928 | tf_op jit(solution)/shard_map/attend_bwd/pallas_call | solution.py:439
  262.4 4.0 collective-permute-done.40
  271.0 15.0 %attend_bwd.3 = (bf16[1024,1024]{1,0:T(8,128)(2,1)}, bf16[1024,1024]{1,0:T(8,128)(2,1)}, bf16[1024,1024]{1,0:T(8,128)(2,1)}, f32[1024,1024]{1,0:T(8,128)}) custom-call(bf16[1024,1024]{1,0:T(8,128)(2,1)} %get-tuple-element.135.q_ref, ...), custom_call_target="tpu_custom_call", output_to_operand_aliasing={{0}: (10, {}), {1}: (11, {}), {2}: (12, {}), {3}: (13, {})} | custom-call | flops 65999998976 | tf_op jit(solution)/shard_map/attend_bwd/pallas_call | solution.py:439
  286.0 5.8 %collective-permute-done.42 = bf16[132,32,128]{2,1,0:T(8,128)(2,1)S(1)} collective-permute-done((bf16[132,32,128]{2,1,0:T(8,128)(2,1)S(1)}, bf16[132,32,128]{2,1,0:T(8,128)(2,1)S(1)}, u32[]{:S(2)}, u32[]{:S(2)}) %collective-permute-start.42) | collective-permute-done | bytes 1081376 | tf_op jit(solution)/shard_map/ppermute | solution.py:59
  291.8 3.0 collective-permute-done.41
  294.8 8.8 %square_send.1 = bf16[4,4,32,32,128]{4,3,2,1,0:T(8,128)(2,1)} custom-call(s32[2]{0:T(128)} %pad_add_fusion.refs_0_.pos, bf16[16,2,32,1024]{3,2,1,0:T(8,128)(2,1)} %get-tuple-element.160.refs_1_, bf16[16,2,32,1024]{3,2,1,0:T(8,128)(2,1)} %get-tuple-element.161.refs_2_, bf16[1024,1024]{1,0:T(8,128)(2,1)} %get-tuple-element.196.refs_3_, ...), custom_call_target="tpu_custom_call" | custom-call | flops 40000000000 | tf_op jit(solution)/shard_map/square_send/pallas_call | solution.py:868
  318.2 10.3 %square_keep.1 = (bf16[2,64,32,128]{3,2,1,0:T(8,128)(2,1)}, bf16[2,64,32,128]{3,2,1,0:T(8,128)(2,1)}, bf16[2,64,32,128]{3,2,1,0:T(8,128)(2,1)}, bf16[2,64,32,128]{3,2,1,0:T(8,128)(2,1)}) custom-call(s32[2]{0:T(128)} %pad_add_fusion.refs_0_.pos, bf16[16,2,32,1024]{3,2,1,0:T(8,128)(2,1)} %get-tuple-element.160.refs_1_, ...), custom_call_target="tpu_custom_call" | custom-call | flops 40000000000 | tf_op jit(solution)/shard_map/square_keep/pallas_call | solution.py:868
  329.8 14.1 %input_grad.1 = f32[1024,1024]{1,0:T(8,128)} custom-call(bf16[1024,1024]{1,0:T(8,128)(2,1)} %bitcast.145, f32[1,1024]{1,0:T(1,128)} %get-tuple-element.253.refs_1_.gain_ref, bf16[1024,1024]{1,0:T(8,128)(2,1)} %get-tuple-element.197.refs_4_.dq_hbm, bf16[1024,1024]{1,0:T(8,128)(2,1)} %get-tuple-element.198.refs_5_.dk_hbm, ...), custom_call_target="tpu_custom_call" | custom-call | flops 56000000000 | tf_op jit(solution)/shard_map/input_grad/pallas_call | solution.py:925
  343.9 9.8 %collective-permute-done.45 = bf16[2,64,32,128]{3,2,1,0:T(8,128)(2,1)S(1)} collective-permute-done((bf16[2,64,32,128]{3,2,1,0:T(8,128)(2,1)}, bf16[2,64,32,128]{3,2,1,0:T(8,128)(2,1)S(1)}, u32[]{:S(2)}, u32[]{:S(2)}) %collective-permute-start.45) | collective-permute-done | bytes 1048608 | tf_op jit(solution)/shard_map/ppermute | solution.py:59
  354.8 7.8 %collective-permute-done.49 = bf16[67,32,128]{2,1,0:T(8,128)(2,1)} collective-permute-done((bf16[67,32,128]{2,1,0:T(8,128)(2,1)S(1)}, bf16[67,32,128]{2,1,0:T(8,128)(2,1)}, u32[]{:S(2)}, u32[]{:S(2)}) %collective-permute-start.49) | collective-permute-done | bytes 548896 | tf_op jit(solution)/shard_map/ppermute | solution.py:68
  362.6 3.0 collective-permute-done.47
  375.0 6.6 %collective-permute-done.56.refs_3_ = bf16[1,67,32,128]{3,2,1,0:T(8,128)(2,1)S(1)} collective-permute-done((bf16[1,67,32,128]{3,2,1,0:T(8,128)(2,1)S(1)}, bf16[1,67,32,128]{3,2,1,0:T(8,128)(2,1)S(1)}, u32[]{:S(2)}, u32[]{:S(2)}) %collective-permute-start.56) | collective-permute-done | bytes 548896 | tf_op jit(solution)/shard_map/ppermute | solution.py:59
  383.0 9.5 %collective-permute-start.60 = (bf16[1,67,32,128]{3,2,1,0:T(8,128)(2,1)S(1)}, bf16[1,67,32,128]{3,2,1,0:T(8,128)(2,1)S(1)}, u32[]{:S(2)}, u32[]{:S(2)}) collective-permute-start(bf16[1,67,32,128]{3,2,1,0:T(8,128)(2,1)S(1)} %maximum_bitcast_fusion.refs_1_), channel_id=1, source_target_pairs={{0,4},{4,0},{8,12},{12,8},{16,20},{20,16},{24,28},{28,24},{1,5},{5... | collective-permute-start | bytes 1646600 | tf_op jit(solution)/shard_map/ppermute | solution.py:59
  400.7 6.2 %collective-permute-done.59.refs_3_ = bf16[1,32,32,128]{3,2,1,0:T(8,128)(2,1)S(1)} collective-permute-done((bf16[1,32,32,128]{3,2,1,0:T(8,128)(2,1)S(1)}, bf16[1,32,32,128]{3,2,1,0:T(8,128)(2,1)S(1)}, u32[]{:S(2)}, u32[]{:S(2)}) %collective-permute-start.59) | collective-permute-done | bytes 262176 | tf_op jit(solution)/shard_map/ppermute | solution.py:59
  411.9 5.9 %place.3 = (f32[256,2816]{1,0:T(8,128)}, f32[256,2816]{1,0:T(8,128)}, f32[704,1024]{1,0:T(8,128)}, f32[32,128]{1,0:T(8,128)}) custom-call(s32[2]{0:T(128)} %pad_add_fusion.refs_0_.pos, bf16[1,67,32,128]{3,2,1,0:T(8,128)(2,1)} %copy-done.17, bf16[1,67,32,128]{3,2,1,0:T(8,128)(2,1)} %copy-done.28, bf16[1,67,32,128]{3,2,1,0:T(8,128)(2,1)} %copy-done.27, ...), custom_call_target="tpu_custom_call" | custom-call | flops 20000000000 | tf_op jit(solution)/shard_map/place/pallas_call | solution.py:971
  425.8 3.8 place.2
  (338 shorter events, 124.0 us)
Async XLA Ops:
  5.6 15.6 %collective-permute-start.1 = (bf16[25,32,128]{2,1,0:T(8,128)(2,1)}, bf16[25,32,128]{2,1,0:T(8,128)(2,1)S(1)}, u32[]{:S(2)}, u32[]{:S(2)}) collective-permute-start(bf16[25,32,128]{2,1,0:T(8,128)(2,1)} %cut.3), channel_id=1, source_target_pairs={{0,2},{1,3},{2,0},{3,1},{4,6},{5,7},{6,4},{7,5},{8,10},{9,11},{10,... | collective-permute-start | bytes 614408 | tf_op jit(solution)/shard_map/ppermute | solution.py:68
  8.1 17.5 %collective-permute-start = (bf16[25,32,128]{2,1,0:T(8,128)(2,1)}, bf16[25,32,128]{2,1,0:T(8,128)(2,1)S(1)}, u32[]{:S(2)}, u32[]{:S(2)}) collective-permute-start(bf16[25,32,128]{2,1,0:T(8,128)(2,1)} %cut.3), channel_id=1, source_target_pairs={{0,1},{1,2},{2,3},{3,0},{4,5},{5,6},{6,7},{7,4},{8,9},{9,10},{10,1... | collective-permute-start | bytes 614408 | tf_op jit(solution)/shard_map/ppermute | solution.py:68
  32.4 14.9 %collective-permute-start.3 = (bf16[3,24,32,128]{3,2,1,0:T(8,128)(2,1)S(1)}, bf16[3,24,32,128]{3,2,1,0:T(8,128)(2,1)}, u32[]{:S(2)}, u32[]{:S(2)}) collective-permute-start(bf16[3,24,32,128]{3,2,1,0:T(8,128)(2,1)S(1)} %pad_maximum_fusion.8.refs_9_), channel_id=1, source_target_pairs={{0,8},{4,12},{8,0},{12,4},{16,24},{20,28},{24,16},{28,20},{1,9},{5... | collective-permute-start | bytes 1769480 | tf_op jit(solution)/shard_map/ppermute | solution.py:59
  42.6 15.8 %collective-permute-start.14 = (bf16[30,32,128]{2,1,0:T(8,128)(2,1)S(1)}, bf16[30,32,128]{2,1,0:T(8,128)(2,1)S(1)}, u32[]{:S(2)}, u32[]{:S(2)}) collective-permute-start(bf16[30,32,128]{2,1,0:T(8,128)(2,1)S(1)} %copy-done.22), channel_id=1, source_target_pairs={{0,2},{1,3},{2,0},{3,1},{4,6},{5,7},{6,4},{7,5},{8,10},{9,11},{10,... | collective-permute-start | bytes 737288 | tf_op jit(solution)/shard_map/ppermute | solution.py:68
  47.3 15.6 %collective-permute-start.11 = (bf16[3,24,32,128]{3,2,1,0:T(8,128)(2,1)S(1)}, bf16[3,24,32,128]{3,2,1,0:T(8,128)(2,1)}, u32[]{:S(2)}, u32[]{:S(2)}) collective-permute-start(bf16[3,24,32,128]{3,2,1,0:T(8,128)(2,1)S(1)} %collective-permute-done.4.refs_11_), channel_id=1, source_target_pairs={{0,4},{4,0},{8,12},{12,8},{16,20},{20,16},{24,28},{28,24},{1,5},{5... | collective-permute-start | bytes 1769480 | tf_op jit(solution)/shard_map/ppermute | solution.py:59
  59.2 32.0 %collective-permute-start.21 = (bf16[44,32,128]{2,1,0:T(8,128)(2,1)S(1)}, bf16[44,32,128]{2,1,0:T(8,128)(2,1)S(1)}, u32[]{:S(2)}, u32[]{:S(2)}) collective-permute-start(bf16[44,32,128]{2,1,0:T(8,128)(2,1)S(1)} %copy-done.20), channel_id=1, source_target_pairs={{0,3},{1,0},{2,1},{3,2},{4,7},{5,4},{6,5},{7,6},{8,11},{9,8},{10,9... | collective-permute-start | bytes 1081352 | tf_op jit(solution)/shard_map/ppermute | solution.py:68
  60.3 31.0 %collective-permute-start.20 = (bf16[44,32,128]{2,1,0:T(8,128)(2,1)S(1)}, bf16[44,32,128]{2,1,0:T(8,128)(2,1)S(1)}, u32[]{:S(2)}, u32[]{:S(2)}) collective-permute-start(bf16[44,32,128]{2,1,0:T(8,128)(2,1)S(1)} %copy-done.20), channel_id=1, source_target_pairs={{0,2},{1,3},{2,0},{3,1},{4,6},{5,7},{6,4},{7,5},{8,10},{9,11},{10,... | collective-permute-start | bytes 1081352 | tf_op jit(solution)/shard_map/ppermute | solution.py:68
  62.9 30.1 %collective-permute-start.19 = (bf16[44,32,128]{2,1,0:T(8,128)(2,1)S(1)}, bf16[44,32,128]{2,1,0:T(8,128)(2,1)S(1)}, u32[]{:S(2)}, u32[]{:S(2)}) collective-permute-start(bf16[44,32,128]{2,1,0:T(8,128)(2,1)S(1)} %copy-done.20), channel_id=1, source_target_pairs={{0,1},{1,2},{2,3},{3,0},{4,5},{5,6},{6,7},{7,4},{8,9},{9,10},{10,1... | collective-permute-start | bytes 1081352 | tf_op jit(solution)/shard_map/ppermute | solution.py:68
  63.4 17.2 %collective-permute-start.16 = (bf16[3,30,32,128]{3,2,1,0:T(8,128)(2,1)S(1)}, bf16[3,30,32,128]{3,2,1,0:T(8,128)(2,1)S(1)}, u32[]{:S(2)}, u32[]{:S(2)}) collective-permute-start(bf16[3,30,32,128]{3,2,1,0:T(8,128)(2,1)S(1)} %pad_maximum_fusion.6.refs_7_), channel_id=1, source_target_pairs={{0,16},{4,20},{8,24},{12,28},{16,0},{20,4},{24,8},{28,12},{1,17},{... | collective-permute-start | bytes 2211848 | tf_op jit(solution)/shard_map/ppermute | solution.py:59
  63.6 17.0 %collective-permute-start.15 = (bf16[3,30,32,128]{3,2,1,0:T(8,128)(2,1)S(1)}, bf16[3,30,32,128]{3,2,1,0:T(8,128)(2,1)S(1)}, u32[]{:S(2)}, u32[]{:S(2)}) collective-permute-start(bf16[3,30,32,128]{3,2,1,0:T(8,128)(2,1)S(1)} %pad_maximum_fusion.6.refs_7_), channel_id=1, source_target_pairs={{0,8},{4,12},{8,0},{12,4},{16,24},{20,28},{24,16},{28,20},{1,9},{5... | collective-permute-start | bytes 2211848 | tf_op jit(solution)/shard_map/ppermute | solution.py:59
  80.6 15.7 %collective-permute-start.17 = (bf16[3,15,32,128]{3,2,1,0:T(8,128)(2,1)S(1)}, bf16[3,15,32,128]{3,2,1,0:T(8,128)(2,1)}, u32[]{:S(2)}, u32[]{:S(2)}) collective-permute-start(bf16[3,15,32,128]{3,2,1,0:T(8,128)(2,1)S(1)} %slice.223), channel_id=1, source_target_pairs={{0,16},{4,20},{8,24},{12,28},{16,0},{20,4},{24,8},{28,12},{1,17},{... | collective-permute-start | bytes 1105928 | tf_op jit(solution)/shard_map/ppermute | solution.py:59
  93.2 24.3 %collective-permute-start.28 = (bf16[3,44,32,128]{3,2,1,0:T(8,128)(2,1)S(1)}, bf16[3,44,32,128]{3,2,1,0:T(8,128)(2,1)}, u32[]{:S(2)}, u32[]{:S(2)}) collective-permute-start(bf16[3,44,32,128]{3,2,1,0:T(8,128)(2,1)S(1)} %pad_maximum_fusion.5.refs_19_), channel_id=1, source_target_pairs={{0,16},{4,20},{8,24},{12,28},{16,0},{20,4},{24,8},{28,12},{1,17},{... | collective-permute-start | bytes 3244040 | tf_op jit(solution)/shard_map/ppermute | solution.py:59
  93.5 25.1 %collective-permute-start.27 = (bf16[3,44,32,128]{3,2,1,0:T(8,128)(2,1)S(1)}, bf16[3,44,32,128]{3,2,1,0:T(8,128)(2,1)}, u32[]{:S(2)}, u32[]{:S(2)}) collective-permute-start(bf16[3,44,32,128]{3,2,1,0:T(8,128)(2,1)S(1)} %pad_maximum_fusion.5.refs_19_), channel_id=1, source_target_pairs={{0,8},{4,12},{8,0},{12,4},{16,24},{20,28},{24,16},{28,20},{1,9},{5... | collective-permute-start | bytes 3244040 | tf_op jit(solution)/shard_map/ppermute | solution.py:59
  93.9 29.4 %collective-permute-start.22 = (bf16[3,30,32,128]{3,2,1,0:T(8,128)(2,1)S(1)}, bf16[3,30,32,128]{3,2,1,0:T(8,128)(2,1)S(1)}, u32[]{:S(2)}, u32[]{:S(2)}) collective-permute-start(bf16[3,30,32,128]{3,2,1,0:T(8,128)(2,1)S(1)} %pad_maximum_fusion.6.refs_7_), channel_id=1, source_target_pairs={{0,4},{4,0},{8,12},{12,8},{16,20},{20,16},{24,28},{28,24},{1,5},{5... | collective-permute-start | bytes 2211848 | tf_op jit(solution)/shard_map/ppermute | solution.py:59
  120.0 14.6 %collective-permute-start.23 = (bf16[3,30,32,128]{3,2,1,0:T(8,128)(2,1)S(1)}, bf16[3,30,32,128]{3,2,1,0:T(8,128)(2,1)S(1)}, u32[]{:S(2)}, u32[]{:S(2)}) collective-permute-start(bf16[3,30,32,128]{3,2,1,0:T(8,128)(2,1)S(1)} %copy-done.25), channel_id=1, source_target_pairs={{0,4},{4,0},{8,12},{12,8},{16,20},{20,16},{24,28},{28,24},{1,5},{5... | collective-permute-start | bytes 2211848 | tf_op jit(solution)/shard_map/ppermute | solution.py:59
  123.4 15.0 %collective-permute-start.31 = (bf16[3,44,32,128]{3,2,1,0:T(8,128)(2,1)S(1)}, bf16[3,44,32,128]{3,2,1,0:T(8,128)(2,1)}, u32[]{:S(2)}, u32[]{:S(2)}) collective-permute-start(bf16[3,44,32,128]{3,2,1,0:T(8,128)(2,1)S(1)} %pad_maximum_fusion.5.refs_19_), channel_id=1, source_target_pairs={{0,4},{4,0},{8,12},{12,8},{16,20},{20,16},{24,28},{28,24},{1,5},{5... | collective-permute-start | bytes 3244040 | tf_op jit(solution)/shard_map/ppermute | solution.py:59
  216.6 49.8 %collective-permute-start.39 = (bf16[2,132,32,128]{3,2,1,0:T(8,128)(2,1)}, bf16[2,132,32,128]{3,2,1,0:T(8,128)(2,1)}, u32[]{:S(2)}, u32[]{:S(2)}) collective-permute-start(bf16[2,132,32,128]{3,2,1,0:T(8,128)(2,1)} %get-tuple-element.172), channel_id=1, source_target_pairs={{0,8},{4,12},{8,0},{12,4},{16,24},{20,28},{24,16},{28,20},{1,9},{5... | collective-permute-start | bytes 6488072 | tf_op jit(solution)/shard_map/ppermute | solution.py:59
  218.1 48.2 %collective-permute-start.40 = (bf16[2,132,32,128]{3,2,1,0:T(8,128)(2,1)}, bf16[2,132,32,128]{3,2,1,0:T(8,128)(2,1)}, u32[]{:S(2)}, u32[]{:S(2)}) collective-permute-start(bf16[2,132,32,128]{3,2,1,0:T(8,128)(2,1)} %get-tuple-element.185), channel_id=1, source_target_pairs={{0,16},{4,20},{8,24},{12,28},{16,0},{20,4},{24,8},{28,12},{1,17},{... | collective-permute-start | bytes 6488072 | tf_op jit(solution)/shard_map/ppermute | solution.py:59
  267.9 23.9 %collective-permute-start.42 = (bf16[132,32,128]{2,1,0:T(8,128)(2,1)S(1)}, bf16[132,32,128]{2,1,0:T(8,128)(2,1)S(1)}, u32[]{:S(2)}, u32[]{:S(2)}) collective-permute-start(bf16[132,32,128]{2,1,0:T(8,128)(2,1)S(1)} %fusion.3), channel_id=1, source_target_pairs={{0,8},{4,12},{8,0},{12,4},{16,24},{20,28},{24,16},{28,20},{1,9},{5... | collective-permute-start | bytes 3244040 | tf_op jit(solution)/shard_map/ppermute | solution.py:59
  270.8 24.0 %collective-permute-start.41 = (bf16[132,32,128]{2,1,0:T(8,128)(2,1)}, bf16[132,32,128]{2,1,0:T(8,128)(2,1)S(1)}, u32[]{:S(2)}, u32[]{:S(2)}) collective-permute-start(bf16[132,32,128]{2,1,0:T(8,128)(2,1)} %fusion.2), channel_id=1, source_target_pairs={{0,16},{4,20},{8,24},{12,28},{16,0},{20,4},{24,8},{28,12},{1,17},{... | collective-permute-start | bytes 3244040 | tf_op jit(solution)/shard_map/ppermute | solution.py:59
  313.5 41.2 %collective-permute-start.50 = (bf16[67,32,128]{2,1,0:T(8,128)(2,1)}, bf16[67,32,128]{2,1,0:T(8,128)(2,1)}, u32[]{:S(2)}, u32[]{:S(2)}) collective-permute-start(bf16[67,32,128]{2,1,0:T(8,128)(2,1)} %get-tuple-element.248), channel_id=1, source_target_pairs={{0,3},{1,0},{2,1},{3,2},{4,7},{5,4},{6,5},{7,6},{8,11},{9,8},{10,9... | collective-permute-start | bytes 1646600 | tf_op jit(solution)/shard_map/ppermute | solution.py:68
  315.1 39.6 %collective-permute-start.48 = (bf16[67,32,128]{2,1,0:T(8,128)(2,1)S(1)}, bf16[67,32,128]{2,1,0:T(8,128)(2,1)}, u32[]{:S(2)}, u32[]{:S(2)}) collective-permute-start(bf16[67,32,128]{2,1,0:T(8,128)(2,1)S(1)} %get-tuple-element.249), channel_id=1, source_target_pairs={{0,1},{1,2},{2,3},{3,0},{4,5},{5,6},{6,7},{7,4},{8,9},{9,10},{10,1... | collective-permute-start | bytes 1646600 | tf_op jit(solution)/shard_map/ppermute | solution.py:68
  316.9 45.7 %collective-permute-start.49 = (bf16[67,32,128]{2,1,0:T(8,128)(2,1)S(1)}, bf16[67,32,128]{2,1,0:T(8,128)(2,1)}, u32[]{:S(2)}, u32[]{:S(2)}) collective-permute-start(bf16[67,32,128]{2,1,0:T(8,128)(2,1)S(1)} %get-tuple-element.250), channel_id=1, source_target_pairs={{0,2},{1,3},{2,0},{3,1},{4,6},{5,7},{6,4},{7,5},{8,10},{9,11},{10,... | collective-permute-start | bytes 1646600 | tf_op jit(solution)/shard_map/ppermute | solution.py:68
  328.5 25.2 %collective-permute-start.44 = (bf16[2,64,32,128]{3,2,1,0:T(8,128)(2,1)}, bf16[2,64,32,128]{3,2,1,0:T(8,128)(2,1)S(1)}, u32[]{:S(2)}, u32[]{:S(2)}) collective-permute-start(bf16[2,64,32,128]{3,2,1,0:T(8,128)(2,1)} %get-tuple-element.204), channel_id=1, source_target_pairs={{0,8},{4,12},{8,0},{12,4},{16,24},{20,28},{24,16},{28,20},{1,9},{5... | collective-permute-start | bytes 3145736 | tf_op jit(solution)/shard_map/ppermute | solution.py:59
  329.5 24.1 %collective-permute-start.45 = (bf16[2,64,32,128]{3,2,1,0:T(8,128)(2,1)}, bf16[2,64,32,128]{3,2,1,0:T(8,128)(2,1)S(1)}, u32[]{:S(2)}, u32[]{:S(2)}) collective-permute-start(bf16[2,64,32,128]{3,2,1,0:T(8,128)(2,1)} %get-tuple-element.212), channel_id=1, source_target_pairs={{0,16},{4,20},{8,24},{12,28},{16,0},{20,4},{24,8},{28,12},{1,17},{... | collective-permute-start | bytes 3145736 | tf_op jit(solution)/shard_map/ppermute | solution.py:59
  371.9 20.7 %collective-permute-start.52 = (bf16[32,32,128]{2,1,0:T(8,128)(2,1)S(1)}, bf16[32,32,128]{2,1,0:T(8,128)(2,1)S(1)}, u32[]{:S(2)}, u32[]{:S(2)}) collective-permute-start(bf16[32,32,128]{2,1,0:T(8,128)(2,1)S(1)} %get-tuple-element.246), channel_id=1, source_target_pairs={{0,2},{1,3},{2,0},{3,1},{4,6},{5,7},{6,4},{7,5},{8,10},{9,11},{10,... | collective-permute-start | bytes 786440 | tf_op jit(solution)/shard_map/ppermute | solution.py:68
  374.7 23.3 %collective-permute-start.53 = (bf16[32,32,128]{2,1,0:T(8,128)(2,1)S(1)}, bf16[32,32,128]{2,1,0:T(8,128)(2,1)S(1)}, u32[]{:S(2)}, u32[]{:S(2)}) collective-permute-start(bf16[32,32,128]{2,1,0:T(8,128)(2,1)S(1)} %get-tuple-element.247), channel_id=1, source_target_pairs={{0,3},{1,0},{2,1},{3,2},{4,7},{5,4},{6,5},{7,6},{8,11},{9,8},{10,9... | collective-permute-start | bytes 786440 | tf_op jit(solution)/shard_map/ppermute | solution.py:68
  381.6 17.3 %collective-permute-start.57 = (bf16[1,34,32,128]{3,2,1,0:T(8,128)(2,1)S(1)}, bf16[1,34,32,128]{3,2,1,0:T(8,128)(2,1)S(1)}, u32[]{:S(2)}, u32[]{:S(2)}) collective-permute-start(bf16[1,34,32,128]{3,2,1,0:T(8,128)(2,1)S(1)} %slice.237), channel_id=1, source_target_pairs={{0,8},{4,12},{8,0},{12,4},{16,24},{20,28},{24,16},{28,20},{1,9},{5... | collective-permute-start | bytes 835592 | tf_op jit(solution)/shard_map/ppermute | solution.py:59
  382.7 16.2 %collective-permute-start.55 = (bf16[1,33,32,128]{3,2,1,0:T(8,128)(2,1)S(1)}, bf16[1,33,32,128]{3,2,1,0:T(8,128)(2,1)S(1)}, u32[]{:S(2)}, u32[]{:S(2)}) collective-permute-start(bf16[1,33,32,128]{3,2,1,0:T(8,128)(2,1)S(1)} %slice.236), channel_id=1, source_target_pairs={{0,16},{4,20},{8,24},{12,28},{16,0},{20,4},{24,8},{28,12},{1,17},{... | collective-permute-start | bytes 811016 | tf_op jit(solution)/shard_map/ppermute | solution.py:59
  383.0 26.0 %collective-permute-start.60 = (bf16[1,67,32,128]{3,2,1,0:T(8,128)(2,1)S(1)}, bf16[1,67,32,128]{3,2,1,0:T(8,128)(2,1)S(1)}, u32[]{:S(2)}, u32[]{:S(2)}) collective-permute-start(bf16[1,67,32,128]{3,2,1,0:T(8,128)(2,1)S(1)} %maximum_bitcast_fusion.refs_1_), channel_id=1, source_target_pairs={{0,4},{4,0},{8,12},{12,8},{16,20},{20,16},{24,28},{28,24},{1,5},{5... | collective-permute-start | bytes 1646600 | tf_op jit(solution)/shard_map/ppermute | solution.py:59
  392.5 18.0 %collective-permute-start.62 = (bf16[1,67,32,128]{3,2,1,0:T(8,128)(2,1)S(1)}, bf16[1,67,32,128]{3,2,1,0:T(8,128)(2,1)S(1)}, u32[]{:S(2)}, u32[]{:S(2)}) collective-permute-start(bf16[1,67,32,128]{3,2,1,0:T(8,128)(2,1)S(1)} %collective-permute-done.56.refs_3_), channel_id=1, source_target_pairs={{0,4},{4,0},{8,12},{12,8},{16,20},{20,16},{24,28},{28,24},{1,5},{5... | collective-permute-start | bytes 1646600 | tf_op jit(solution)/shard_map/ppermute | solution.py:59
  409.0 15.0 %collective-permute-start.67 = (bf16[1,32,32,128]{3,2,1,0:T(8,128)(2,1)S(1)}, bf16[1,32,32,128]{3,2,1,0:T(8,128)(2,1)}, u32[]{:S(2)}, u32[]{:S(2)}) collective-permute-start(bf16[1,32,32,128]{3,2,1,0:T(8,128)(2,1)S(1)} %bitcast.130), channel_id=1, source_target_pairs={{0,4},{4,0},{8,12},{12,8},{16,20},{20,16},{24,28},{28,24},{1,5},{5... | collective-permute-start | bytes 786440 | tf_op jit(solution)/shard_map/ppermute | solution.py:59
  (95 other events, 1018.7 us)
